TPU v7x, 256 devices: a whole 4x4x8 slice. The times are simulated.
256 devices in a mesh: grp: 4 (over x_hi, core), par: 64 (over z, x_lo, y).
Axes of the slice: x: 4 (x_hi: 2, x_lo: 2; x = x_hi * 2 + x_lo), y: 4, z: 8, core: 2. Of those that a mesh axis runs over, the one named last changes fastest.
Arguments:
- activations: bfloat16 [4096, 98304], P('par', 'grp'), may hold values from -6 to 6
- out_grads: bfloat16 [11008, 98304], P('par', 'grp'), may hold values from -6 to 6
- example_ids: int32 [4, 24576], P('grp'), may hold values from 0 to 31, never falling along the last dimension, each value on 1 to 1536 neighbouring positions
- train_flags: int32 [128], P('grp'), may hold values 0 or 1
- in_proj: bfloat16 [4096, 32], P('par'), may hold values from -0.09375 to 0.09375
- out_proj: bfloat16 [11008, 32], P('par'), may hold values from -0.0546875 to 0.0546875
Outputs:
- kernel: float32 [128, 128], P('grp')
Inputs may be any that keep to these rules, and one draw needn't show every extreme that they name: `example_ids`: along each row ids never fall; each of the 32 examples has 1 to 1536 tokens, one exactly 1536.
All inputs are finite; a program needn't handle non-finite values. No bound on the sum of `train_flags` on one device may be relied on, other than what follows from the above.
Results may differ from a plain program's by a relative error of at most 0.0003.
Values sent between devices are 32-bit elements; how exact they have to be, the bound alone decides.
No kernel may reach another device: no remote copies, remote signals or barrier semaphores. Data moves between devices by JAX's collectives and lax.ppermute only.
A program may use at most 128 MiB of HBM per device.

v0:
```python
import jax
import jax.numpy as jnp
from jax import lax
from jax.sharding import PartitionSpec as P

PROJ_IN = 32
PROJ_OUT = 32
TOK_GRP = 24576
EX_GRP = 32


def shifted(value, axis, steps):
    count = lax.axis_size(axis)
    pairs = [(source, (source + steps) % count) for source in range(count)]
    return lax.ppermute(value, axis, pairs)


def token_features(left_part, right_part, group_ids):
    count = left_part.shape[1]
    width = 2048
    steps = count // width
    lefts = left_part.reshape(PROJ_IN, steps, width).transpose(1, 0, 2)
    rights = right_part.reshape(PROJ_OUT, steps, width).transpose(1, 0, 2)
    idents = group_ids.reshape(steps, width)
    labels = jnp.arange(EX_GRP, dtype=jnp.int32)

    def add_block(total, packed):
        left_block, right_block, id_block = packed
        onehot = (id_block[None, :] == labels[:, None]).astype(jnp.float32)
        spread = (left_block[:, None, :] * onehot[None, :, :]).reshape(PROJ_IN * EX_GRP, width)
        summed = lax.dot_general(
            spread, right_block, (((1,), (1,)), ((), ())), precision=lax.Precision.HIGHEST
        )
        return (total + summed.reshape(PROJ_IN, EX_GRP, PROJ_OUT), None)

    start = jnp.zeros((PROJ_IN, EX_GRP, PROJ_OUT), jnp.float32)
    total, unused = lax.scan(add_block, start, (lefts, rights, idents))
    return total.transpose(1, 0, 2).reshape(EX_GRP, PROJ_IN * PROJ_OUT)


def on_device(activations, out_grads, example_ids, train_flags, in_proj, out_proj):
    left_proj = lax.dot_general(
        in_proj, activations, (((0,), (0,)), ((), ())), preferred_element_type=jnp.float32
    )
    right_proj = lax.dot_general(
        out_proj, out_grads, (((0,), (0,)), ((), ())), preferred_element_type=jnp.float32
    )
    group_ids = example_ids[0]
    left_proj, right_proj = lax.psum((left_proj, right_proj), "par")
    features = token_features(left_proj, right_proj, group_ids)
    flags = train_flags.astype(jnp.float32)
    factor = 1.0 / (PROJ_IN * (TOK_GRP // EX_GRP))
    row_side = features * (flags * factor)[:, None]
    col_side = features * (1.0 - flags)[:, None]
    group_count = lax.axis_size("grp")
    empty = jnp.zeros((row_side.shape[0], row_side.shape[0] * group_count), jnp.float32)
    position = lax.axis_index("grp")
    moving = col_side
    kernel = empty
    for turn_index in range(group_count):
        if turn_index > 0:
            moving = shifted(moving, "grp", 1)
        anchor = (position - turn_index) % group_count
        block = jnp.dot(row_side, moving.T, precision=lax.Precision.HIGHEST)
        kernel = lax.dynamic_update_slice_in_dim(kernel, block, anchor * row_side.shape[0], 1)
    return kernel


def solution(mesh):
    return jax.shard_map(
        on_device,
        mesh=mesh,
        in_specs=(
            P("par", "grp"),
            P("par", "grp"),
            P("grp", None),
            P("grp"),
            P("par", None),
            P("par", None),
        ),
        out_specs=P("grp", None),
        check_vma=False,
    )
```

profile of v0, /device:TPU:32, one launch (start us, length us, event | category | flops | bytes accessed | tf_op | source)
XLA Modules:
  0.0 843.0 jit_solution(16067441390838722043)
XLA Ops:
  6.5 1.9 copy-done
  8.4 2.9 fusion.24
  11.3 3.8 reshape.59
  15.2 6.8 fusion.25
  22.0 3.8 reshape.60
  25.9 0.5 broadcast.44
  26.4 0.3 copy-done.1
  26.7 0.9 reduce.3
  27.6 0.5 convert_multiply_fusion
  28.2 628.0 %all-reduce.3.cloned.1.call-done = (f32[12,32,2048]{2,0,1:T(8,128)}, f32[12,32,2048]{2,0,1:T(8,128)}) async-done(((f32[12,32,2048]{2,0,1:T(8,128)}, f32[12,32,2048]{2,0,1:T(8,128)}), (f32[12,32,2048]{2,0,1:T(8,128)}, f32[12,32,2048]{2,0,1:T(8,128)})) %all-reduce.3.cloned.1.call-update) | async-done | bytes 6291472 | tf_op jit(solution)/shard_map/psum | solution.py:49
  656.1 156.2 %while.11 = (s32[]{:T(128)}, f32[32,32,32]{2,1,0:T(8,128)}, f32[12,32,2048]{2,0,1:T(8,128)}, s32[12,2048]{1,0:T(8,128)S(1)}, f32[12,32,2048]{2,0,1:T(8,128)}, /*index=5*/s32[]{:T(128)}, s32[]{:T(128)}) while((s32[]{:T(128)}, f32[32,32,32]{2,1,0:T(8,128)}, f32[12,32,2048]{2,0,1:T(8,128)}, s32[12,2048]{1,0:T(8,128)S(1)}, ...), condition=%wide.region_3.4_spmd.clone, body=%wide.region_2.3_spmd.clone.sunk | while | flops 807600128 | bytes 2908255 | solution.py:37
  656.1 3.4 constant_dynamic-slice_fusion.6
  659.5 0.1 copy.21
  659.6 0.8 fusion.37
  660.4 8.6 %fusion.38 = f32[32,32,32]{2,1,0:T(8,128)} fusion(f32[32,2048]{1,0:T(8,128)} %fusion.37, f32[32,2048]{1,0:T(8,128)S(1)} %bitcast.34, f32[32,32,32]{2,1,0:T(8,128)} %get-tuple-element.122, f32[1,32,2048]{2,0,1:T(1,128)} %get-tuple-element.113, pred[]{:T(512)S(6)} %compare.7), kind=kOutput, calls=%fused_computation.5.clone.1 | convolution fusion | flops 807469056 | bytes 1048577 | tf_op jit(solution)/shard_map/while/body/eval_jaxpr/dot_general | solution.py:31
  669.0 3.4 constant_dynamic-slice_fusion.6
  672.5 0.8 fusion.37
  673.3 8.8 %fusion.38 = f32[32,32,32]{2,1,0:T(8,128)} fusion(f32[32,2048]{1,0:T(8,128)} %fusion.37, f32[32,2048]{1,0:T(8,128)S(1)} %bitcast.34, f32[32,32,32]{2,1,0:T(8,128)} %get-tuple-element.122, f32[1,32,2048]{2,0,1:T(1,128)} %get-tuple-element.113, pred[]{:T(512)S(6)} %compare.7), kind=kOutput, calls=%fused_computation.5.clone.1 | convolution fusion | flops 807469056 | bytes 1048577 | tf_op jit(solution)/shard_map/while/body/eval_jaxpr/dot_general | solution.py:31
  682.0 3.4 constant_dynamic-slice_fusion.6
  685.5 0.8 fusion.37
  686.3 8.8 %fusion.38 = f32[32,32,32]{2,1,0:T(8,128)} fusion(f32[32,2048]{1,0:T(8,128)} %fusion.37, f32[32,2048]{1,0:T(8,128)S(1)} %bitcast.34, f32[32,32,32]{2,1,0:T(8,128)} %get-tuple-element.122, f32[1,32,2048]{2,0,1:T(1,128)} %get-tuple-element.113, pred[]{:T(512)S(6)} %compare.7), kind=kOutput, calls=%fused_computation.5.clone.1 | convolution fusion | flops 807469056 | bytes 1048577 | tf_op jit(solution)/shard_map/while/body/eval_jaxpr/dot_general | solution.py:31
  695.0 3.4 constant_dynamic-slice_fusion.6
  698.5 0.8 fusion.37
  699.3 8.8 %fusion.38 = f32[32,32,32]{2,1,0:T(8,128)} fusion(f32[32,2048]{1,0:T(8,128)} %fusion.37, f32[32,2048]{1,0:T(8,128)S(1)} %bitcast.34, f32[32,32,32]{2,1,0:T(8,128)} %get-tuple-element.122, f32[1,32,2048]{2,0,1:T(1,128)} %get-tuple-element.113, pred[]{:T(512)S(6)} %compare.7), kind=kOutput, calls=%fused_computation.5.clone.1 | convolution fusion | flops 807469056 | bytes 1048577 | tf_op jit(solution)/shard_map/while/body/eval_jaxpr/dot_general | solution.py:31
  708.1 3.4 constant_dynamic-slice_fusion.6
  711.6 0.8 fusion.37
  712.4 8.8 %fusion.38 = f32[32,32,32]{2,1,0:T(8,128)} fusion(f32[32,2048]{1,0:T(8,128)} %fusion.37, f32[32,2048]{1,0:T(8,128)S(1)} %bitcast.34, f32[32,32,32]{2,1,0:T(8,128)} %get-tuple-element.122, f32[1,32,2048]{2,0,1:T(1,128)} %get-tuple-element.113, pred[]{:T(512)S(6)} %compare.7), kind=kOutput, calls=%fused_computation.5.clone.1 | convolution fusion | flops 807469056 | bytes 1048577 | tf_op jit(solution)/shard_map/while/body/eval_jaxpr/dot_general | solution.py:31
  721.1 3.4 constant_dynamic-slice_fusion.6
  724.6 0.8 fusion.37
  725.4 8.8 %fusion.38 = f32[32,32,32]{2,1,0:T(8,128)} fusion(f32[32,2048]{1,0:T(8,128)} %fusion.37, f32[32,2048]{1,0:T(8,128)S(1)} %bitcast.34, f32[32,32,32]{2,1,0:T(8,128)} %get-tuple-element.122, f32[1,32,2048]{2,0,1:T(1,128)} %get-tuple-element.113, pred[]{:T(512)S(6)} %compare.7), kind=kOutput, calls=%fused_computation.5.clone.1 | convolution fusion | flops 807469056 | bytes 1048577 | tf_op jit(solution)/shard_map/while/body/eval_jaxpr/dot_general | solution.py:31
  734.2 3.4 constant_dynamic-slice_fusion.6
  737.6 0.8 fusion.37
  738.4 8.8 %fusion.38 = f32[32,32,32]{2,1,0:T(8,128)} fusion(f32[32,2048]{1,0:T(8,128)} %fusion.37, f32[32,2048]{1,0:T(8,128)S(1)} %bitcast.34, f32[32,32,32]{2,1,0:T(8,128)} %get-tuple-element.122, f32[1,32,2048]{2,0,1:T(1,128)} %get-tuple-element.113, pred[]{:T(512)S(6)} %compare.7), kind=kOutput, calls=%fused_computation.5.clone.1 | convolution fusion | flops 807469056 | bytes 1048577 | tf_op jit(solution)/shard_map/while/body/eval_jaxpr/dot_general | solution.py:31
  747.2 3.4 constant_dynamic-slice_fusion.6
  750.7 0.8 fusion.37
  751.5 8.8 %fusion.38 = f32[32,32,32]{2,1,0:T(8,128)} fusion(f32[32,2048]{1,0:T(8,128)} %fusion.37, f32[32,2048]{1,0:T(8,128)S(1)} %bitcast.34, f32[32,32,32]{2,1,0:T(8,128)} %get-tuple-element.122, f32[1,32,2048]{2,0,1:T(1,128)} %get-tuple-element.113, pred[]{:T(512)S(6)} %compare.7), kind=kOutput, calls=%fused_computation.5.clone.1 | convolution fusion | flops 807469056 | bytes 1048577 | tf_op jit(solution)/shard_map/while/body/eval_jaxpr/dot_general | solution.py:31
  760.2 3.4 constant_dynamic-slice_fusion.6
  763.7 0.8 fusion.37
  764.5 8.8 %fusion.38 = f32[32,32,32]{2,1,0:T(8,128)} fusion(f32[32,2048]{1,0:T(8,128)} %fusion.37, f32[32,2048]{1,0:T(8,128)S(1)} %bitcast.34, f32[32,32,32]{2,1,0:T(8,128)} %get-tuple-element.122, f32[1,32,2048]{2,0,1:T(1,128)} %get-tuple-element.113, pred[]{:T(512)S(6)} %compare.7), kind=kOutput, calls=%fused_computation.5.clone.1 | convolution fusion | flops 807469056 | bytes 1048577 | tf_op jit(solution)/shard_map/while/body/eval_jaxpr/dot_general | solution.py:31
  773.3 3.4 constant_dynamic-slice_fusion.6
  776.8 0.8 fusion.37
  777.5 8.8 %fusion.38 = f32[32,32,32]{2,1,0:T(8,128)} fusion(f32[32,2048]{1,0:T(8,128)} %fusion.37, f32[32,2048]{1,0:T(8,128)S(1)} %bitcast.34, f32[32,32,32]{2,1,0:T(8,128)} %get-tuple-element.122, f32[1,32,2048]{2,0,1:T(1,128)} %get-tuple-element.113, pred[]{:T(512)S(6)} %compare.7), kind=kOutput, calls=%fused_computation.5.clone.1 | convolution fusion | flops 807469056 | bytes 1048577 | tf_op jit(solution)/shard_map/while/body/eval_jaxpr/dot_general | solution.py:31
  786.3 3.4 constant_dynamic-slice_fusion.6
  789.8 0.8 fusion.37
  790.6 8.8 %fusion.38 = f32[32,32,32]{2,1,0:T(8,128)} fusion(f32[32,2048]{1,0:T(8,128)} %fusion.37, f32[32,2048]{1,0:T(8,128)S(1)} %bitcast.34, f32[32,32,32]{2,1,0:T(8,128)} %get-tuple-element.122, f32[1,32,2048]{2,0,1:T(1,128)} %get-tuple-element.113, pred[]{:T(512)S(6)} %compare.7), kind=kOutput, calls=%fused_computation.5.clone.1 | convolution fusion | flops 807469056 | bytes 1048577 | tf_op jit(solution)/shard_map/while/body/eval_jaxpr/dot_general | solution.py:31
  799.3 3.4 constant_dynamic-slice_fusion.6
  802.8 0.8 fusion.37
  803.6 8.8 %fusion.38 = f32[32,32,32]{2,1,0:T(8,128)} fusion(f32[32,2048]{1,0:T(8,128)} %fusion.37, f32[32,2048]{1,0:T(8,128)S(1)} %bitcast.34, f32[32,32,32]{2,1,0:T(8,128)} %get-tuple-element.122, f32[1,32,2048]{2,0,1:T(1,128)} %get-tuple-element.113, pred[]{:T(512)S(6)} %compare.7), kind=kOutput, calls=%fused_computation.5.clone.1 | convolution fusion | flops 807469056 | bytes 1048577 | tf_op jit(solution)/shard_map/while/body/eval_jaxpr/dot_general | solution.py:31
  812.4 2.1 copy.11
  814.5 1.3 reshape.61
  815.9 0.3 collective-permute-start
  816.1 2.0 convolution_bitcast_fusion
  818.2 0.6 broadcast_in_dim.4
  818.8 1.3 dynamic_update_slice.12
  820.1 1.9 collective-permute-done
  822.0 0.9 collective-permute-start.1
  823.0 0.9 fusion.18
  823.9 1.4 dynamic_update_slice.13
  825.3 2.6 collective-permute-done.1
  827.9 0.9 fusion.16
  828.9 1.4 dynamic_update_slice.14
  830.3 3.5 collective-permute-done.2
  833.8 0.9 fusion.14
  834.8 1.4 dynamic_update_slice.15
  (37 shorter events, 1.2 us)
Async XLA Ops:
  6.5 1.9 copy-start
  6.5 649.6 %all-reduce.3.cloned.1.call-start = ((), (), s32[]{:S(2)}) async-start(), calls=%async_computation | async-start | bytes 16777216 | tf_op jit(solution)/shard_map/psum | solution.py:49
  11.3 3.8 copy-start.2
  25.8 0.9 copy-start.1
  25.8 1.8 copy-start.4
  28.2 787.6 %copy-start.3 = (f32[32]{0:T(128)}, f32[32]{0:T(128)S(1)}, u32[]{:S(2)}) copy-start(f32[32]{0:T(128)S(1)} %get-tuple-element.78) | copy-start | bytes 388
  815.9 6.2 collective-permute-start
  822.0 5.9 collective-permute-start.1
  827.9 5.9 collective-permute-start.2
Sparse Core Ops, SparseCore 0:
  25.9 630.1 all-reduce.2
where the time goes:
time: 853 us; the launch traced here: 843 us
  waiting for transfers between devices  636 us (75%)
  matrix products  120 us (14%)
  local copies, waits for them, and re-layouts  61.8 us (7%)
  between operations  13.6 us (2%)
  other arithmetic  10.8 us (1%)
    psum x1, waiting for transfers between devices, on_device(): left_proj, right_proj = lax.psum((left_proj, right_proj), 'par')  628 us
    dot_general x12, matrix products, add_block(): lax.dot_general(spread, right_block, (((1,), (1,)), ((), ())), precision=...  105 us
    dynamic_slice x36, local copies, waits for them, and re-layouts, token_features(): total, unused = lax.scan(add_block, start, (lefts, rights, idents))  41.9 us
  transfers between devices with their start and end apart: 4, of which 4 were waited for; matrix products, arithmetic and copies ran while one was open for 1% of the time, Pallas kernels for 0%

commit v1 on v0

v1 whole, which is shorter than its diff:
```python
import functools
import jax
import jax.numpy as jnp
from jax import lax
from jax.experimental import pallas as pl
from jax.experimental.pallas import tpu as pltpu
from jax.sharding import PartitionSpec as P

ROWS = 32
TOK_GRP = 24576
EX_GRP = 32
Z, X, Y = 8, 2, 4
BLOCK = TOK_GRP // (Z * X * Y)
SIZE = {"z": Z, "x": X, "y": Y}


def parts_of(index):
    return {"z": index // (X * Y), "x": index // Y % X, "y": index % Y}


def index_of(parts):
    return (parts["z"] * X + parts["x"]) * Y + parts["y"]


def send(value, axis, change):
    pairs = []
    for source in range(Z * X * Y):
        parts = parts_of(source)
        parts[axis] = change(parts[axis]) % SIZE[axis]
        pairs.append((source, index_of(parts)))
    return lax.ppermute(value, "par", pairs)


def up(value, axis):
    return send(value, axis, lambda at: at + 1)


def down(value, axis):
    return send(value, axis, lambda at: at - 1)


def pick(chunks, at):
    return lax.dynamic_index_in_dim(chunks, at, 0, keepdims=False)


def ring_sum(chunks, axis, at):
    count = SIZE[axis]
    far = count // 2
    own = lambda steps: pick(chunks, (at + steps) % count)
    opposite = own(far)
    half = opposite.shape[0] // 2
    rising, falling = up(opposite[:half], axis), down(opposite[half:], axis)
    ahead, behind = own(far - 1), own(1 - far)
    ahead = jnp.concatenate([ahead[:half] + rising, ahead[half:]])
    behind = jnp.concatenate([behind[:half], behind[half:] + falling])
    for steps in range(far - 1, 0, -1):
        rising, falling = up(ahead, axis), down(behind, axis)
        if steps > 1:
            ahead, behind = own(steps - 1) + rising, own(1 - steps) + falling
    return own(0) + rising + falling


def left_kernel(weight_ref, input_ref, out_ref):
    out = lax.dot_general(
        weight_ref[...], input_ref[...], (((0,), (0,)), ((), ())), preferred_element_type=jnp.float32
    )
    for y in range(Y):
        for x in range(X):
            at = (y * X + x) * BLOCK
            out_ref[0, y, x] = out[:, at : at + BLOCK]


def right_kernel(weight_ref, input_ref, out_ref):
    out = lax.dot_general(
        weight_ref[...], input_ref[...], (((0,), (0,)), ((), ())), preferred_element_type=jnp.float32
    )
    for y in range(Y):
        for x in range(X):
            at = (y * X + x) * BLOCK
            out_ref[y, x, 0] = out[:, at : at + BLOCK]


def projected(kernel, weight, inputs, shape, spec):
    depth = inputs.shape[0]
    wide = TOK_GRP // Z
    return pl.pallas_call(
        kernel,
        grid=(Z,),
        in_specs=[
            pl.BlockSpec((depth, ROWS), lambda step: (0, 0)),
            pl.BlockSpec((depth, wide), lambda step: (0, step)),
        ],
        out_specs=spec,
        out_shape=jax.ShapeDtypeStruct(shape, jnp.float32),
        compiler_params=pltpu.CompilerParams(vmem_limit_bytes=32 * 1024 * 1024),
    )(weight, inputs)


def feature_kernel(left_ref, right_ref, ids_ref, out_ref):
    labels = lax.broadcasted_iota(jnp.int32, (EX_GRP, BLOCK), 0)
    member = (ids_ref[...] == labels).astype(jnp.float32).astype(jnp.bfloat16)
    right = right_ref[...]
    over = (((1,), (1,)), ((), ()))
    for part in range(8):
        rows = [left_ref[part * 4 + a : part * 4 + a + 1, :] * right for a in range(4)]
        product = jnp.concatenate(rows, axis=0)
        high = product.astype(jnp.bfloat16)
        low = (product - high.astype(jnp.float32)).astype(jnp.bfloat16)
        out_ref[part] = lax.dot_general(
            member, high, over, preferred_element_type=jnp.float32
        ) + lax.dot_general(member, low, over, preferred_element_type=jnp.float32)


def on_device(activations, out_grads, example_ids, train_flags, in_proj, out_proj):
    index = lax.axis_index("par")
    at = parts_of(index)
    group = lax.axis_index("grp")

    left = projected(
        left_kernel, in_proj, activations, (Z, Y, X, ROWS, BLOCK),
        pl.BlockSpec((1, Y, X, ROWS, BLOCK), lambda step: (step, 0, 0, 0, 0)),
    )
    right = projected(
        right_kernel, out_proj, out_grads, (Y, X, Z, ROWS, BLOCK),
        pl.BlockSpec((Y, X, 1, ROWS, BLOCK), lambda step: (0, 0, step, 0, 0)),
    )

    left = ring_sum(left, "z", at["z"])
    left = ring_sum(left, "y", at["y"])
    left = pick(left, at["x"]) + send(pick(left, 1 - at["x"]), "x", lambda i: 1 - i)

    right = ring_sum(right, "y", at["y"])
    right = pick(right, at["x"]) + send(pick(right, 1 - at["x"]), "x", lambda i: 1 - i)
    right = ring_sum(right, "z", at["z"])

    place = (at["z"] * Y + at["y"]) * X + at["x"]
    ids = lax.dynamic_slice(example_ids, (0, place * BLOCK), (1, BLOCK))
    features = pl.pallas_call(
        feature_kernel,
        out_shape=jax.ShapeDtypeStruct((8, EX_GRP, 128), jnp.float32),
    )(left, right, ids)

    first, second = (at["y"] ^ (at["y"] >> 1)) & 1, at["y"] >> 1
    features = features.reshape(2, 4, EX_GRP, 128)
    features = pick(features, first) + send(pick(features, 1 - first), "y", lambda i: i ^ 1)
    features = features.reshape(2, 2, EX_GRP, 128)
    features = pick(features, second) + send(pick(features, 1 - second), "y", lambda i: i ^ 3)
    features = pick(features, at["x"]) + send(pick(features, 1 - at["x"]), "x", lambda i: 1 - i)
    for bit in (1, 2, 4):
        features = features + send(features, "z", lambda i: i ^ bit)

    flags = train_flags.astype(jnp.float32)
    row_side = features * (flags * (1.0 / TOK_GRP))[:, None]
    cols = (features * (1.0 - flags)[:, None])[None]
    for bit in (1, 2):
        other = lax.ppermute(cols, "grp", [(i, i ^ bit) for i in range(4)])
        late = (group & bit) > 0
        cols = jnp.concatenate([jnp.where(late, other, cols), jnp.where(late, cols, other)])
    cols = cols.reshape(4 * EX_GRP, 128)
    kernel = lax.dot_general(
        row_side, cols, (((1,), (1,)), ((), ())), precision=lax.Precision.HIGHEST
    )
    kernel = kernel + send(kernel, "y", lambda i: i ^ 1)
    kernel = kernel + send(kernel, "y", lambda i: i ^ 3)
    kernel = kernel + send(kernel, "x", lambda i: 1 - i)
    return kernel


def solution(mesh):
    return jax.shard_map(
        on_device,
        mesh=mesh,
        in_specs=(
            P("par", "grp"),
            P("par", "grp"),
            P("grp", None),
            P("grp"),
            P("par", None),
            P("par", None),
        ),
        out_specs=P("grp", None),
        check_vma=False,
    )
```

time: 853 us -> 151 us (0.18)
  waiting for transfers between devices: 636 us -> 53.4 us
  matrix products: 120 us -> 0.23 us
  starting transfers between devices: 1.2 us -> 56.8 us
  local copies, waits for them, and re-layouts: 61.8 us -> 12.4 us
  between operations: 13.6 us -> 0.33 us
    psum x1 -> x0, waiting for transfers between devices: 628 us -> none  [on_device(): left_proj, right_proj = lax.psum((left_proj, right_proj), 'par')]
    dot_general x18 -> x1, matrix products: 120 us -> 0.23 us  [on_device(): lax.dot_general(row_side, cols, (((1,), (1,)), ((), ())), precision=lax.P...]
    ppermute x3 -> x37, starting transfers between devices: 1.19 us -> 56.8 us  [the longest x35 54 us: send(): return lax.ppermute(value, 'par', pairs)]
    ppermute x3 -> x37, waiting for transfers between devices: 8.05 us -> 53.4 us  [the longest x35 49.6 us: send(): return lax.ppermute(value, 'par', pairs)]
    dynamic_slice x36 -> x1, local copies, waits for them, and re-layouts: 41.9 us -> 0.56 us  [on_device(): ids = lax.dynamic_slice(example_ids, (0, place * BLOCK), (1, BLOCK))]
    add x0 -> x24, other arithmetic: none -> 13 us  [the longest x6 5.04 us: ring_sum(): ahead, behind = (own(steps - 1) + rising, own(1 - steps) + falling)]
    convert_element_type x12 -> x0, other arithmetic: 9.26 us -> none  [add_block(): onehot = (id_block[None, :] == labels[:, None]).astype(jnp.float32)]
    reshape x3 -> x0, local copies, waits for them, and re-layouts: 8.89 us -> none  [the longest x1 3.83 us: token_features(): lefts = left_part.reshape(PROJ_IN, steps, width).transpose(1, 0, 2)]
  transfers between devices with their start and end apart: 4 -> 37, of which waited for: 4 -> 24; matrix products, arithmetic and copies ran while one was open for 1% -> 11% of each run, Pallas kernels for 0% -> 1%
where the time goes in v1:
time: 151 us; the launch traced here: 149 us
  starting transfers between devices  56.8 us (38%)
  waiting for transfers between devices  53.4 us (35%)
  other arithmetic  17.6 us (12%)
  local copies, waits for them, and re-layouts  12.4 us (8%)
  Pallas kernels  7.8 us (5%)
    ppermute x35, starting transfers between devices, send(): return lax.ppermute(value, 'par', pairs)  54 us
    ppermute x35, waiting for transfers between devices, send(): return lax.ppermute(value, 'par', pairs)  49.6 us
    unnamed x20, local copies, waits for them, and re-layouts  8.86 us
    pallas_call x2, Pallas kernels, projected(): pl.pallas_call(kernel, grid=(Z,), in_specs=[pl.BlockSpec((depth, ROWS), l...  5.64 us
    add x6, other arithmetic, ring_sum(): ahead, behind = (own(steps - 1) + rising, own(1 - steps) + falling)  5.04 us
    ppermute x2, waiting for transfers between devices, on_device(): other = lax.ppermute(cols, 'grp', [(i, i ^ bit) for i in range(4)])  3.84 us
  transfers between devices with their start and end apart: 37, of which 24 were waited for; matrix products, arithmetic and copies ran while one was open for 11% of the time, Pallas kernels for 1%

profile of v1, /device:TPU:32, one launch (start us, length us, event | category | flops | bytes accessed | tf_op | source)
XLA Modules:
  0.0 148.6 jit_solution(1763839860011326799)
XLA Ops:
  0.0 0.9 copy.8.weight_ref
  0.9 3.4 %copy-done.2 = bf16[172,24576]{1,0:T(8,128)(2,1)S(1)} copy-done((bf16[172,24576]{1,0:T(8,128)(2,1)S(1)}, bf16[172,24576]{1,0:T(8,128)(2,1)}, u32[]{:S(2)}) %copy-start.2) | copy-done | bytes 8454168
  4.3 3.5 %shard_map.65 = f32[4,2,8,32,384]{4,3,2,1,0:T(8,128)S(1)} custom-call(bf16[172,32]{1,0:T(8,128)(2,1)S(1)} %copy.8.weight_ref, bf16[172,24576]{1,0:T(8,128)(2,1)S(1)} %copy-done.2), custom_call_target="tpu_custom_call" | custom-call | tf_op jit(solution)/shard_map/pallas_call | solution.py:86
  7.9 1.6 %copy-done.1 = f32[4,2,8,32,384]{4,3,2,1,0:T(8,128)} copy-done((f32[4,2,8,32,384]{4,3,2,1,0:T(8,128)}, f32[4,2,8,32,384]{4,3,2,1,0:T(8,128)S(1)}, u32[]{:S(2)}) %copy-start.1) | copy-done | bytes 3145752
  9.5 1.2 dynamic-slice_bitcast_fusion.4
  10.7 1.6 %collective-permute-start.13 = (f32[1,8,32,384]{3,2,1,0:T(8,128)}, f32[1,8,32,384]{3,2,1,0:T(8,128)}, u32[]{:S(2)}, u32[]{:S(2)}) collective-permute-start(f32[1,8,32,384]{3,2,1,0:T(8,128)} %get-tuple-element.7), channel_id=1, source_target_pairs={{0,1},{1,2},{2,3},{3,0},{4,5},{5,6},{6,7},{7,4},{8,9},{9,10},{10,1... | collective-permute-start | bytes 1179656 | tf_op jit(solution)/shard_map/ppermute | solution.py:31
  12.3 1.7 %collective-permute-start.15 = (f32[1,8,32,384]{3,2,1,0:T(8,128)}, f32[1,8,32,384]{3,2,1,0:T(8,128)}, u32[]{:S(2)}, u32[]{:S(2)}) collective-permute-start(f32[1,8,32,384]{3,2,1,0:T(8,128)} %get-tuple-element.9), channel_id=1, source_target_pairs={{0,3},{1,0},{2,1},{3,2},{4,7},{5,4},{6,5},{7,6},{8,11},{9,8},{10,9... | collective-permute-start | bytes 1179656 | tf_op jit(solution)/shard_map/ppermute | solution.py:31
  14.1 1.9 %copy-done.3 = bf16[64,24576]{1,0:T(8,128)(2,1)S(1)} copy-done((bf16[64,24576]{1,0:T(8,128)(2,1)S(1)}, bf16[64,24576]{1,0:T(8,128)(2,1)}, u32[]{:S(2)}) %copy-start.3) | copy-done | bytes 3145752
  16.0 2.1 %shard_map.64 = f32[8,4,2,32,384]{4,3,2,1,0:T(8,128)S(1)} custom-call(bf16[64,32]{1,0:T(8,128)(2,1)S(1)} %copy.7.weight_ref, bf16[64,24576]{1,0:T(8,128)(2,1)S(1)} %copy-done.3), custom_call_target="tpu_custom_call" | custom-call | tf_op jit(solution)/shard_map/pallas_call | solution.py:86
  18.2 2.0 %collective-permute-start = (f32[2,2,32,384]{3,2,1,0:T(8,128)S(1)}, f32[2,2,32,384]{3,2,1,0:T(8,128)S(1)}, u32[]{:S(2)}, u32[]{:S(2)}) collective-permute-start(f32[2,2,32,384]{3,2,1,0:T(8,128)S(1)} %get-tuple-element.15), channel_id=1, source_target_pairs={{0,8},{1,9},{2,10},{3,11},{4,12},{5,13},{6,14},{7,15},{8,16},{9,17... | collective-permute-start | bytes 589832 | tf_op jit(solution)/shard_map/ppermute | solution.py:31
  20.3 2.8 %collective-permute-done.13 = f32[1,8,32,384]{3,2,1,0:T(8,128)} collective-permute-done((f32[1,8,32,384]{3,2,1,0:T(8,128)}, f32[1,8,32,384]{3,2,1,0:T(8,128)}, u32[]{:S(2)}, u32[]{:S(2)}) %collective-permute-start.13) | collective-permute-done | bytes 393248 | tf_op jit(solution)/shard_map/ppermute | solution.py:31
  23.2 1.4 fusion.2
  24.6 0.9 pad_maximum_fusion
  25.6 1.6 %collective-permute-start.14 = (f32[2,8,32,384]{3,2,1,0:T(8,128)}, f32[2,8,32,384]{3,2,1,0:T(8,128)}, u32[]{:S(2)}, u32[]{:S(2)}) collective-permute-start(f32[2,8,32,384]{3,2,1,0:T(8,128)} %pad_maximum_fusion), channel_id=1, source_target_pairs={{0,1},{1,2},{2,3},{3,0},{4,5},{5,6},{6,7},{7,4},{8,9},{9,10},{10,1... | collective-permute-start | bytes 2359304 | tf_op jit(solution)/shard_map/ppermute | solution.py:31
  27.2 1.0 pad_maximum_fusion.1
  28.1 1.7 %collective-permute-start.16 = (f32[2,8,32,384]{3,2,1,0:T(8,128)}, f32[2,8,32,384]{3,2,1,0:T(8,128)}, u32[]{:S(2)}, u32[]{:S(2)}) collective-permute-start(f32[2,8,32,384]{3,2,1,0:T(8,128)} %pad_maximum_fusion.1), channel_id=1, source_target_pairs={{0,3},{1,0},{2,1},{3,2},{4,7},{5,4},{6,5},{7,6},{8,11},{9,8},{10,9... | collective-permute-start | bytes 2359304 | tf_op jit(solution)/shard_map/ppermute | solution.py:31
  30.5 0.8 pad_maximum_fusion.2
  31.4 1.9 %collective-permute-start.1 = (f32[4,2,32,384]{3,2,1,0:T(8,128)}, f32[4,2,32,384]{3,2,1,0:T(8,128)}, u32[]{:S(2)}, u32[]{:S(2)}) collective-permute-start(f32[4,2,32,384]{3,2,1,0:T(8,128)} %pad_maximum_fusion.2), channel_id=1, source_target_pairs={{0,8},{1,9},{2,10},{3,11},{4,12},{5,13},{6,14},{7,15},{8,16},{9,17... | collective-permute-start | bytes 1179656 | tf_op jit(solution)/shard_map/ppermute | solution.py:31
  33.3 1.7 %pad_maximum_fusion.3 = f32[4,2,32,384]{3,2,1,0:T(8,128)} fusion(f32[2,2,32,384]{3,2,1,0:T(8,128)} %get-tuple-element.14, f32[2,2,32,384]{3,2,1,0:T(8,128)S(1)} %get-tuple-element.16), kind=kLoop, calls=%fused_computation.13 | loop fusion | flops 98304 | bytes 786432 | tf_op jit(solution)/shard_map/concatenate | solution.py:55
  35.1 6.0 %collective-permute-done.1 = f32[4,2,32,384]{3,2,1,0:T(8,128)} collective-permute-done((f32[4,2,32,384]{3,2,1,0:T(8,128)}, f32[4,2,32,384]{3,2,1,0:T(8,128)}, u32[]{:S(2)}, u32[]{:S(2)}) %collective-permute-start.1) | collective-permute-done | bytes 393248 | tf_op jit(solution)/shard_map/ppermute | solution.py:31
  41.2 1.9 %bitcast_add_fusion.4 = f32[4,2,32,384]{3,2,1,0:T(8,128)} fusion(f32[4,2,32,384]{3,2,1,0:T(8,128)} %collective-permute-done.1, f32[8,4,2,32,384]{4,3,2,1,0:T(8,128)S(1)} %shard_map.64, s32[]{:T(128)S(6)} %select_n.202), kind=kLoop, calls=%fused_computation.17 | loop fusion | flops 98304 | bytes 1179652 | tf_op jit(solution)/shard_map/add | solution.py:59
  43.0 1.9 %collective-permute-start.2 = (f32[4,2,32,384]{3,2,1,0:T(8,128)}, f32[4,2,32,384]{3,2,1,0:T(8,128)}, u32[]{:S(2)}, u32[]{:S(2)}) collective-permute-start(f32[4,2,32,384]{3,2,1,0:T(8,128)} %bitcast_add_fusion.4), channel_id=1, source_target_pairs={{0,8},{1,9},{2,10},{3,11},{4,12},{5,13},{6,14},{7,15},{8,16},{9,17... | collective-permute-start | bytes 1179656 | tf_op jit(solution)/shard_map/ppermute | solution.py:31
  46.3 1.8 %fusion = f32[2,8,32,384]{3,2,1,0:T(8,128)S(1)} fusion(f32[2,8,32,384]{3,2,1,0:T(8,128)} %collective-permute-done.16, f32[2,8,32,384]{3,2,1,0:T(8,128)} %collective-permute-done.14, f32[4,2,8,32,384]{4,3,2,1,0:T(8,128)} %copy-done.1, s32[]{:T(128)S(6)} %select_n.215), kind=kLoop, calls=%fused_computation.3 | loop fusion | flops 393216 | bytes 3145732 | tf_op jit(solution)/shard_map/add | solution.py:60
  48.0 0.9 copy-done.4
  48.9 0.8 dynamic-slice_bitcast_fusion.6
  49.7 1.5 %collective-permute-start.17 = (f32[8,32,384]{2,1,0:T(8,128)}, f32[8,32,384]{2,1,0:T(8,128)}, u32[]{:S(2)}, u32[]{:S(2)}) collective-permute-start(f32[8,32,384]{2,1,0:T(8,128)} %dynamic-slice_bitcast_fusion.6), channel_id=1, source_target_pairs={{0,4},{1,5},{2,6},{3,7},{4,0},{5,1},{6,2},{7,3},{8,12},{9,13},{10,... | collective-permute-start | bytes 1179656 | tf_op jit(solution)/shard_map/ppermute | solution.py:31
  51.2 3.4 %collective-permute-done.2 = f32[4,2,32,384]{3,2,1,0:T(8,128)} collective-permute-done((f32[4,2,32,384]{3,2,1,0:T(8,128)}, f32[4,2,32,384]{3,2,1,0:T(8,128)}, u32[]{:S(2)}, u32[]{:S(2)}) %collective-permute-start.2) | collective-permute-done | bytes 393248 | tf_op jit(solution)/shard_map/ppermute | solution.py:31
  54.6 2.1 %bitcast_add_fusion.5 = (f32[4,2,32,384]{3,2,1,0:T(8,128)}, f32[4,2,32,384]{3,2,1,0:T(8,128)}) fusion(f32[4,2,32,384]{3,2,1,0:T(8,128)} %collective-permute-done.2, f32[8,4,2,32,384]{4,3,2,1,0:T(8,128)S(1)} %shard_map.64, s32[]{:T(128)S(6)} %select_n.200, f32[4,2,32,384]{3,2,1,0:T(8,128)} %collective-permute-done.5, s32[]{:T(128)S(6)} %select_n.210), kind=kLoop, calls=%fused_computation.18 | loop fusion | flops 196608 | bytes 2359304 | tf_op jit(solution)/shard_map/add | solution.py:59
  56.7 3.0 %collective-permute-start.6 = (f32[4,2,32,384]{3,2,1,0:T(8,128)}, f32[4,2,32,384]{3,2,1,0:T(8,128)}, u32[]{:S(2)}, u32[]{:S(2)}) collective-permute-start(f32[4,2,32,384]{3,2,1,0:T(8,128)} %get-tuple-element.12), channel_id=1, source_target_pairs={{0,56},{1,57},{2,58},{3,59},{4,60},{5,61},{6,62},{7,63},{8,0},{9,1... | collective-permute-start | bytes 1179656 | tf_op jit(solution)/shard_map/ppermute | solution.py:31
  60.3 1.2 bitcast_add_fusion.1
  61.7 2.2 %collective-permute-start.22 = (f32[16,384]{1,0:T(8,128)S(1)}, f32[16,384]{1,0:T(8,128)S(1)}, u32[]{:S(2)}, u32[]{:S(2)}) collective-permute-start(f32[16,384]{1,0:T(8,128)S(1)} %get-tuple-element.25), channel_id=1, source_target_pairs={{0,56},{1,57},{2,58},{3,59},{4,60},{5,61},{6,62},{7,63},{8,0},{9,1... | collective-permute-start | bytes 73736 | tf_op jit(solution)/shard_map/ppermute | solution.py:31
  63.8 2.3 %collective-permute-done.6 = f32[4,2,32,384]{3,2,1,0:T(8,128)} collective-permute-done((f32[4,2,32,384]{3,2,1,0:T(8,128)}, f32[4,2,32,384]{3,2,1,0:T(8,128)}, u32[]{:S(2)}, u32[]{:S(2)}) %collective-permute-start.6) | collective-permute-done | bytes 393248 | tf_op jit(solution)/shard_map/ppermute | solution.py:31
  66.1 1.0 bitcast_add_fusion.3
  67.2 2.6 %collective-permute-start.7 = (f32[4,2,32,384]{3,2,1,0:T(8,128)S(1)}, f32[4,2,32,384]{3,2,1,0:T(8,128)S(1)}, u32[]{:S(2)}, u32[]{:S(2)}) collective-permute-start(f32[4,2,32,384]{3,2,1,0:T(8,128)S(1)} %bitcast_add_fusion.3), channel_id=1, source_target_pairs={{0,56},{1,57},{2,58},{3,59},{4,60},{5,61},{6,62},{7,63},{8,0},{9,1... | collective-permute-start | bytes 1179656 | tf_op jit(solution)/shard_map/ppermute | solution.py:31
  69.9 2.0 %collective-permute-start.23 = (f32[32,384]{1,0:T(8,128)S(1)}, f32[32,384]{1,0:T(8,128)S(1)}, u32[]{:S(2)}, u32[]{:S(2)}) collective-permute-start(f32[32,384]{1,0:T(8,128)S(1)} %pad_maximum_fusion.8), channel_id=1, source_target_pairs={{0,56},{1,57},{2,58},{3,59},{4,60},{5,61},{6,62},{7,63},{8,0},{9,1... | collective-permute-start | bytes 147464 | tf_op jit(solution)/shard_map/ppermute | solution.py:31
  71.9 2.1 %collective-permute-done.19 = f32[32,384]{1,0:T(8,128)S(1)} collective-permute-done((f32[32,384]{1,0:T(8,128)S(1)}, f32[32,384]{1,0:T(8,128)S(1)}, u32[]{:S(2)}, u32[]{:S(2)}) %collective-permute-start.19) | collective-permute-done | bytes 49184 | tf_op jit(solution)/shard_map/ppermute | solution.py:31
  75.3 2.5 %collective-permute-start.10 = (f32[1,32,384]{2,1,0:T(8,128)S(1)}, f32[1,32,384]{2,1,0:T(8,128)S(1)}, u32[]{:S(2)}, u32[]{:S(2)}) collective-permute-start(f32[1,32,384]{2,1,0:T(8,128)S(1)} %get-tuple-element.31), channel_id=1, source_target_pairs={{0,3},{1,0},{2,1},{3,2},{4,7},{5,4},{6,5},{7,6},{8,11},{9,8},{10,9... | collective-permute-start | bytes 147464 | tf_op jit(solution)/shard_map/ppermute | solution.py:31
  78.4 3.3 %collective-permute-start.24 = (f32[32,384]{1,0:T(8,128)S(1)}, f32[32,384]{1,0:T(8,128)S(1)}, u32[]{:S(2)}, u32[]{:S(2)}) collective-permute-start(f32[32,384]{1,0:T(8,128)S(1)} %get-tuple-element.20), channel_id=1, source_target_pairs={{0,56},{1,57},{2,58},{3,59},{4,60},{5,61},{6,62},{7,63},{8,0},{9,1... | collective-permute-start | bytes 147464 | tf_op jit(solution)/shard_map/ppermute | solution.py:31
  81.7 1.4 collective-permute-done.8
  83.2 3.3 %collective-permute-start.11 = (f32[2,32,384]{2,1,0:T(8,128)S(1)}, f32[2,32,384]{2,1,0:T(8,128)S(1)}, u32[]{:S(2)}, u32[]{:S(2)}) collective-permute-start(f32[2,32,384]{2,1,0:T(8,128)S(1)} %pad_maximum_fusion.5), channel_id=1, source_target_pairs={{0,3},{1,0},{2,1},{3,2},{4,7},{5,4},{6,5},{7,6},{8,11},{9,8},{10,9... | collective-permute-start | bytes 294920 | tf_op jit(solution)/shard_map/ppermute | solution.py:31
  86.5 2.1 %collective-permute-start.25 = (f32[32,384]{1,0:T(8,128)S(1)}, f32[32,384]{1,0:T(8,128)S(1)}, u32[]{:S(2)}, u32[]{:S(2)}) collective-permute-start(f32[32,384]{1,0:T(8,128)S(1)} %bitcast_add_fusion.10), channel_id=1, source_target_pairs={{0,56},{1,57},{2,58},{3,59},{4,60},{5,61},{6,62},{7,63},{8,0},{9,1... | collective-permute-start | bytes 147464 | tf_op jit(solution)/shard_map/ppermute | solution.py:31
  89.1 1.5 %collective-permute-start.12 = (f32[32,384]{1,0:T(8,128)S(1)}, f32[32,384]{1,0:T(8,128)S(1)}, u32[]{:S(2)}, u32[]{:S(2)}) collective-permute-start(f32[32,384]{1,0:T(8,128)S(1)} %dynamic-slice_bitcast_fusion.20), channel_id=1, source_target_pairs={{0,4},{1,5},{2,6},{3,7},{4,0},{5,1},{6,2},{7,3},{8,12},{9,13},{10,... | collective-permute-start | bytes 147464 | tf_op jit(solution)/shard_map/ppermute | solution.py:31
  91.7 1.6 %collective-permute-done.12 = f32[32,384]{1,0:T(8,128)S(1)} collective-permute-done((f32[32,384]{1,0:T(8,128)S(1)}, f32[32,384]{1,0:T(8,128)S(1)}, u32[]{:S(2)}, u32[]{:S(2)}) %collective-permute-start.12) | collective-permute-done | bytes 49184 | tf_op jit(solution)/shard_map/ppermute | solution.py:31
  93.9 2.2 %shard_map.66 = f32[8,32,128]{2,1,0:T(8,128)} custom-call(f32[32,384]{1,0:T(8,128)} %bitcast_add_fusion.14.left_ref, f32[32,384]{1,0:T(8,128)} %fusion.9.right_ref, s32[1,384]{1,0:T(1,128)} %constant_dynamic-slice_fusion.ids_ref), custom_call_target="tpu_custom_call" | custom-call | tf_op jit(solution)/shard_map/pallas_call | solution.py:138
  96.0 0.8 dynamic-slice_bitcast_fusion.13
  97.3 3.8 %collective-permute-done.26 = f32[4,32,128]{2,1,0:T(8,128)S(1)} collective-permute-done((f32[4,32,128]{2,1,0:T(8,128)S(1)}, f32[4,32,128]{2,1,0:T(8,128)S(1)}, u32[]{:S(2)}, u32[]{:S(2)}) %collective-permute-start.26) | collective-permute-done | bytes 65568 | tf_op jit(solution)/shard_map/ppermute | solution.py:31
  101.2 0.8 bitcast_add_fusion.8
  102.0 3.4 %collective-permute-start.27 = (f32[2,32,128]{2,1,0:T(8,128)S(1)}, f32[2,32,128]{2,1,0:T(8,128)S(1)}, u32[]{:S(2)}, u32[]{:S(2)}) collective-permute-start(f32[2,32,128]{2,1,0:T(8,128)S(1)} %dynamic-slice_bitcast_fusion.21), channel_id=1, source_target_pairs={{0,3},{1,2},{2,1},{3,0},{4,7},{5,6},{6,5},{7,4},{8,11},{9,10},{10,... | collective-permute-start | bytes 98312 | tf_op jit(solution)/shard_map/ppermute | solution.py:31
  105.4 1.9 %collective-permute-done.27 = f32[2,32,128]{2,1,0:T(8,128)S(1)} collective-permute-done((f32[2,32,128]{2,1,0:T(8,128)S(1)}, f32[2,32,128]{2,1,0:T(8,128)S(1)}, u32[]{:S(2)}, u32[]{:S(2)}) %collective-permute-start.27) | collective-permute-done | bytes 32800 | tf_op jit(solution)/shard_map/ppermute | solution.py:31
  107.3 1.5 %collective-permute-start.28 = (f32[32,128]{1,0:T(8,128)S(1)}, f32[32,128]{1,0:T(8,128)S(1)}, u32[]{:S(2)}, u32[]{:S(2)}) collective-permute-start(f32[32,128]{1,0:T(8,128)S(1)} %dynamic-slice_bitcast_fusion.28), channel_id=1, source_target_pairs={{0,4},{1,5},{2,6},{3,7},{4,0},{5,1},{6,2},{7,3},{8,12},{9,13},{10,... | collective-permute-start | bytes 49160 | tf_op jit(solution)/shard_map/ppermute | solution.py:31
  108.9 2.3 %collective-permute-done.28 = f32[32,128]{1,0:T(8,128)S(1)} collective-permute-done((f32[32,128]{1,0:T(8,128)S(1)}, f32[32,128]{1,0:T(8,128)S(1)}, u32[]{:S(2)}, u32[]{:S(2)}) %collective-permute-start.28) | collective-permute-done | bytes 16416 | tf_op jit(solution)/shard_map/ppermute | solution.py:31
  111.2 3.3 %collective-permute-start.29 = (f32[32,128]{1,0:T(8,128)S(1)}, f32[32,128]{1,0:T(8,128)S(1)}, u32[]{:S(2)}, u32[]{:S(2)}) collective-permute-start(f32[32,128]{1,0:T(8,128)S(1)} %bitcast_add_fusion.16), channel_id=1, source_target_pairs={{0,8},{1,9},{2,10},{3,11},{4,12},{5,13},{6,14},{7,15},{8,0},{9,1},... | collective-permute-start | bytes 49160 | tf_op jit(solution)/shard_map/ppermute | solution.py:31
  114.4 1.7 %collective-permute-done.29 = f32[32,128]{1,0:T(8,128)S(1)} collective-permute-done((f32[32,128]{1,0:T(8,128)S(1)}, f32[32,128]{1,0:T(8,128)S(1)}, u32[]{:S(2)}, u32[]{:S(2)}) %collective-permute-start.29) | collective-permute-done | bytes 16416 | tf_op jit(solution)/shard_map/ppermute | solution.py:31
  116.1 1.8 %collective-permute-start.30 = (f32[32,128]{1,0:T(8,128)S(1)}, f32[32,128]{1,0:T(8,128)S(1)}, u32[]{:S(2)}, u32[]{:S(2)}) collective-permute-start(f32[32,128]{1,0:T(8,128)S(1)} %add.367), channel_id=1, source_target_pairs={{0,16},{1,17},{2,18},{3,19},{4,20},{5,21},{6,22},{7,23},{8,24},{9,... | collective-permute-start | bytes 49160 | tf_op jit(solution)/shard_map/ppermute | solution.py:31
  117.9 2.8 %collective-permute-done.30 = f32[32,128]{1,0:T(8,128)S(1)} collective-permute-done((f32[32,128]{1,0:T(8,128)S(1)}, f32[32,128]{1,0:T(8,128)S(1)}, u32[]{:S(2)}, u32[]{:S(2)}) %collective-permute-start.30) | collective-permute-done | bytes 16416 | tf_op jit(solution)/shard_map/ppermute | solution.py:31
  120.8 3.4 %collective-permute-start.31 = (f32[32,128]{1,0:T(8,128)S(1)}, f32[32,128]{1,0:T(8,128)S(1)}, u32[]{:S(2)}, u32[]{:S(2)}) collective-permute-start(f32[32,128]{1,0:T(8,128)S(1)} %add.368), channel_id=1, source_target_pairs={{0,32},{1,33},{2,34},{3,35},{4,36},{5,37},{6,38},{7,39},{8,40},{9,... | collective-permute-start | bytes 49160 | tf_op jit(solution)/shard_map/ppermute | solution.py:31
  124.2 4.2 %collective-permute-done.31 = f32[32,128]{1,0:T(8,128)S(1)} collective-permute-done((f32[32,128]{1,0:T(8,128)S(1)}, f32[32,128]{1,0:T(8,128)S(1)}, u32[]{:S(2)}, u32[]{:S(2)}) %collective-permute-start.31) | collective-permute-done | bytes 16416 | tf_op jit(solution)/shard_map/ppermute | solution.py:31
  128.5 1.2 collective-permute-done.32
  129.7 2.8 %collective-permute-start.33 = (f32[2,32,128]{2,1,0:T(8,128)S(1)}, f32[2,32,128]{2,1,0:T(8,128)S(1)}, u32[]{:S(2)}, u32[]{:S(2)}) collective-permute-start(f32[2,32,128]{2,1,0:T(8,128)S(1)} %pad_maximum_fusion.9), channel_id=1, source_target_pairs={{0,128},{64,192},{128,0},{192,64},{1,129},{65,193},{129,1},{193,65... | collective-permute-start | bytes 98312 | tf_op jit(solution)/shard_map/ppermute | solution.py:156
  132.5 2.7 %collective-permute-done.33 = f32[2,32,128]{2,1,0:T(8,128)S(1)} collective-permute-done((f32[2,32,128]{2,1,0:T(8,128)S(1)}, f32[2,32,128]{2,1,0:T(8,128)S(1)}, u32[]{:S(2)}, u32[]{:S(2)}) %collective-permute-start.33) | collective-permute-done | bytes 32800 | tf_op jit(solution)/shard_map/ppermute | solution.py:156
  135.6 3.7 %collective-permute-done.34 = f32[32,128]{1,0:T(8,128)S(1)} collective-permute-done((f32[32,128]{1,0:T(8,128)S(1)}, f32[32,128]{1,0:T(8,128)S(1)}, u32[]{:S(2)}, u32[]{:S(2)}) %collective-permute-start.34) | collective-permute-done | bytes 16416 | tf_op jit(solution)/shard_map/ppermute | solution.py:31
  139.3 2.1 %collective-permute-start.35 = (f32[32,128]{1,0:T(8,128)S(1)}, f32[32,128]{1,0:T(8,128)S(1)}, u32[]{:S(2)}, u32[]{:S(2)}) collective-permute-start(f32[32,128]{1,0:T(8,128)S(1)} %add.370), channel_id=1, source_target_pairs={{0,3},{1,2},{2,1},{3,0},{4,7},{5,6},{6,5},{7,4},{8,11},{9,10},{10,... | collective-permute-start | bytes 49160 | tf_op jit(solution)/shard_map/ppermute | solution.py:31
  141.4 2.8 %collective-permute-done.35 = f32[32,128]{1,0:T(8,128)S(1)} collective-permute-done((f32[32,128]{1,0:T(8,128)S(1)}, f32[32,128]{1,0:T(8,128)S(1)}, u32[]{:S(2)}, u32[]{:S(2)}) %collective-permute-start.35) | collective-permute-done | bytes 16416 | tf_op jit(solution)/shard_map/ppermute | solution.py:31
  144.8 3.2 %collective-permute-done.36 = f32[32,128]{1,0:T(8,128)S(1)} collective-permute-done((f32[32,128]{1,0:T(8,128)S(1)}, f32[32,128]{1,0:T(8,128)S(1)}, u32[]{:S(2)}, u32[]{:S(2)}) %collective-permute-start.36) | collective-permute-done | bytes 16416 | tf_op jit(solution)/shard_map/ppermute | solution.py:31
  (82 shorter events, 9.7 us)
Async XLA Ops:
  0.0 59.7 %copy-start = (s32[1,24576]{1,0:T(1,128)S(1)}, s32[1,24576]{1,0:T(1,128)}, u32[]{:S(2)}) copy-start(s32[1,24576]{1,0:T(1,128)} %param.8) | copy-start | bytes 294916
  0.9 3.5 %copy-start.2 = (bf16[172,24576]{1,0:T(8,128)(2,1)S(1)}, bf16[172,24576]{1,0:T(8,128)(2,1)}, u32[]{:S(2)}) copy-start(bf16[172,24576]{1,0:T(8,128)(2,1)} %input_ref.3) | copy-start | bytes 25362436
  7.9 1.6 %copy-start.1 = (f32[4,2,8,32,384]{4,3,2,1,0:T(8,128)}, f32[4,2,8,32,384]{4,3,2,1,0:T(8,128)S(1)}, u32[]{:S(2)}) copy-start(f32[4,2,8,32,384]{4,3,2,1,0:T(8,128)S(1)} %shard_map.65) | copy-start | bytes 9437188
  9.5 4.5 %copy-start.7 = (bf16[64,32]{0,1:T(8,128)(2,1)S(1)}, bf16[64,32]{0,1:T(8,128)(2,1)}, u32[]{:S(2)}) copy-start(bf16[64,32]{0,1:T(8,128)(2,1)} %param.10) | copy-start | bytes 12292
  10.7 12.4 %collective-permute-start.13 = (f32[1,8,32,384]{3,2,1,0:T(8,128)}, f32[1,8,32,384]{3,2,1,0:T(8,128)}, u32[]{:S(2)}, u32[]{:S(2)}) collective-permute-start(f32[1,8,32,384]{3,2,1,0:T(8,128)} %get-tuple-element.7), channel_id=1, source_target_pairs={{0,1},{1,2},{2,3},{3,0},{4,5},{5,6},{6,7},{7,4},{8,9},{9,10},{10,1... | collective-permute-start | bytes 1179656 | tf_op jit(solution)/shard_map/ppermute | solution.py:31
  12.3 10.9 %collective-permute-start.15 = (f32[1,8,32,384]{3,2,1,0:T(8,128)}, f32[1,8,32,384]{3,2,1,0:T(8,128)}, u32[]{:S(2)}, u32[]{:S(2)}) collective-permute-start(f32[1,8,32,384]{3,2,1,0:T(8,128)} %get-tuple-element.9), channel_id=1, source_target_pairs={{0,3},{1,0},{2,1},{3,2},{4,7},{5,4},{6,5},{7,6},{8,11},{9,8},{10,9... | collective-permute-start | bytes 1179656 | tf_op jit(solution)/shard_map/ppermute | solution.py:31
  14.1 1.9 %copy-start.3 = (bf16[64,24576]{1,0:T(8,128)(2,1)S(1)}, bf16[64,24576]{1,0:T(8,128)(2,1)}, u32[]{:S(2)}) copy-start(bf16[64,24576]{1,0:T(8,128)(2,1)} %input_ref.2) | copy-start | bytes 9437188
  18.1 6.5 %copy-start.6 = (f32[1,8,32,384]{3,2,1,0:T(8,128)S(1)}, f32[1,8,32,384]{3,2,1,0:T(8,128)}, u32[]{:S(2)}) copy-start(f32[1,8,32,384]{3,2,1,0:T(8,128)} %get-tuple-element.10) | copy-start | bytes 1179652
  18.1 9.1 %copy-start.5 = (f32[1,8,32,384]{3,2,1,0:T(8,128)S(1)}, f32[1,8,32,384]{3,2,1,0:T(8,128)}, u32[]{:S(2)}) copy-start(f32[1,8,32,384]{3,2,1,0:T(8,128)} %get-tuple-element.8) | copy-start | bytes 1179652
  18.2 11.6 %collective-permute-start = (f32[2,2,32,384]{3,2,1,0:T(8,128)S(1)}, f32[2,2,32,384]{3,2,1,0:T(8,128)S(1)}, u32[]{:S(2)}, u32[]{:S(2)}) collective-permute-start(f32[2,2,32,384]{3,2,1,0:T(8,128)S(1)} %get-tuple-element.15), channel_id=1, source_target_pairs={{0,8},{1,9},{2,10},{3,11},{4,12},{5,13},{6,14},{7,15},{8,16},{9,17... | collective-permute-start | bytes 589832 | tf_op jit(solution)/shard_map/ppermute | solution.py:31
  20.2 9.6 %collective-permute-start.4 = (f32[2,2,32,384]{3,2,1,0:T(8,128)S(1)}, f32[2,2,32,384]{3,2,1,0:T(8,128)S(1)}, u32[]{:S(2)}, u32[]{:S(2)}) collective-permute-start(f32[2,2,32,384]{3,2,1,0:T(8,128)S(1)} %get-tuple-element.17), channel_id=1, source_target_pairs={{0,56},{1,57},{2,58},{3,59},{4,60},{5,61},{6,62},{7,63},{8,0},{9,1... | collective-permute-start | bytes 589832 | tf_op jit(solution)/shard_map/ppermute | solution.py:31
  25.6 20.0 %collective-permute-start.14 = (f32[2,8,32,384]{3,2,1,0:T(8,128)}, f32[2,8,32,384]{3,2,1,0:T(8,128)}, u32[]{:S(2)}, u32[]{:S(2)}) collective-permute-start(f32[2,8,32,384]{3,2,1,0:T(8,128)} %pad_maximum_fusion), channel_id=1, source_target_pairs={{0,1},{1,2},{2,3},{3,0},{4,5},{5,6},{6,7},{7,4},{8,9},{9,10},{10,1... | collective-permute-start | bytes 2359304 | tf_op jit(solution)/shard_map/ppermute | solution.py:31
  28.1 18.1 %collective-permute-start.16 = (f32[2,8,32,384]{3,2,1,0:T(8,128)}, f32[2,8,32,384]{3,2,1,0:T(8,128)}, u32[]{:S(2)}, u32[]{:S(2)}) collective-permute-start(f32[2,8,32,384]{3,2,1,0:T(8,128)} %pad_maximum_fusion.1), channel_id=1, source_target_pairs={{0,3},{1,0},{2,1},{3,2},{4,7},{5,4},{6,5},{7,6},{8,11},{9,8},{10,9... | collective-permute-start | bytes 2359304 | tf_op jit(solution)/shard_map/ppermute | solution.py:31
  31.4 9.8 %collective-permute-start.1 = (f32[4,2,32,384]{3,2,1,0:T(8,128)}, f32[4,2,32,384]{3,2,1,0:T(8,128)}, u32[]{:S(2)}, u32[]{:S(2)}) collective-permute-start(f32[4,2,32,384]{3,2,1,0:T(8,128)} %pad_maximum_fusion.2), channel_id=1, source_target_pairs={{0,8},{1,9},{2,10},{3,11},{4,12},{5,13},{6,14},{7,15},{8,16},{9,17... | collective-permute-start | bytes 1179656 | tf_op jit(solution)/shard_map/ppermute | solution.py:31
  35.0 16.2 %collective-permute-start.5 = (f32[4,2,32,384]{3,2,1,0:T(8,128)}, f32[4,2,32,384]{3,2,1,0:T(8,128)}, u32[]{:S(2)}, u32[]{:S(2)}) collective-permute-start(f32[4,2,32,384]{3,2,1,0:T(8,128)} %pad_maximum_fusion.3), channel_id=1, source_target_pairs={{0,56},{1,57},{2,58},{3,59},{4,60},{5,61},{6,62},{7,63},{8,0},{9,1... | collective-permute-start | bytes 1179656 | tf_op jit(solution)/shard_map/ppermute | solution.py:31
  43.0 11.6 %collective-permute-start.2 = (f32[4,2,32,384]{3,2,1,0:T(8,128)}, f32[4,2,32,384]{3,2,1,0:T(8,128)}, u32[]{:S(2)}, u32[]{:S(2)}) collective-permute-start(f32[4,2,32,384]{3,2,1,0:T(8,128)} %bitcast_add_fusion.4), channel_id=1, source_target_pairs={{0,8},{1,9},{2,10},{3,11},{4,12},{5,13},{6,14},{7,15},{8,16},{9,17... | collective-permute-start | bytes 1179656 | tf_op jit(solution)/shard_map/ppermute | solution.py:31
  48.0 0.9 copy-start.4
  49.7 10.6 %collective-permute-start.17 = (f32[8,32,384]{2,1,0:T(8,128)}, f32[8,32,384]{2,1,0:T(8,128)}, u32[]{:S(2)}, u32[]{:S(2)}) collective-permute-start(f32[8,32,384]{2,1,0:T(8,128)} %dynamic-slice_bitcast_fusion.6), channel_id=1, source_target_pairs={{0,4},{1,5},{2,6},{3,7},{4,0},{5,1},{6,2},{7,3},{8,12},{9,13},{10,... | collective-permute-start | bytes 1179656 | tf_op jit(solution)/shard_map/ppermute | solution.py:31
  56.7 9.4 %collective-permute-start.6 = (f32[4,2,32,384]{3,2,1,0:T(8,128)}, f32[4,2,32,384]{3,2,1,0:T(8,128)}, u32[]{:S(2)}, u32[]{:S(2)}) collective-permute-start(f32[4,2,32,384]{3,2,1,0:T(8,128)} %get-tuple-element.12), channel_id=1, source_target_pairs={{0,56},{1,57},{2,58},{3,59},{4,60},{5,61},{6,62},{7,63},{8,0},{9,1... | collective-permute-start | bytes 1179656 | tf_op jit(solution)/shard_map/ppermute | solution.py:31
  60.3 14.2 %collective-permute-start.3 = (f32[4,2,32,384]{3,2,1,0:T(8,128)}, f32[4,2,32,384]{3,2,1,0:T(8,128)S(1)}, u32[]{:S(2)}, u32[]{:S(2)}) collective-permute-start(f32[4,2,32,384]{3,2,1,0:T(8,128)} %get-tuple-element.11), channel_id=1, source_target_pairs={{0,8},{1,9},{2,10},{3,11},{4,12},{5,13},{6,14},{7,15},{8,16},{9,17... | collective-permute-start | bytes 1179656 | tf_op jit(solution)/shard_map/ppermute | solution.py:31
  61.5 8.3 %collective-permute-start.18 = (f32[16,384]{1,0:T(8,128)S(1)}, f32[16,384]{1,0:T(8,128)S(1)}, u32[]{:S(2)}, u32[]{:S(2)}) collective-permute-start(f32[16,384]{1,0:T(8,128)S(1)} %get-tuple-element.23), channel_id=1, source_target_pairs={{0,8},{1,9},{2,10},{3,11},{4,12},{5,13},{6,14},{7,15},{8,16},{9,17... | collective-permute-start | bytes 73736 | tf_op jit(solution)/shard_map/ppermute | solution.py:31
  61.7 62.5 %copy-start.8 = (s32[32]{0:T(128)S(1)}, s32[32]{0:T(128)}, u32[]{:S(2)}) copy-start(s32[32]{0:T(128)} %param.9) | copy-start | bytes 388
  61.7 8.0 %collective-permute-start.22 = (f32[16,384]{1,0:T(8,128)S(1)}, f32[16,384]{1,0:T(8,128)S(1)}, u32[]{:S(2)}, u32[]{:S(2)}) collective-permute-start(f32[16,384]{1,0:T(8,128)S(1)} %get-tuple-element.25), channel_id=1, source_target_pairs={{0,56},{1,57},{2,58},{3,59},{4,60},{5,61},{6,62},{7,63},{8,0},{9,1... | collective-permute-start | bytes 73736 | tf_op jit(solution)/shard_map/ppermute | solution.py:31
  67.2 8.0 %collective-permute-start.7 = (f32[4,2,32,384]{3,2,1,0:T(8,128)S(1)}, f32[4,2,32,384]{3,2,1,0:T(8,128)S(1)}, u32[]{:S(2)}, u32[]{:S(2)}) collective-permute-start(f32[4,2,32,384]{3,2,1,0:T(8,128)S(1)} %bitcast_add_fusion.3), channel_id=1, source_target_pairs={{0,56},{1,57},{2,58},{3,59},{4,60},{5,61},{6,62},{7,63},{8,0},{9,1... | collective-permute-start | bytes 1179656 | tf_op jit(solution)/shard_map/ppermute | solution.py:31
  69.7 4.2 %collective-permute-start.19 = (f32[32,384]{1,0:T(8,128)S(1)}, f32[32,384]{1,0:T(8,128)S(1)}, u32[]{:S(2)}, u32[]{:S(2)}) collective-permute-start(f32[32,384]{1,0:T(8,128)S(1)} %pad_maximum_fusion.7), channel_id=1, source_target_pairs={{0,8},{1,9},{2,10},{3,11},{4,12},{5,13},{6,14},{7,15},{8,16},{9,17... | collective-permute-start | bytes 147464 | tf_op jit(solution)/shard_map/ppermute | solution.py:31
  69.9 7.9 %collective-permute-start.23 = (f32[32,384]{1,0:T(8,128)S(1)}, f32[32,384]{1,0:T(8,128)S(1)}, u32[]{:S(2)}, u32[]{:S(2)}) collective-permute-start(f32[32,384]{1,0:T(8,128)S(1)} %pad_maximum_fusion.8), channel_id=1, source_target_pairs={{0,56},{1,57},{2,58},{3,59},{4,60},{5,61},{6,62},{7,63},{8,0},{9,1... | collective-permute-start | bytes 147464 | tf_op jit(solution)/shard_map/ppermute | solution.py:31
  73.9 4.4 %collective-permute-start.20 = (f32[32,384]{1,0:T(8,128)S(1)}, f32[32,384]{1,0:T(8,128)S(1)}, u32[]{:S(2)}, u32[]{:S(2)}) collective-permute-start(f32[32,384]{1,0:T(8,128)S(1)} %bitcast_add_fusion.11), channel_id=1, source_target_pairs={{0,8},{1,9},{2,10},{3,11},{4,12},{5,13},{6,14},{7,15},{8,16},{9,17... | collective-permute-start | bytes 147464 | tf_op jit(solution)/shard_map/ppermute | solution.py:31
  75.3 6.4 %collective-permute-start.10 = (f32[1,32,384]{2,1,0:T(8,128)S(1)}, f32[1,32,384]{2,1,0:T(8,128)S(1)}, u32[]{:S(2)}, u32[]{:S(2)}) collective-permute-start(f32[1,32,384]{2,1,0:T(8,128)S(1)} %get-tuple-element.31), channel_id=1, source_target_pairs={{0,3},{1,0},{2,1},{3,2},{4,7},{5,4},{6,5},{7,6},{8,11},{9,8},{10,9... | collective-permute-start | bytes 147464 | tf_op jit(solution)/shard_map/ppermute | solution.py:31
  77.8 5.3 %collective-permute-start.8 = (f32[1,32,384]{2,1,0:T(8,128)S(1)}, f32[1,32,384]{2,1,0:T(8,128)S(1)}, u32[]{:S(2)}, u32[]{:S(2)}) collective-permute-start(f32[1,32,384]{2,1,0:T(8,128)S(1)} %get-tuple-element.29), channel_id=1, source_target_pairs={{0,1},{1,2},{2,3},{3,0},{4,5},{5,6},{6,7},{7,4},{8,9},{9,10},{10,1... | collective-permute-start | bytes 147464 | tf_op jit(solution)/shard_map/ppermute | solution.py:31
  78.4 8.1 %collective-permute-start.24 = (f32[32,384]{1,0:T(8,128)S(1)}, f32[32,384]{1,0:T(8,128)S(1)}, u32[]{:S(2)}, u32[]{:S(2)}) collective-permute-start(f32[32,384]{1,0:T(8,128)S(1)} %get-tuple-element.20), channel_id=1, source_target_pairs={{0,56},{1,57},{2,58},{3,59},{4,60},{5,61},{6,62},{7,63},{8,0},{9,1... | collective-permute-start | bytes 147464 | tf_op jit(solution)/shard_map/ppermute | solution.py:31
  81.7 8.9 %collective-permute-start.21 = (f32[32,384]{1,0:T(8,128)S(1)}, f32[32,384]{1,0:T(8,128)S(1)}, u32[]{:S(2)}, u32[]{:S(2)}) collective-permute-start(f32[32,384]{1,0:T(8,128)S(1)} %get-tuple-element.19), channel_id=1, source_target_pairs={{0,8},{1,9},{2,10},{3,11},{4,12},{5,13},{6,14},{7,15},{8,16},{9,17... | collective-permute-start | bytes 147464 | tf_op jit(solution)/shard_map/ppermute | solution.py:31
  83.1 5.9 %collective-permute-start.9 = (f32[2,32,384]{2,1,0:T(8,128)S(1)}, f32[2,32,384]{2,1,0:T(8,128)S(1)}, u32[]{:S(2)}, u32[]{:S(2)}) collective-permute-start(f32[2,32,384]{2,1,0:T(8,128)S(1)} %pad_maximum_fusion.4), channel_id=1, source_target_pairs={{0,1},{1,2},{2,3},{3,0},{4,5},{5,6},{6,7},{7,4},{8,9},{9,10},{10,1... | collective-permute-start | bytes 294920 | tf_op jit(solution)/shard_map/ppermute | solution.py:31
  83.2 5.8 %collective-permute-start.11 = (f32[2,32,384]{2,1,0:T(8,128)S(1)}, f32[2,32,384]{2,1,0:T(8,128)S(1)}, u32[]{:S(2)}, u32[]{:S(2)}) collective-permute-start(f32[2,32,384]{2,1,0:T(8,128)S(1)} %pad_maximum_fusion.5), channel_id=1, source_target_pairs={{0,3},{1,0},{2,1},{3,2},{4,7},{5,4},{6,5},{7,6},{8,11},{9,8},{10,9... | collective-permute-start | bytes 294920 | tf_op jit(solution)/shard_map/ppermute | solution.py:31
  86.5 4.5 %collective-permute-start.25 = (f32[32,384]{1,0:T(8,128)S(1)}, f32[32,384]{1,0:T(8,128)S(1)}, u32[]{:S(2)}, u32[]{:S(2)}) collective-permute-start(f32[32,384]{1,0:T(8,128)S(1)} %bitcast_add_fusion.10), channel_id=1, source_target_pairs={{0,56},{1,57},{2,58},{3,59},{4,60},{5,61},{6,62},{7,63},{8,0},{9,1... | collective-permute-start | bytes 147464 | tf_op jit(solution)/shard_map/ppermute | solution.py:31
  89.1 4.2 %collective-permute-start.12 = (f32[32,384]{1,0:T(8,128)S(1)}, f32[32,384]{1,0:T(8,128)S(1)}, u32[]{:S(2)}, u32[]{:S(2)}) collective-permute-start(f32[32,384]{1,0:T(8,128)S(1)} %dynamic-slice_bitcast_fusion.20), channel_id=1, source_target_pairs={{0,4},{1,5},{2,6},{3,7},{4,0},{5,1},{6,2},{7,3},{8,12},{9,13},{10,... | collective-permute-start | bytes 147464 | tf_op jit(solution)/shard_map/ppermute | solution.py:31
  96.9 4.3 %collective-permute-start.26 = (f32[4,32,128]{2,1,0:T(8,128)S(1)}, f32[4,32,128]{2,1,0:T(8,128)S(1)}, u32[]{:S(2)}, u32[]{:S(2)}) collective-permute-start(f32[4,32,128]{2,1,0:T(8,128)S(1)} %dynamic-slice_bitcast_fusion.13), channel_id=1, source_target_pairs={{0,1},{1,0},{2,3},{3,2},{4,5},{5,4},{6,7},{7,6},{8,9},{9,8},{10,11... | collective-permute-start | bytes 196616 | tf_op jit(solution)/shard_map/ppermute | solution.py:31
  102.0 5.3 %collective-permute-start.27 = (f32[2,32,128]{2,1,0:T(8,128)S(1)}, f32[2,32,128]{2,1,0:T(8,128)S(1)}, u32[]{:S(2)}, u32[]{:S(2)}) collective-permute-start(f32[2,32,128]{2,1,0:T(8,128)S(1)} %dynamic-slice_bitcast_fusion.21), channel_id=1, source_target_pairs={{0,3},{1,2},{2,1},{3,0},{4,7},{5,6},{6,5},{7,4},{8,11},{9,10},{10,... | collective-permute-start | bytes 98312 | tf_op jit(solution)/shard_map/ppermute | solution.py:31
  107.3 3.8 %collective-permute-start.28 = (f32[32,128]{1,0:T(8,128)S(1)}, f32[32,128]{1,0:T(8,128)S(1)}, u32[]{:S(2)}, u32[]{:S(2)}) collective-permute-start(f32[32,128]{1,0:T(8,128)S(1)} %dynamic-slice_bitcast_fusion.28), channel_id=1, source_target_pairs={{0,4},{1,5},{2,6},{3,7},{4,0},{5,1},{6,2},{7,3},{8,12},{9,13},{10,... | collective-permute-start | bytes 49160 | tf_op jit(solution)/shard_map/ppermute | solution.py:31
  111.2 5.0 %collective-permute-start.29 = (f32[32,128]{1,0:T(8,128)S(1)}, f32[32,128]{1,0:T(8,128)S(1)}, u32[]{:S(2)}, u32[]{:S(2)}) collective-permute-start(f32[32,128]{1,0:T(8,128)S(1)} %bitcast_add_fusion.16), channel_id=1, source_target_pairs={{0,8},{1,9},{2,10},{3,11},{4,12},{5,13},{6,14},{7,15},{8,0},{9,1},... | collective-permute-start | bytes 49160 | tf_op jit(solution)/shard_map/ppermute | solution.py:31
  116.1 4.6 %collective-permute-start.30 = (f32[32,128]{1,0:T(8,128)S(1)}, f32[32,128]{1,0:T(8,128)S(1)}, u32[]{:S(2)}, u32[]{:S(2)}) collective-permute-start(f32[32,128]{1,0:T(8,128)S(1)} %add.367), channel_id=1, source_target_pairs={{0,16},{1,17},{2,18},{3,19},{4,20},{5,21},{6,22},{7,23},{8,24},{9,... | collective-permute-start | bytes 49160 | tf_op jit(solution)/shard_map/ppermute | solution.py:31
  120.8 7.6 %collective-permute-start.31 = (f32[32,128]{1,0:T(8,128)S(1)}, f32[32,128]{1,0:T(8,128)S(1)}, u32[]{:S(2)}, u32[]{:S(2)}) collective-permute-start(f32[32,128]{1,0:T(8,128)S(1)} %add.368), channel_id=1, source_target_pairs={{0,32},{1,33},{2,34},{3,35},{4,36},{5,37},{6,38},{7,39},{8,40},{9,... | collective-permute-start | bytes 49160 | tf_op jit(solution)/shard_map/ppermute | solution.py:31
  128.5 1.2 collective-permute-start.32
  129.7 5.5 %collective-permute-start.33 = (f32[2,32,128]{2,1,0:T(8,128)S(1)}, f32[2,32,128]{2,1,0:T(8,128)S(1)}, u32[]{:S(2)}, u32[]{:S(2)}) collective-permute-start(f32[2,32,128]{2,1,0:T(8,128)S(1)} %pad_maximum_fusion.9), channel_id=1, source_target_pairs={{0,128},{64,192},{128,0},{192,64},{1,129},{65,193},{129,1},{193,65... | collective-permute-start | bytes 98312 | tf_op jit(solution)/shard_map/ppermute | solution.py:156
  135.5 3.8 %collective-permute-start.34 = (f32[32,128]{1,0:T(8,128)S(1)}, f32[32,128]{1,0:T(8,128)S(1)}, u32[]{:S(2)}, u32[]{:S(2)}) collective-permute-start(f32[32,128]{1,0:T(8,128)S(1)} %fusion.12), channel_id=1, source_target_pairs={{0,1},{1,0},{2,3},{3,2},{4,5},{5,4},{6,7},{7,6},{8,9},{9,8},{10,11... | collective-permute-start | bytes 49160 | tf_op jit(solution)/shard_map/ppermute | solution.py:31
  139.3 4.9 %collective-permute-start.35 = (f32[32,128]{1,0:T(8,128)S(1)}, f32[32,128]{1,0:T(8,128)S(1)}, u32[]{:S(2)}, u32[]{:S(2)}) collective-permute-start(f32[32,128]{1,0:T(8,128)S(1)} %add.370), channel_id=1, source_target_pairs={{0,3},{1,2},{2,1},{3,0},{4,7},{5,6},{6,5},{7,4},{8,11},{9,10},{10,... | collective-permute-start | bytes 49160 | tf_op jit(solution)/shard_map/ppermute | solution.py:31
  144.3 3.7 %collective-permute-start.36 = (f32[32,128]{1,0:T(8,128)S(1)}, f32[32,128]{1,0:T(8,128)S(1)}, u32[]{:S(2)}, u32[]{:S(2)}) collective-permute-start(f32[32,128]{1,0:T(8,128)S(1)} %add.371), channel_id=1, source_target_pairs={{0,4},{1,5},{2,6},{3,7},{4,0},{5,1},{6,2},{7,3},{8,12},{9,13},{10,... | collective-permute-start | bytes 49160 | tf_op jit(solution)/shard_map/ppermute | solution.py:31

commit v2 on v0

v2 whole, which is shorter than its diff:
```python
import jax
import jax.numpy as jnp
from jax import lax
from jax.experimental import pallas as pl
from jax.experimental.pallas import tpu as pltpu
from jax.sharding import PartitionSpec as P

ROWS = 32
TOK_GRP = 24576
EX_GRP = 32
Z, X, Y = 8, 2, 4
LEFT = ROWS // Y
RIGHT = ROWS // X
WIDE = TOK_GRP // Z
SUB = WIDE // Y
SIZE = {"z": Z, "x": X, "y": Y}
MIB = 1024 * 1024
SMEM = pl.BlockSpec(memory_space=pltpu.SMEM)
VMEM = pl.BlockSpec(memory_space=pltpu.VMEM)


def parts_of(index):
    return {"z": index // (X * Y), "x": index // Y % X, "y": index % Y}


def index_of(parts):
    return (parts["z"] * X + parts["x"]) * Y + parts["y"]


def send(value, axis, change):
    pairs = []
    for source in range(Z * X * Y):
        parts = parts_of(source)
        parts[axis] = change(parts[axis]) % SIZE[axis]
        pairs.append((source, index_of(parts)))
    return lax.ppermute(value, "par", pairs)


def both_ways(rising, falling, axis):
    return send(rising, axis, lambda at: at + 1), send(falling, axis, lambda at: at - 1)


def mixed(value, axis, bits):
    return send(value, axis, lambda at: at ^ bits)


def local(kernel, at, values, shapes, scratch=(), alias=None):
    lead = [jnp.stack(at)] if at else []
    return pl.pallas_call(
        kernel,
        in_specs=[SMEM] * len(lead) + [VMEM] * len(values),
        out_specs=[VMEM] * len(shapes),
        out_shape=[pltpu.VMEM(shape, jnp.float32) for shape in shapes],
        scratch_shapes=[pltpu.VMEM(shape, jnp.float32) for shape in scratch],
        input_output_aliases=alias or {},
        compiler_params=pltpu.CompilerParams(vmem_limit_bytes=2 * MIB),
    )(*lead, *[pltpu.with_memory_space_constraint(value, pltpu.VMEM) for value in values])


def projections(at_ref, weight_ref, input_ref, buffer, arrived):
    copies = []
    for step in range(Z):
        begin = pl.multiple_of(lax.rem(at_ref[0] + step, Z) * WIDE, WIDE)
        copies.append(
            pltpu.make_async_copy(
                input_ref.at[:, pl.ds(begin, WIDE)], buffer.at[step], arrived.at[step]
            )
        )
        copies[-1].start()
    for step in range(Z):
        copies[step].wait()
        yield lax.dot_general(
            weight_ref[...], buffer[step], (((0,), (0,)), ((), ())), preferred_element_type=jnp.float32
        )


def left_kernel(at_ref, weight_ref, input_ref, *refs):
    outs, rising_ref, falling_ref = refs[:7], refs[7], refs[8]
    buffer, arrived = refs[9:]
    for step, out in enumerate(projections(at_ref, weight_ref, input_ref, buffer, arrived)):
        if step == Z // 2:
            rising_ref[...] = out[: ROWS // 2]
            falling_ref[...] = out[ROWS // 2 :]
        else:
            outs[step - (step > Z // 2)][...] = out


def right_kernel(at_ref, weight_ref, input_ref, own_ref, next_ref, last_ref, rising_ref, falling_ref, *rest):
    buffer, arrived, held = rest
    y, x = at_ref[1], at_ref[2]
    for step, out in enumerate(projections(at_ref, weight_ref, input_ref, buffer, arrived)):
        for sub in range(Y):
            for half in range(X):
                held[sub, half] = out[half * RIGHT : (half + 1) * RIGHT, sub * SUB : (sub + 1) * SUB]
        for half in range(X):
            rows = lax.rem(x + half, X)
            own_ref[half, step] = held[y, rows]
            next_ref[half, step] = held[lax.rem(y + 1, Y), rows]
            last_ref[half, step] = held[lax.rem(y + 3, Y), rows]
            (rising_ref if half == 0 else falling_ref)[step] = held[lax.rem(y + 2, Y), rows]


def projected(kernel, at, weight, inputs, shapes, scratch):
    depth = inputs.shape[0]
    return pl.pallas_call(
        kernel,
        in_specs=[SMEM, VMEM, pl.BlockSpec(memory_space=pltpu.HBM)],
        out_specs=[VMEM] * len(shapes),
        out_shape=[pltpu.VMEM(shape, jnp.float32) for shape in shapes],
        scratch_shapes=[
            pltpu.VMEM((Z, depth, WIDE), jnp.bfloat16),
            pltpu.SemaphoreType.DMA((Z,)),
            *scratch,
        ],
        compiler_params=pltpu.CompilerParams(vmem_limit_bytes=20 * MIB),
    )(jnp.stack(at), weight, pltpu.with_memory_space_constraint(inputs, pltpu.HBM))


def half_add_kernel(ahead_ref, behind_ref, rising_ref, falling_ref, up_ref, down_ref):
    half = rising_ref.shape[0]
    up_ref[:half] = ahead_ref[:half] + rising_ref[...]
    down_ref[half:] = behind_ref[half:] + falling_ref[...]


def half_add(ahead, behind, rising, falling):
    return local(
        half_add_kernel, (), [ahead, behind, rising, falling], [ahead.shape] * 2, alias={0: 0, 1: 1}
    )


def pair_add_kernel(ahead_ref, behind_ref, rising_ref, falling_ref, up_ref, down_ref):
    up_ref[...] = ahead_ref[...] + rising_ref[...]
    down_ref[...] = behind_ref[...] + falling_ref[...]


def pair_add(ahead, behind, rising, falling):
    return local(
        pair_add_kernel, (), [ahead, behind, rising, falling], [ahead.shape] * 2, alias={0: 0, 1: 1}
    )


def ring(chunks, rising, falling, axis):
    far = SIZE[axis] // 2
    moved = both_ways(rising, falling, axis)
    for steps in range(far - 1, 0, -1):
        add = half_add if steps == far - 1 else pair_add
        moved = both_ways(*add(chunks[steps], chunks[SIZE[axis] - steps], *moved), axis)
    return moved


def left_half_kernel(at_ref, own_ref, rising_ref, falling_ref, keep_ref, give_ref, held):
    total = own_ref[...] + rising_ref[...] + falling_ref[...]
    held[0], held[1] = total[: ROWS // 2], total[ROWS // 2 :]
    keep_ref[...] = held[at_ref[0]]
    give_ref[...] = held[1 - at_ref[0]]


def left_quarter_kernel(at_ref, own_ref, moved_ref, keep_ref, give_ref, held):
    total = own_ref[...] + moved_ref[...]
    held[0], held[1] = total[:LEFT], total[LEFT:]
    keep_ref[...] = held[at_ref[0]]
    give_ref[...] = held[1 - at_ref[0]]


def add_kernel(own_ref, moved_ref, out_ref):
    out_ref[...] = own_ref[...] + moved_ref[...]


def right_half_kernel(own_ref, rising_ref, falling_ref, keep_ref, give_ref):
    keep_ref[...] = own_ref[0] + rising_ref[0] + falling_ref[0]
    give_ref[...] = own_ref[1] + rising_ref[1] + falling_ref[1]


def right_chunks_kernel(own_ref, moved_ref, *refs):
    outs, rising_ref, falling_ref = refs[:7], refs[7], refs[8]
    for step in range(Z):
        total = own_ref[step] + moved_ref[step]
        if step == Z // 2:
            rising_ref[...] = total[: RIGHT // 2]
            falling_ref[...] = total[RIGHT // 2 :]
        else:
            outs[step - (step > Z // 2)][...] = total


def three_kernel(own_ref, rising_ref, falling_ref, out_ref):
    out_ref[...] = own_ref[...] + rising_ref[...] + falling_ref[...]


def spread(outs):
    return [*outs[: Z // 2], None, *outs[Z // 2 : Z - 1]], outs[Z - 1], outs[Z]


def feature_kernel(at_ref, left_ref, moved_ref, first_ref, second_ref, pair_ref, ids_ref, out_ref, held):
    left = left_ref[...] + moved_ref[...]
    for sub in range(Y):
        held[sub] = left[:, sub * SUB : (sub + 1) * SUB]
    labels = lax.broadcasted_iota(jnp.int32, (EX_GRP, SUB), 0)
    over = (((1,), (1,)), ((), ()))
    total = jnp.zeros((EX_GRP, LEFT * RIGHT), jnp.float32)
    pieces = [first_ref[...], second_ref[...], pair_ref[0], pair_ref[1]]
    for bits, right in zip((0, 1, 3, 2), pieces):
        sub = at_ref[0] ^ bits
        member = (ids_ref[sub] == labels).astype(jnp.float32).astype(jnp.bfloat16)
        part = held[sub]
        product = jnp.concatenate([part[a : a + 1] * right for a in range(LEFT)], axis=0)
        high = product.astype(jnp.bfloat16)
        low = (product - high.astype(jnp.float32)).astype(jnp.bfloat16)
        total += lax.dot_general(member, high, over, preferred_element_type=jnp.float32)
        total += lax.dot_general(member, low, over, preferred_element_type=jnp.float32)
    out_ref[...] = total


def on_device(activations, out_grads, example_ids, train_flags, in_proj, out_proj):
    at = parts_of(lax.axis_index("par"))
    group = lax.axis_index("grp")
    place = (at["z"], at["y"], at["x"])

    quarter = (X, Z, RIGHT, SUB)
    own, ahead, behind, rising, falling = projected(
        right_kernel, place, out_proj, out_grads, [quarter] * 3 + [quarter[1:]] * 2,
        [pltpu.VMEM((Y, X, RIGHT, SUB), jnp.float32)],
    )
    moved = both_ways(rising, falling, "y")
    left, low, high = spread(
        projected(left_kernel, place, in_proj, activations, [(ROWS, WIDE)] * 7 + [(ROWS // 2, WIDE)] * 2, [])
    )

    rising, falling = ring(left, low, high, "z")
    first, second = (at["y"] ^ (at["y"] >> 1)) & 1, at["y"] >> 1
    keep, give = local(
        left_half_kernel, (first,), [left[0], rising, falling], [(ROWS // 2, WIDE)] * 2,
        [(2, ROWS // 2, WIDE)],
    )
    keep, give = local(
        left_quarter_kernel, (second,), [keep, mixed(give, "y", 1)], [(LEFT, WIDE)] * 2, [(2, LEFT, WIDE)]
    )
    (left,) = local(add_kernel, (), [keep, mixed(give, "y", 3)], [(LEFT, WIDE)])
    left_moved = mixed(left, "x", 1)

    ahead, behind = local(
        right_first_kernel, (), [ahead, behind, *moved], [quarter] * 2, alias={0: 0, 1: 1}
    )
    rising, falling = both_ways(ahead, behind, "y")
    keep, give = local(right_half_kernel, (), [own, rising, falling], [quarter[1:]] * 2)
    right, low, high = spread(
        local(
            right_chunks_kernel, (), [keep, mixed(give, "x", 1)],
            [(RIGHT, SUB)] * 7 + [(RIGHT // 2, SUB)] * 2,
        )
    )
    rising, falling = ring(right, low, high, "z")
    (right,) = local(three_kernel, (), [right[0], rising, falling], [(RIGHT, SUB)])
    near = mixed(right, "y", 1)
    pair = mixed(jnp.stack([right, near]), "y", 3)

    ids = lax.dynamic_slice(example_ids, (0, at["z"] * WIDE), (1, WIDE)).reshape(Y, 1, SUB)
    features = pl.pallas_call(
        feature_kernel,
        in_specs=[SMEM] + [VMEM] * 6,
        out_specs=VMEM,
        out_shape=jax.ShapeDtypeStruct((EX_GRP, LEFT * RIGHT), jnp.float32),
        scratch_shapes=[pltpu.VMEM((Y, LEFT, SUB), jnp.float32)],
        compiler_params=pltpu.CompilerParams(vmem_limit_bytes=8 * MIB),
    )(jnp.stack([at["y"]]), left, left_moved, right, near, pair, ids)
    for bits in (1, 2, 7):
        features = features + mixed(features, "z", bits)

    flags = train_flags.astype(jnp.float32)
    row_side = features * (flags * (1.0 / TOK_GRP))[:, None]
    cols = (features * (1.0 - flags)[:, None])[None]
    for bit in (1, 2):
        other = lax.ppermute(cols, "grp", [(i, i ^ bit) for i in range(4)])
        late = (group & bit) > 0
        cols = jnp.concatenate([jnp.where(late, other, cols), jnp.where(late, cols, other)])
    cols = cols.reshape(4 * EX_GRP, LEFT * RIGHT)
    kernel = lax.dot_general(
        row_side, cols, (((1,), (1,)), ((), ())), precision=lax.Precision.HIGHEST
    )
    kernel = kernel + mixed(kernel, "y", 1)
    kernel = kernel + mixed(kernel, "y", 3)
    return kernel + mixed(kernel, "x", 1)


def right_first_kernel(ahead_ref, behind_ref, rising_ref, falling_ref, up_ref, down_ref):
    up_ref[0] = ahead_ref[0] + rising_ref[...]
    down_ref[1] = behind_ref[1] + falling_ref[...]


def solution(mesh):
    return jax.shard_map(
        on_device,
        mesh=mesh,
        in_specs=(
            P("par", "grp"),
            P("par", "grp"),
            P("grp", None),
            P("grp"),
            P("par", None),
            P("par", None),
        ),
        out_specs=P("grp", None),
        check_vma=False,
    )
```

time: 853 us -> 129 us (0.15); the launches traced: 843 us -> 128 us
  waiting for transfers between devices: 636 us -> 67.1 us
  matrix products: 120 us -> 0.23 us
  local copies, waits for them, and re-layouts: 61.8 us -> 1.99 us
  starting transfers between devices: 1.2 us -> 44.5 us
  Pallas kernels: 0 us -> 13.5 us
  between operations: 13.6 us -> 0.21 us
  other arithmetic: 10.8 us -> 0.81 us
    psum x1 -> x0, waiting for transfers between devices: 628 us -> none  [on_device(): left_proj, right_proj = lax.psum((left_proj, right_proj), 'par')]
    dot_general x18 -> x1, matrix products: 120 us -> 0.23 us  [on_device(): lax.dot_general(row_side, cols, (((1,), (1,)), ((), ())), precision=lax.P...]
    ppermute x3 -> x34, waiting for transfers between devices: 8.05 us -> 67.1 us  [the longest x32 63.6 us: send(): return lax.ppermute(value, 'par', pairs)]
    ppermute x3 -> x34, starting transfers between devices: 1.19 us -> 44.5 us  [the longest x32 41.4 us: send(): return lax.ppermute(value, 'par', pairs)]
    dynamic_slice x36 -> x1, local copies, waits for them, and re-layouts: 41.9 us -> 0.01 us  [on_device(): lax.dynamic_slice(example_ids, (0, at['z'] * WIDE), (1, WIDE))]
    pallas_call x0 -> x16, Pallas kernels: none -> 13.5 us  [the longest x2 10 us: projected(): pl.pallas_call(kernel, in_specs=[SMEM, VMEM, pl.BlockSpec(memory_space=pl...]
    convert_element_type x12 -> x0, other arithmetic: 9.26 us -> none  [add_block(): onehot = (id_block[None, :] == labels[:, None]).astype(jnp.float32)]
    reshape x3 -> x0, local copies, waits for them, and re-layouts: 8.89 us -> none  [the longest x1 3.83 us: token_features(): lefts = left_part.reshape(PROJ_IN, steps, width).transpose(1, 0, 2)]
  transfers between devices with their start and end apart: 4 -> 34, of which waited for: 4 -> 26; matrix products, arithmetic and copies ran while one was open for 1% -> 0% of each run, Pallas kernels for 0% -> 6%
where the time goes in v2:
time: 129 us; the launch traced here: 128 us
  waiting for transfers between devices  67.1 us (52%)
  starting transfers between devices  44.5 us (34%)
  Pallas kernels  13.5 us (10%)
  local copies, waits for them, and re-layouts  1.99 us (2%)
    ppermute x32, waiting for transfers between devices, send(): return lax.ppermute(value, 'par', pairs)  63.6 us
    ppermute x32, starting transfers between devices, send(): return lax.ppermute(value, 'par', pairs)  41.4 us
    pallas_call x2, Pallas kernels, projected(): pl.pallas_call(kernel, in_specs=[SMEM, VMEM, pl.BlockSpec(memory_space=pl...  10 us
    ppermute x2, waiting for transfers between devices, on_device(): other = lax.ppermute(cols, 'grp', [(i, i ^ bit) for i in range(4)])  3.56 us
    ppermute x2, starting transfers between devices, on_device(): other = lax.ppermute(cols, 'grp', [(i, i ^ bit) for i in range(4)])  3.13 us
    pallas_call x13, Pallas kernels, local(): pl.pallas_call(kernel, in_specs=[SMEM] * len(lead) + [VMEM] * len(values)...  2.81 us
  transfers between devices with their start and end apart: 34, of which 26 were waited for; matrix products, arithmetic and copies ran while one was open for 0% of the time, Pallas kernels for 6%

profile of v2, /device:TPU:32, one launch (start us, length us, event | category | flops | bytes accessed | tf_op | source)
XLA Modules:
  0.0 128.4 jit_solution(7725601517556475370)
XLA Ops:
  0.0 0.9 copy.22.weight_ref
  1.0 5.8 %shard_map.71 = (f32[2,8,16,768]{3,2,1,0:T(8,128)S(1)}, f32[2,8,16,768]{3,2,1,0:T(8,128)S(1)}, f32[2,8,16,768]{3,2,1,0:T(8,128)S(1)}, f32[8,16,768]{2,1,0:T(8,128)}, f32[8,16,768]{2,1,0:T(8,128)}) custom-call(s32[3]{0:T(128)S(1)} %pad_add_fusion.at_ref, bf16[172,32]{1,0:T(8,128)(2,1)S(1)} %copy.22.weight_ref, bf16[172,24576]{1,0:T(8,128)(2,1)} %input_ref.3), custom_call_target="tpu_custom_call" | custom-call | tf_op jit(solution)/shard_map/pallas_call | solution.py:105
  6.8 1.7 %collective-permute-start.11 = (f32[8,16,768]{2,1,0:T(8,128)}, f32[8,16,768]{2,1,0:T(8,128)S(1)}, u32[]{:S(2)}, u32[]{:S(2)}) collective-permute-start(f32[8,16,768]{2,1,0:T(8,128)} %get-tuple-element.70), channel_id=1, source_target_pairs={{0,1},{1,2},{2,3},{3,0},{4,5},{5,6},{6,7},{7,4},{8,9},{9,10},{10,1... | collective-permute-start | bytes 1179656 | tf_op jit(solution)/shard_map/ppermute | solution.py:36
  8.4 1.7 %collective-permute-start.12 = (f32[8,16,768]{2,1,0:T(8,128)}, f32[8,16,768]{2,1,0:T(8,128)S(1)}, u32[]{:S(2)}, u32[]{:S(2)}) collective-permute-start(f32[8,16,768]{2,1,0:T(8,128)} %get-tuple-element.71), channel_id=1, source_target_pairs={{0,3},{1,0},{2,1},{3,2},{4,7},{5,4},{6,5},{7,6},{8,11},{9,8},{10,9... | collective-permute-start | bytes 1179656 | tf_op jit(solution)/shard_map/ppermute | solution.py:36
  10.2 4.3 %shard_map.64 = (f32[32,3072]{1,0:T(8,128)S(1)}, f32[32,3072]{1,0:T(8,128)}, f32[32,3072]{1,0:T(8,128)S(1)}, f32[32,3072]{1,0:T(8,128)S(1)}, f32[32,3072]{1,0:T(...) custom-call(s32[3]{0:T(128)S(1)} %pad_add_fusion.at_ref, ...), custom_call_target="tpu_custom_call" | custom-call | tf_op jit(solution)/shard_map/pallas_call | solution.py:105
  14.5 2.0 %collective-permute-start = (f32[16,3072]{1,0:T(8,128)S(1)}, f32[16,3072]{1,0:T(8,128)S(1)}, u32[]{:S(2)}, u32[]{:S(2)}) collective-permute-start(f32[16,3072]{1,0:T(8,128)S(1)} %get-tuple-element.55), channel_id=1, source_target_pairs={{0,8},{1,9},{2,10},{3,11},{4,12},{5,13},{6,14},{7,15},{8,16},{9,17... | collective-permute-start | bytes 589832 | tf_op jit(solution)/shard_map/ppermute | solution.py:36
  16.6 4.2 %collective-permute-done.rising_ref = f32[16,3072]{1,0:T(8,128)S(1)} collective-permute-done((f32[16,3072]{1,0:T(8,128)S(1)}, f32[16,3072]{1,0:T(8,128)S(1)}, u32[]{:S(2)}, u32[]{:S(2)}) %collective-permute-start) | collective-permute-done | bytes 196640 | tf_op jit(solution)/shard_map/ppermute | solution.py:36
  20.8 1.8 %collective-permute-done.1.falling_ref = f32[16,3072]{1,0:T(8,128)S(1)} collective-permute-done((f32[16,3072]{1,0:T(8,128)S(1)}, f32[16,3072]{1,0:T(8,128)S(1)}, u32[]{:S(2)}, u32[]{:S(2)}) %collective-permute-start.1) | collective-permute-done | bytes 196640 | tf_op jit(solution)/shard_map/ppermute | solution.py:36
  22.7 3.2 %collective-permute-start.2 = (f32[32,3072]{1,0:T(8,128)S(1)}, f32[32,3072]{1,0:T(8,128)S(1)}, u32[]{:S(2)}, u32[]{:S(2)}) collective-permute-start(f32[32,3072]{1,0:T(8,128)S(1)} %get-tuple-element.57), channel_id=1, source_target_pairs={{0,8},{1,9},{2,10},{3,11},{4,12},{5,13},{6,14},{7,15},{8,16},{9,17... | collective-permute-start | bytes 1179656 | tf_op jit(solution)/shard_map/ppermute | solution.py:36
  25.9 0.1 shard_map.72
  26.0 0.3 collective-permute-start.13
  26.3 3.0 %collective-permute-start.14 = (f32[2,8,16,768]{3,2,1,0:T(8,128)S(1)}, f32[2,8,16,768]{3,2,1,0:T(8,128)S(1)}, u32[]{:S(2)}, u32[]{:S(2)}) collective-permute-start(f32[2,8,16,768]{3,2,1,0:T(8,128)S(1)} %get-tuple-element.73), channel_id=1, source_target_pairs={{0,3},{1,0},{2,1},{3,2},{4,7},{5,4},{6,5},{7,6},{8,11},{9,8},{10,9... | collective-permute-start | bytes 2359304 | tf_op jit(solution)/shard_map/ppermute | solution.py:36
  29.3 3.9 %collective-permute-done.2.rising_ref = f32[32,3072]{1,0:T(8,128)S(1)} collective-permute-done((f32[32,3072]{1,0:T(8,128)S(1)}, f32[32,3072]{1,0:T(8,128)S(1)}, u32[]{:S(2)}, u32[]{:S(2)}) %collective-permute-start.2) | collective-permute-done | bytes 393248 | tf_op jit(solution)/shard_map/ppermute | solution.py:36
  33.2 2.8 %collective-permute-done.3.falling_ref = f32[32,3072]{1,0:T(8,128)S(1)} collective-permute-done((f32[32,3072]{1,0:T(8,128)S(1)}, f32[32,3072]{1,0:T(8,128)S(1)}, u32[]{:S(2)}, u32[]{:S(2)}) %collective-permute-start.3) | collective-permute-done | bytes 393248 | tf_op jit(solution)/shard_map/ppermute | solution.py:36
  36.0 0.1 shard_map.66
  36.2 1.8 %collective-permute-start.4 = (f32[32,3072]{1,0:T(8,128)S(1)}, f32[32,3072]{1,0:T(8,128)S(1)}, u32[]{:S(2)}, u32[]{:S(2)}) collective-permute-start(f32[32,3072]{1,0:T(8,128)S(1)} %get-tuple-element.59), channel_id=1, source_target_pairs={{0,8},{1,9},{2,10},{3,11},{4,12},{5,13},{6,14},{7,15},{8,16},{9,17... | collective-permute-start | bytes 1179656 | tf_op jit(solution)/shard_map/ppermute | solution.py:36
  38.0 0.3 collective-permute-start.5
  38.3 6.3 %collective-permute-done.4.rising_ref = f32[32,3072]{1,0:T(8,128)S(1)} collective-permute-done((f32[32,3072]{1,0:T(8,128)S(1)}, f32[32,3072]{1,0:T(8,128)S(1)}, u32[]{:S(2)}, u32[]{:S(2)}) %collective-permute-start.4) | collective-permute-done | bytes 393248 | tf_op jit(solution)/shard_map/ppermute | solution.py:36
  44.6 1.5 %collective-permute-done.5.falling_ref = f32[32,3072]{1,0:T(8,128)S(1)} collective-permute-done((f32[32,3072]{1,0:T(8,128)S(1)}, f32[32,3072]{1,0:T(8,128)S(1)}, u32[]{:S(2)}, u32[]{:S(2)}) %collective-permute-start.5) | collective-permute-done | bytes 393248 | tf_op jit(solution)/shard_map/ppermute | solution.py:36
  46.1 2.1 %shard_map.67 = (f32[32,3072]{1,0:T(8,128)}, f32[32,3072]{1,0:T(8,128)}) custom-call(f32[32,3072]{1,0:T(8,128)} %get-tuple-element.49.ahead_ref, f32[32,3072]{1,0:T(8,128)} %get-tuple-element.50.behind_ref, f32[32,3072]{1,0:T(8,128)S(1)} %collective-permute-done.4.rising_ref, ...), custom_call_target="tpu_custom_call", output_to_operand_aliasing={{0}: (0, {}), {1}: (1, {})} | custom-call | tf_op jit(solution)/shard_map/pallas_call | solution.py:49
  48.2 1.7 %collective-permute-start.6 = (f32[32,3072]{1,0:T(8,128)}, f32[32,3072]{1,0:T(8,128)S(1)}, u32[]{:S(2)}, u32[]{:S(2)}) collective-permute-start(f32[32,3072]{1,0:T(8,128)} %get-tuple-element.61), channel_id=1, source_target_pairs={{0,8},{1,9},{2,10},{3,11},{4,12},{5,13},{6,14},{7,15},{8,16},{9,17... | collective-permute-start | bytes 1179656 | tf_op jit(solution)/shard_map/ppermute | solution.py:36
  49.9 0.3 collective-permute-start.7
  50.4 1.6 %collective-permute-start.15 = (f32[8,16,768]{2,1,0:T(8,128)S(1)}, f32[8,16,768]{2,1,0:T(8,128)S(1)}, u32[]{:S(2)}, u32[]{:S(2)}) collective-permute-start(f32[8,16,768]{2,1,0:T(8,128)S(1)} %get-tuple-element.75), channel_id=1, source_target_pairs={{0,4},{1,5},{2,6},{3,7},{4,0},{5,1},{6,2},{7,3},{8,12},{9,13},{10,... | collective-permute-start | bytes 1179656 | tf_op jit(solution)/shard_map/ppermute | solution.py:36
  52.0 4.2 %collective-permute-done.6.rising_ref = f32[32,3072]{1,0:T(8,128)S(1)} collective-permute-done((f32[32,3072]{1,0:T(8,128)}, f32[32,3072]{1,0:T(8,128)S(1)}, u32[]{:S(2)}, u32[]{:S(2)}) %collective-permute-start.6) | collective-permute-done | bytes 393248 | tf_op jit(solution)/shard_map/ppermute | solution.py:36
  56.2 1.7 %collective-permute-done.7.falling_ref = f32[32,3072]{1,0:T(8,128)S(1)} collective-permute-done((f32[32,3072]{1,0:T(8,128)}, f32[32,3072]{1,0:T(8,128)S(1)}, u32[]{:S(2)}, u32[]{:S(2)}) %collective-permute-start.7) | collective-permute-done | bytes 393248 | tf_op jit(solution)/shard_map/ppermute | solution.py:36
  57.9 1.0 copy-done.2
  59.2 1.9 %collective-permute-start.16 = (f32[8,768]{1,0:T(8,128)S(1)}, f32[8,768]{1,0:T(8,128)S(1)}, u32[]{:S(2)}, u32[]{:S(2)}) collective-permute-start(f32[8,768]{1,0:T(8,128)S(1)} %get-tuple-element.83), channel_id=1, source_target_pairs={{0,8},{1,9},{2,10},{3,11},{4,12},{5,13},{6,14},{7,15},{8,16},{9,17... | collective-permute-start | bytes 73736 | tf_op jit(solution)/shard_map/ppermute | solution.py:36
  61.0 0.3 collective-permute-start.17
  61.3 1.8 %collective-permute-done.16.rising_ref = f32[8,768]{1,0:T(8,128)S(1)} collective-permute-done((f32[8,768]{1,0:T(8,128)S(1)}, f32[8,768]{1,0:T(8,128)S(1)}, u32[]{:S(2)}, u32[]{:S(2)}) %collective-permute-start.16) | collective-permute-done | bytes 24608 | tf_op jit(solution)/shard_map/ppermute | solution.py:36
  63.1 1.8 %collective-permute-done.17.falling_ref = f32[8,768]{1,0:T(8,128)S(1)} collective-permute-done((f32[8,768]{1,0:T(8,128)S(1)}, f32[8,768]{1,0:T(8,128)S(1)}, u32[]{:S(2)}, u32[]{:S(2)}) %collective-permute-start.17) | collective-permute-done | bytes 24608 | tf_op jit(solution)/shard_map/ppermute | solution.py:36
  64.9 1.6 %collective-permute-start.18 = (f32[16,768]{1,0:T(8,128)S(1)}, f32[16,768]{1,0:T(8,128)S(1)}, u32[]{:S(2)}, u32[]{:S(2)}) collective-permute-start(f32[16,768]{1,0:T(8,128)S(1)} %get-tuple-element.85), channel_id=1, source_target_pairs={{0,8},{1,9},{2,10},{3,11},{4,12},{5,13},{6,14},{7,15},{8,16},{9,17... | collective-permute-start | bytes 147464 | tf_op jit(solution)/shard_map/ppermute | solution.py:36
  66.4 0.5 collective-permute-start.19
  67.0 2.1 %collective-permute-done.18.rising_ref = f32[16,768]{1,0:T(8,128)S(1)} collective-permute-done((f32[16,768]{1,0:T(8,128)S(1)}, f32[16,768]{1,0:T(8,128)S(1)}, u32[]{:S(2)}, u32[]{:S(2)}) %collective-permute-start.18) | collective-permute-done | bytes 49184 | tf_op jit(solution)/shard_map/ppermute | solution.py:36
  69.0 1.5 %collective-permute-done.19.falling_ref = f32[16,768]{1,0:T(8,128)S(1)} collective-permute-done((f32[16,768]{1,0:T(8,128)S(1)}, f32[16,768]{1,0:T(8,128)S(1)}, u32[]{:S(2)}, u32[]{:S(2)}) %collective-permute-start.19) | collective-permute-done | bytes 49184 | tf_op jit(solution)/shard_map/ppermute | solution.py:36
  70.6 2.1 %collective-permute-start.20 = (f32[16,768]{1,0:T(8,128)S(1)}, f32[16,768]{1,0:T(8,128)S(1)}, u32[]{:S(2)}, u32[]{:S(2)}) collective-permute-start(f32[16,768]{1,0:T(8,128)S(1)} %get-tuple-element.87), channel_id=1, source_target_pairs={{0,8},{1,9},{2,10},{3,11},{4,12},{5,13},{6,14},{7,15},{8,16},{9,17... | collective-permute-start | bytes 147464 | tf_op jit(solution)/shard_map/ppermute | solution.py:36
  72.7 2.1 %collective-permute-start.9 = (f32[8,3072]{1,0:T(8,128)S(1)}, f32[8,3072]{1,0:T(8,128)S(1)}, u32[]{:S(2)}, u32[]{:S(2)}) collective-permute-start(f32[8,3072]{1,0:T(8,128)S(1)} %get-tuple-element.66), channel_id=1, source_target_pairs={{0,3},{1,2},{2,1},{3,0},{4,7},{5,6},{6,5},{7,4},{8,11},{9,10},{10,... | collective-permute-start | bytes 294920 | tf_op jit(solution)/shard_map/ppermute | solution.py:36
  74.9 1.9 %collective-permute-done.21.falling_ref = f32[16,768]{1,0:T(8,128)S(1)} collective-permute-done((f32[16,768]{1,0:T(8,128)S(1)}, f32[16,768]{1,0:T(8,128)S(1)}, u32[]{:S(2)}, u32[]{:S(2)}) %collective-permute-start.21) | collective-permute-done | bytes 49184 | tf_op jit(solution)/shard_map/ppermute | solution.py:36
  76.8 1.4 %collective-permute-start.22 = (f32[16,768]{1,0:T(8,128)S(1)}, f32[16,768]{1,0:T(8,128)S(1)}, u32[]{:S(2)}, u32[]{:S(2)}) collective-permute-start(f32[16,768]{1,0:T(8,128)S(1)} %get-tuple-element.89), channel_id=1, source_target_pairs={{0,8},{1,9},{2,10},{3,11},{4,12},{5,13},{6,14},{7,15},{8,16},{9,17... | collective-permute-start | bytes 147464 | tf_op jit(solution)/shard_map/ppermute | solution.py:36
  78.2 0.7 collective-permute-start.23
  78.9 2.1 %collective-permute-done.22.rising_ref = f32[16,768]{1,0:T(8,128)S(1)} collective-permute-done((f32[16,768]{1,0:T(8,128)S(1)}, f32[16,768]{1,0:T(8,128)S(1)}, u32[]{:S(2)}, u32[]{:S(2)}) %collective-permute-start.22) | collective-permute-done | bytes 49184 | tf_op jit(solution)/shard_map/ppermute | solution.py:36
  81.0 1.3 %collective-permute-done.23.falling_ref = f32[16,768]{1,0:T(8,128)S(1)} collective-permute-done((f32[16,768]{1,0:T(8,128)S(1)}, f32[16,768]{1,0:T(8,128)S(1)}, u32[]{:S(2)}, u32[]{:S(2)}) %collective-permute-start.23) | collective-permute-done | bytes 49184 | tf_op jit(solution)/shard_map/ppermute | solution.py:36
  82.3 1.3 %collective-permute-start.24 = (f32[16,768]{1,0:T(8,128)S(1)}, f32[16,768]{1,0:T(8,128)S(1)}, u32[]{:S(2)}, u32[]{:S(2)}) collective-permute-start(f32[16,768]{1,0:T(8,128)S(1)} %shard_map.78.first_ref), channel_id=1, source_target_pairs={{0,1},{1,0},{2,3},{3,2},{4,5},{5,4},{6,7},{7,6},{8,9},{9,8},{10,11... | collective-permute-start | bytes 147464 | tf_op jit(solution)/shard_map/ppermute | solution.py:36
  83.6 1.6 %collective-permute-start.10 = (f32[8,3072]{1,0:T(8,128)S(1)}, f32[8,3072]{1,0:T(8,128)S(1)}, u32[]{:S(2)}, u32[]{:S(2)}) collective-permute-start(f32[8,3072]{1,0:T(8,128)S(1)} %shard_map.70.left_ref), channel_id=1, source_target_pairs={{0,4},{1,5},{2,6},{3,7},{4,0},{5,1},{6,2},{7,3},{8,12},{9,13},{10,... | collective-permute-start | bytes 294920 | tf_op jit(solution)/shard_map/ppermute | solution.py:36
  85.3 1.2 collective-permute-done.24.second_ref
  86.5 1.4 %collective-permute-start.25 = (f32[2,16,768]{2,1,0:T(8,128)S(1)}, f32[2,16,768]{2,1,0:T(8,128)S(1)}, u32[]{:S(2)}, u32[]{:S(2)}) collective-permute-start(f32[2,16,768]{2,1,0:T(8,128)S(1)} %pad_maximum_fusion), channel_id=1, source_target_pairs={{0,3},{1,2},{2,1},{3,0},{4,7},{5,6},{6,5},{7,4},{8,11},{9,10},{10,... | collective-permute-start | bytes 294920 | tf_op jit(solution)/shard_map/ppermute | solution.py:36
  87.9 0.4 collective-permute-done.10.moved_ref
  88.3 4.0 %collective-permute-done.25.pair_ref = f32[2,16,768]{2,1,0:T(8,128)S(1)} collective-permute-done((f32[2,16,768]{2,1,0:T(8,128)S(1)}, f32[2,16,768]{2,1,0:T(8,128)S(1)}, u32[]{:S(2)}, u32[]{:S(2)}) %collective-permute-start.25) | collective-permute-done | bytes 98336 | tf_op jit(solution)/shard_map/ppermute | solution.py:36
  92.4 0.6 shard_map.79
  93.0 0.8 collective-permute-start.26
  93.8 3.0 %collective-permute-done.26 = f32[32,128]{1,0:T(8,128)S(1)} collective-permute-done((f32[32,128]{1,0:T(8,128)S(1)}, f32[32,128]{1,0:T(8,128)S(1)}, u32[]{:S(2)}, u32[]{:S(2)}) %collective-permute-start.26) | collective-permute-done | bytes 16416 | tf_op jit(solution)/shard_map/ppermute | solution.py:36
  96.8 2.0 %collective-permute-start.27 = (f32[32,128]{1,0:T(8,128)S(1)}, f32[32,128]{1,0:T(8,128)S(1)}, u32[]{:S(2)}, u32[]{:S(2)}) collective-permute-start(f32[32,128]{1,0:T(8,128)S(1)} %add.33), channel_id=1, source_target_pairs={{0,16},{1,17},{2,18},{3,19},{4,20},{5,21},{6,22},{7,23},{8,24},{9,... | collective-permute-start | bytes 49160 | tf_op jit(solution)/shard_map/ppermute | solution.py:36
  98.8 2.6 %collective-permute-done.27 = f32[32,128]{1,0:T(8,128)S(1)} collective-permute-done((f32[32,128]{1,0:T(8,128)S(1)}, f32[32,128]{1,0:T(8,128)S(1)}, u32[]{:S(2)}, u32[]{:S(2)}) %collective-permute-start.27) | collective-permute-done | bytes 16416 | tf_op jit(solution)/shard_map/ppermute | solution.py:36
  101.4 2.7 %collective-permute-start.28 = (f32[32,128]{1,0:T(8,128)S(1)}, f32[32,128]{1,0:T(8,128)S(1)}, u32[]{:S(2)}, u32[]{:S(2)}) collective-permute-start(f32[32,128]{1,0:T(8,128)S(1)} %add.34), channel_id=1, source_target_pairs={{0,56},{1,57},{2,58},{3,59},{4,60},{5,61},{6,62},{7,63},{8,48},{9,... | collective-permute-start | bytes 49160 | tf_op jit(solution)/shard_map/ppermute | solution.py:36
  104.1 4.0 %collective-permute-done.28 = f32[32,128]{1,0:T(8,128)S(1)} collective-permute-done((f32[32,128]{1,0:T(8,128)S(1)}, f32[32,128]{1,0:T(8,128)S(1)}, u32[]{:S(2)}, u32[]{:S(2)}) %collective-permute-start.28) | collective-permute-done | bytes 16416 | tf_op jit(solution)/shard_map/ppermute | solution.py:36
  108.3 1.2 collective-permute-done.29
  109.4 3.1 %collective-permute-start.30 = (f32[2,32,128]{2,1,0:T(8,128)S(1)}, f32[2,32,128]{2,1,0:T(8,128)S(1)}, u32[]{:S(2)}, u32[]{:S(2)}) collective-permute-start(f32[2,32,128]{2,1,0:T(8,128)S(1)} %pad_maximum_fusion.2), channel_id=1, source_target_pairs={{0,128},{64,192},{128,0},{192,64},{1,129},{65,193},{129,1},{193,65... | collective-permute-start | bytes 98312 | tf_op jit(solution)/shard_map/ppermute | solution.py:272
  112.6 2.4 %collective-permute-done.30 = f32[2,32,128]{2,1,0:T(8,128)S(1)} collective-permute-done((f32[2,32,128]{2,1,0:T(8,128)S(1)}, f32[2,32,128]{2,1,0:T(8,128)S(1)}, u32[]{:S(2)}, u32[]{:S(2)}) %collective-permute-start.30) | collective-permute-done | bytes 32800 | tf_op jit(solution)/shard_map/ppermute | solution.py:272
  115.0 0.2 fusion
  115.4 3.7 %collective-permute-done.31 = f32[32,128]{1,0:T(8,128)S(1)} collective-permute-done((f32[32,128]{1,0:T(8,128)S(1)}, f32[32,128]{1,0:T(8,128)S(1)}, u32[]{:S(2)}, u32[]{:S(2)}) %collective-permute-start.31) | collective-permute-done | bytes 16416 | tf_op jit(solution)/shard_map/ppermute | solution.py:36
  119.1 1.4 %collective-permute-start.32 = (f32[32,128]{1,0:T(8,128)S(1)}, f32[32,128]{1,0:T(8,128)S(1)}, u32[]{:S(2)}, u32[]{:S(2)}) collective-permute-start(f32[32,128]{1,0:T(8,128)S(1)} %add.36), channel_id=1, source_target_pairs={{0,3},{1,2},{2,1},{3,0},{4,7},{5,6},{6,5},{7,4},{8,11},{9,10},{10,... | collective-permute-start | bytes 49160 | tf_op jit(solution)/shard_map/ppermute | solution.py:36
  120.4 3.6 %collective-permute-done.32 = f32[32,128]{1,0:T(8,128)S(1)} collective-permute-done((f32[32,128]{1,0:T(8,128)S(1)}, f32[32,128]{1,0:T(8,128)S(1)}, u32[]{:S(2)}, u32[]{:S(2)}) %collective-permute-start.32) | collective-permute-done | bytes 16416 | tf_op jit(solution)/shard_map/ppermute | solution.py:36
  124.0 1.6 %collective-permute-start.33 = (f32[32,128]{1,0:T(8,128)S(1)}, f32[32,128]{1,0:T(8,128)S(1)}, u32[]{:S(2)}, u32[]{:S(2)}) collective-permute-start(f32[32,128]{1,0:T(8,128)S(1)} %add.37), channel_id=1, source_target_pairs={{0,4},{1,5},{2,6},{3,7},{4,0},{5,1},{6,2},{7,3},{8,12},{9,13},{10,... | collective-permute-start | bytes 49160 | tf_op jit(solution)/shard_map/ppermute | solution.py:36
  125.6 2.2 %collective-permute-done.33 = f32[32,128]{1,0:T(8,128)S(1)} collective-permute-done((f32[32,128]{1,0:T(8,128)S(1)}, f32[32,128]{1,0:T(8,128)S(1)}, u32[]{:S(2)}, u32[]{:S(2)}) %collective-permute-start.33) | collective-permute-done | bytes 16416 | tf_op jit(solution)/shard_map/ppermute | solution.py:36
  127.7 0.6 add.38
  (47 shorter events, 1.1 us)
Async XLA Ops:
  0.0 87.9 %copy-start = (s32[1,24576]{1,0:T(1,128)S(1)}, s32[1,24576]{1,0:T(1,128)}, u32[]{:S(2)}) copy-start(s32[1,24576]{1,0:T(1,128)} %param.8) | copy-start | bytes 294916
  0.0 10.1 %copy-start.3 = (bf16[64,32]{0,1:T(8,128)(2,1)S(1)}, bf16[64,32]{0,1:T(8,128)(2,1)}, u32[]{:S(2)}) copy-start(bf16[64,32]{0,1:T(8,128)(2,1)} %param.10) | copy-start | bytes 12292
  6.8 97.4 %copy-start.4 = (s32[32]{0:T(128)S(1)}, s32[32]{0:T(128)}, u32[]{:S(2)}) copy-start(s32[32]{0:T(128)} %param.9) | copy-start | bytes 388
  6.8 19.1 %collective-permute-start.11 = (f32[8,16,768]{2,1,0:T(8,128)}, f32[8,16,768]{2,1,0:T(8,128)S(1)}, u32[]{:S(2)}, u32[]{:S(2)}) collective-permute-start(f32[8,16,768]{2,1,0:T(8,128)} %get-tuple-element.70), channel_id=1, source_target_pairs={{0,1},{1,2},{2,3},{3,0},{4,5},{5,6},{6,7},{7,4},{8,9},{9,10},{10,1... | collective-permute-start | bytes 1179656 | tf_op jit(solution)/shard_map/ppermute | solution.py:36
  8.4 17.5 %collective-permute-start.12 = (f32[8,16,768]{2,1,0:T(8,128)}, f32[8,16,768]{2,1,0:T(8,128)S(1)}, u32[]{:S(2)}, u32[]{:S(2)}) collective-permute-start(f32[8,16,768]{2,1,0:T(8,128)} %get-tuple-element.71), channel_id=1, source_target_pairs={{0,3},{1,0},{2,1},{3,2},{4,7},{5,4},{6,5},{7,6},{8,11},{9,8},{10,9... | collective-permute-start | bytes 1179656 | tf_op jit(solution)/shard_map/ppermute | solution.py:36
  14.5 35.9 %copy-start.1 = (f32[32,3072]{1,0:T(8,128)}, f32[32,3072]{1,0:T(8,128)S(1)}, u32[]{:S(2)}) copy-start(f32[32,3072]{1,0:T(8,128)S(1)} %get-tuple-element.48.own_ref) | copy-start | bytes 1179652
  14.5 6.3 %collective-permute-start = (f32[16,3072]{1,0:T(8,128)S(1)}, f32[16,3072]{1,0:T(8,128)S(1)}, u32[]{:S(2)}, u32[]{:S(2)}) collective-permute-start(f32[16,3072]{1,0:T(8,128)S(1)} %get-tuple-element.55), channel_id=1, source_target_pairs={{0,8},{1,9},{2,10},{3,11},{4,12},{5,13},{6,14},{7,15},{8,16},{9,17... | collective-permute-start | bytes 589832 | tf_op jit(solution)/shard_map/ppermute | solution.py:36
  16.5 6.1 %collective-permute-start.1 = (f32[16,3072]{1,0:T(8,128)S(1)}, f32[16,3072]{1,0:T(8,128)S(1)}, u32[]{:S(2)}, u32[]{:S(2)}) collective-permute-start(f32[16,3072]{1,0:T(8,128)S(1)} %get-tuple-element.56), channel_id=1, source_target_pairs={{0,56},{1,57},{2,58},{3,59},{4,60},{5,61},{6,62},{7,63},{8,0},{9,1... | collective-permute-start | bytes 589832 | tf_op jit(solution)/shard_map/ppermute | solution.py:36
  22.7 10.6 %collective-permute-start.2 = (f32[32,3072]{1,0:T(8,128)S(1)}, f32[32,3072]{1,0:T(8,128)S(1)}, u32[]{:S(2)}, u32[]{:S(2)}) collective-permute-start(f32[32,3072]{1,0:T(8,128)S(1)} %get-tuple-element.57), channel_id=1, source_target_pairs={{0,8},{1,9},{2,10},{3,11},{4,12},{5,13},{6,14},{7,15},{8,16},{9,17... | collective-permute-start | bytes 1179656 | tf_op jit(solution)/shard_map/ppermute | solution.py:36
  25.9 10.2 %collective-permute-start.3 = (f32[32,3072]{1,0:T(8,128)S(1)}, f32[32,3072]{1,0:T(8,128)S(1)}, u32[]{:S(2)}, u32[]{:S(2)}) collective-permute-start(f32[32,3072]{1,0:T(8,128)S(1)} %get-tuple-element.58), channel_id=1, source_target_pairs={{0,56},{1,57},{2,58},{3,59},{4,60},{5,61},{6,62},{7,63},{8,0},{9,1... | collective-permute-start | bytes 1179656 | tf_op jit(solution)/shard_map/ppermute | solution.py:36
  26.0 24.2 %collective-permute-start.13 = (f32[2,8,16,768]{3,2,1,0:T(8,128)S(1)}, f32[2,8,16,768]{3,2,1,0:T(8,128)S(1)}, u32[]{:S(2)}, u32[]{:S(2)}) collective-permute-start(f32[2,8,16,768]{3,2,1,0:T(8,128)S(1)} %get-tuple-element.72), channel_id=1, source_target_pairs={{0,1},{1,2},{2,3},{3,0},{4,5},{5,6},{6,7},{7,4},{8,9},{9,10},{10,1... | collective-permute-start | bytes 2359304 | tf_op jit(solution)/shard_map/ppermute | solution.py:36
  26.3 23.9 %collective-permute-start.14 = (f32[2,8,16,768]{3,2,1,0:T(8,128)S(1)}, f32[2,8,16,768]{3,2,1,0:T(8,128)S(1)}, u32[]{:S(2)}, u32[]{:S(2)}) collective-permute-start(f32[2,8,16,768]{3,2,1,0:T(8,128)S(1)} %get-tuple-element.73), channel_id=1, source_target_pairs={{0,3},{1,0},{2,1},{3,2},{4,7},{5,4},{6,5},{7,6},{8,11},{9,8},{10,9... | collective-permute-start | bytes 2359304 | tf_op jit(solution)/shard_map/ppermute | solution.py:36
  36.2 8.4 %collective-permute-start.4 = (f32[32,3072]{1,0:T(8,128)S(1)}, f32[32,3072]{1,0:T(8,128)S(1)}, u32[]{:S(2)}, u32[]{:S(2)}) collective-permute-start(f32[32,3072]{1,0:T(8,128)S(1)} %get-tuple-element.59), channel_id=1, source_target_pairs={{0,8},{1,9},{2,10},{3,11},{4,12},{5,13},{6,14},{7,15},{8,16},{9,17... | collective-permute-start | bytes 1179656 | tf_op jit(solution)/shard_map/ppermute | solution.py:36
  38.0 8.1 %collective-permute-start.5 = (f32[32,3072]{1,0:T(8,128)S(1)}, f32[32,3072]{1,0:T(8,128)S(1)}, u32[]{:S(2)}, u32[]{:S(2)}) collective-permute-start(f32[32,3072]{1,0:T(8,128)S(1)} %get-tuple-element.60), channel_id=1, source_target_pairs={{0,56},{1,57},{2,58},{3,59},{4,60},{5,61},{6,62},{7,63},{8,0},{9,1... | collective-permute-start | bytes 1179656 | tf_op jit(solution)/shard_map/ppermute | solution.py:36
  48.2 8.0 %collective-permute-start.6 = (f32[32,3072]{1,0:T(8,128)}, f32[32,3072]{1,0:T(8,128)S(1)}, u32[]{:S(2)}, u32[]{:S(2)}) collective-permute-start(f32[32,3072]{1,0:T(8,128)} %get-tuple-element.61), channel_id=1, source_target_pairs={{0,8},{1,9},{2,10},{3,11},{4,12},{5,13},{6,14},{7,15},{8,16},{9,17... | collective-permute-start | bytes 1179656 | tf_op jit(solution)/shard_map/ppermute | solution.py:36
  49.9 8.0 %collective-permute-start.7 = (f32[32,3072]{1,0:T(8,128)}, f32[32,3072]{1,0:T(8,128)S(1)}, u32[]{:S(2)}, u32[]{:S(2)}) collective-permute-start(f32[32,3072]{1,0:T(8,128)} %get-tuple-element.62), channel_id=1, source_target_pairs={{0,56},{1,57},{2,58},{3,59},{4,60},{5,61},{6,62},{7,63},{8,0},{9,1... | collective-permute-start | bytes 1179656 | tf_op jit(solution)/shard_map/ppermute | solution.py:36
  50.4 8.8 %collective-permute-start.15 = (f32[8,16,768]{2,1,0:T(8,128)S(1)}, f32[8,16,768]{2,1,0:T(8,128)S(1)}, u32[]{:S(2)}, u32[]{:S(2)}) collective-permute-start(f32[8,16,768]{2,1,0:T(8,128)S(1)} %get-tuple-element.75), channel_id=1, source_target_pairs={{0,4},{1,5},{2,6},{3,7},{4,0},{5,1},{6,2},{7,3},{8,12},{9,13},{10,... | collective-permute-start | bytes 1179656 | tf_op jit(solution)/shard_map/ppermute | solution.py:36
  57.9 1.0 copy-start.2
  59.0 13.7 %collective-permute-start.8 = (f32[16,3072]{1,0:T(8,128)S(1)}, f32[16,3072]{1,0:T(8,128)S(1)}, u32[]{:S(2)}, u32[]{:S(2)}) collective-permute-start(f32[16,3072]{1,0:T(8,128)S(1)} %get-tuple-element.64), channel_id=1, source_target_pairs={{0,1},{1,0},{2,3},{3,2},{4,5},{5,4},{6,7},{7,6},{8,9},{9,8},{10,11... | collective-permute-start | bytes 589832 | tf_op jit(solution)/shard_map/ppermute | solution.py:36
  59.2 3.9 %collective-permute-start.16 = (f32[8,768]{1,0:T(8,128)S(1)}, f32[8,768]{1,0:T(8,128)S(1)}, u32[]{:S(2)}, u32[]{:S(2)}) collective-permute-start(f32[8,768]{1,0:T(8,128)S(1)} %get-tuple-element.83), channel_id=1, source_target_pairs={{0,8},{1,9},{2,10},{3,11},{4,12},{5,13},{6,14},{7,15},{8,16},{9,17... | collective-permute-start | bytes 73736 | tf_op jit(solution)/shard_map/ppermute | solution.py:36
  61.0 3.8 %collective-permute-start.17 = (f32[8,768]{1,0:T(8,128)S(1)}, f32[8,768]{1,0:T(8,128)S(1)}, u32[]{:S(2)}, u32[]{:S(2)}) collective-permute-start(f32[8,768]{1,0:T(8,128)S(1)} %get-tuple-element.84), channel_id=1, source_target_pairs={{0,56},{1,57},{2,58},{3,59},{4,60},{5,61},{6,62},{7,63},{8,0},{9,1... | collective-permute-start | bytes 73736 | tf_op jit(solution)/shard_map/ppermute | solution.py:36
  64.9 4.2 %collective-permute-start.18 = (f32[16,768]{1,0:T(8,128)S(1)}, f32[16,768]{1,0:T(8,128)S(1)}, u32[]{:S(2)}, u32[]{:S(2)}) collective-permute-start(f32[16,768]{1,0:T(8,128)S(1)} %get-tuple-element.85), channel_id=1, source_target_pairs={{0,8},{1,9},{2,10},{3,11},{4,12},{5,13},{6,14},{7,15},{8,16},{9,17... | collective-permute-start | bytes 147464 | tf_op jit(solution)/shard_map/ppermute | solution.py:36
  66.4 4.1 %collective-permute-start.19 = (f32[16,768]{1,0:T(8,128)S(1)}, f32[16,768]{1,0:T(8,128)S(1)}, u32[]{:S(2)}, u32[]{:S(2)}) collective-permute-start(f32[16,768]{1,0:T(8,128)S(1)} %get-tuple-element.86), channel_id=1, source_target_pairs={{0,56},{1,57},{2,58},{3,59},{4,60},{5,61},{6,62},{7,63},{8,0},{9,1... | collective-permute-start | bytes 147464 | tf_op jit(solution)/shard_map/ppermute | solution.py:36
  70.6 4.3 %collective-permute-start.20 = (f32[16,768]{1,0:T(8,128)S(1)}, f32[16,768]{1,0:T(8,128)S(1)}, u32[]{:S(2)}, u32[]{:S(2)}) collective-permute-start(f32[16,768]{1,0:T(8,128)S(1)} %get-tuple-element.87), channel_id=1, source_target_pairs={{0,8},{1,9},{2,10},{3,11},{4,12},{5,13},{6,14},{7,15},{8,16},{9,17... | collective-permute-start | bytes 147464 | tf_op jit(solution)/shard_map/ppermute | solution.py:36
  72.7 4.1 %collective-permute-start.21 = (f32[16,768]{1,0:T(8,128)S(1)}, f32[16,768]{1,0:T(8,128)S(1)}, u32[]{:S(2)}, u32[]{:S(2)}) collective-permute-start(f32[16,768]{1,0:T(8,128)S(1)} %get-tuple-element.88), channel_id=1, source_target_pairs={{0,56},{1,57},{2,58},{3,59},{4,60},{5,61},{6,62},{7,63},{8,0},{9,1... | collective-permute-start | bytes 147464 | tf_op jit(solution)/shard_map/ppermute | solution.py:36
  72.7 10.9 %collective-permute-start.9 = (f32[8,3072]{1,0:T(8,128)S(1)}, f32[8,3072]{1,0:T(8,128)S(1)}, u32[]{:S(2)}, u32[]{:S(2)}) collective-permute-start(f32[8,3072]{1,0:T(8,128)S(1)} %get-tuple-element.66), channel_id=1, source_target_pairs={{0,3},{1,2},{2,1},{3,0},{4,7},{5,6},{6,5},{7,4},{8,11},{9,10},{10,... | collective-permute-start | bytes 294920 | tf_op jit(solution)/shard_map/ppermute | solution.py:36
  76.8 4.2 %collective-permute-start.22 = (f32[16,768]{1,0:T(8,128)S(1)}, f32[16,768]{1,0:T(8,128)S(1)}, u32[]{:S(2)}, u32[]{:S(2)}) collective-permute-start(f32[16,768]{1,0:T(8,128)S(1)} %get-tuple-element.89), channel_id=1, source_target_pairs={{0,8},{1,9},{2,10},{3,11},{4,12},{5,13},{6,14},{7,15},{8,16},{9,17... | collective-permute-start | bytes 147464 | tf_op jit(solution)/shard_map/ppermute | solution.py:36
  78.2 4.1 %collective-permute-start.23 = (f32[16,768]{1,0:T(8,128)S(1)}, f32[16,768]{1,0:T(8,128)S(1)}, u32[]{:S(2)}, u32[]{:S(2)}) collective-permute-start(f32[16,768]{1,0:T(8,128)S(1)} %get-tuple-element.90), channel_id=1, source_target_pairs={{0,56},{1,57},{2,58},{3,59},{4,60},{5,61},{6,62},{7,63},{8,0},{9,1... | collective-permute-start | bytes 147464 | tf_op jit(solution)/shard_map/ppermute | solution.py:36
  82.3 4.2 %collective-permute-start.24 = (f32[16,768]{1,0:T(8,128)S(1)}, f32[16,768]{1,0:T(8,128)S(1)}, u32[]{:S(2)}, u32[]{:S(2)}) collective-permute-start(f32[16,768]{1,0:T(8,128)S(1)} %shard_map.78.first_ref), channel_id=1, source_target_pairs={{0,1},{1,0},{2,3},{3,2},{4,5},{5,4},{6,7},{7,6},{8,9},{9,8},{10,11... | collective-permute-start | bytes 147464 | tf_op jit(solution)/shard_map/ppermute | solution.py:36
  83.6 4.7 %collective-permute-start.10 = (f32[8,3072]{1,0:T(8,128)S(1)}, f32[8,3072]{1,0:T(8,128)S(1)}, u32[]{:S(2)}, u32[]{:S(2)}) collective-permute-start(f32[8,3072]{1,0:T(8,128)S(1)} %shard_map.70.left_ref), channel_id=1, source_target_pairs={{0,4},{1,5},{2,6},{3,7},{4,0},{5,1},{6,2},{7,3},{8,12},{9,13},{10,... | collective-permute-start | bytes 294920 | tf_op jit(solution)/shard_map/ppermute | solution.py:36
  86.5 5.9 %collective-permute-start.25 = (f32[2,16,768]{2,1,0:T(8,128)S(1)}, f32[2,16,768]{2,1,0:T(8,128)S(1)}, u32[]{:S(2)}, u32[]{:S(2)}) collective-permute-start(f32[2,16,768]{2,1,0:T(8,128)S(1)} %pad_maximum_fusion), channel_id=1, source_target_pairs={{0,3},{1,2},{2,1},{3,0},{4,7},{5,6},{6,5},{7,4},{8,11},{9,10},{10,... | collective-permute-start | bytes 294920 | tf_op jit(solution)/shard_map/ppermute | solution.py:36
  93.0 3.8 %collective-permute-start.26 = (f32[32,128]{1,0:T(8,128)S(1)}, f32[32,128]{1,0:T(8,128)S(1)}, u32[]{:S(2)}, u32[]{:S(2)}) collective-permute-start(f32[32,128]{1,0:T(8,128)S(1)} %shard_map.79), channel_id=1, source_target_pairs={{0,8},{1,9},{2,10},{3,11},{4,12},{5,13},{6,14},{7,15},{8,0},{9,1},... | collective-permute-start | bytes 49160 | tf_op jit(solution)/shard_map/ppermute | solution.py:36
  96.8 4.6 %collective-permute-start.27 = (f32[32,128]{1,0:T(8,128)S(1)}, f32[32,128]{1,0:T(8,128)S(1)}, u32[]{:S(2)}, u32[]{:S(2)}) collective-permute-start(f32[32,128]{1,0:T(8,128)S(1)} %add.33), channel_id=1, source_target_pairs={{0,16},{1,17},{2,18},{3,19},{4,20},{5,21},{6,22},{7,23},{8,24},{9,... | collective-permute-start | bytes 49160 | tf_op jit(solution)/shard_map/ppermute | solution.py:36
  101.4 6.7 %collective-permute-start.28 = (f32[32,128]{1,0:T(8,128)S(1)}, f32[32,128]{1,0:T(8,128)S(1)}, u32[]{:S(2)}, u32[]{:S(2)}) collective-permute-start(f32[32,128]{1,0:T(8,128)S(1)} %add.34), channel_id=1, source_target_pairs={{0,56},{1,57},{2,58},{3,59},{4,60},{5,61},{6,62},{7,63},{8,48},{9,... | collective-permute-start | bytes 49160 | tf_op jit(solution)/shard_map/ppermute | solution.py:36
  108.2 1.2 collective-permute-start.29
  109.4 5.5 %collective-permute-start.30 = (f32[2,32,128]{2,1,0:T(8,128)S(1)}, f32[2,32,128]{2,1,0:T(8,128)S(1)}, u32[]{:S(2)}, u32[]{:S(2)}) collective-permute-start(f32[2,32,128]{2,1,0:T(8,128)S(1)} %pad_maximum_fusion.2), channel_id=1, source_target_pairs={{0,128},{64,192},{128,0},{192,64},{1,129},{65,193},{129,1},{193,65... | collective-permute-start | bytes 98312 | tf_op jit(solution)/shard_map/ppermute | solution.py:272
  115.2 3.8 %collective-permute-start.31 = (f32[32,128]{1,0:T(8,128)S(1)}, f32[32,128]{1,0:T(8,128)S(1)}, u32[]{:S(2)}, u32[]{:S(2)}) collective-permute-start(f32[32,128]{1,0:T(8,128)S(1)} %fusion), channel_id=1, source_target_pairs={{0,1},{1,0},{2,3},{3,2},{4,5},{5,4},{6,7},{7,6},{8,9},{9,8},{10,11... | collective-permute-start | bytes 49160 | tf_op jit(solution)/shard_map/ppermute | solution.py:36
  119.1 4.9 %collective-permute-start.32 = (f32[32,128]{1,0:T(8,128)S(1)}, f32[32,128]{1,0:T(8,128)S(1)}, u32[]{:S(2)}, u32[]{:S(2)}) collective-permute-start(f32[32,128]{1,0:T(8,128)S(1)} %add.36), channel_id=1, source_target_pairs={{0,3},{1,2},{2,1},{3,0},{4,7},{5,6},{6,5},{7,4},{8,11},{9,10},{10,... | collective-permute-start | bytes 49160 | tf_op jit(solution)/shard_map/ppermute | solution.py:36
  124.0 3.7 %collective-permute-start.33 = (f32[32,128]{1,0:T(8,128)S(1)}, f32[32,128]{1,0:T(8,128)S(1)}, u32[]{:S(2)}, u32[]{:S(2)}) collective-permute-start(f32[32,128]{1,0:T(8,128)S(1)} %add.37), channel_id=1, source_target_pairs={{0,4},{1,5},{2,6},{3,7},{4,0},{5,1},{6,2},{7,3},{8,12},{9,13},{10,... | collective-permute-start | bytes 49160 | tf_op jit(solution)/shard_map/ppermute | solution.py:36

commit v3 on v2

v3 whole, which is shorter than its diff:
```python
import jax
import jax.numpy as jnp
from jax import lax
from jax.experimental import pallas as pl
from jax.experimental.pallas import tpu as pltpu
from jax.sharding import PartitionSpec as P

ROWS = 32
TOK_GRP = 24576
EX_GRP = 32
Z, X, Y = 8, 2, 4
LEFT = ROWS // Y
RIGHT = ROWS // X
WIDE = TOK_GRP // Z
SUB = WIDE // Y
FAR, REST, ALL = (4,), (3, 5, 2, 6, 1, 7, 0), tuple(range(Z))
SIZE = {"z": Z, "x": X, "y": Y}
MIB = 1024 * 1024
SMEM = pl.BlockSpec(memory_space=pltpu.SMEM)
VMEM = pl.BlockSpec(memory_space=pltpu.VMEM)
ANY = pl.BlockSpec(memory_space=pl.ANY)


def parts_of(index):
    return {"z": index // (X * Y), "x": index // Y % X, "y": index % Y}


def index_of(parts):
    return (parts["z"] * X + parts["x"]) * Y + parts["y"]


def send(value, axis, change):
    pairs = []
    for source in range(Z * X * Y):
        parts = parts_of(source)
        parts[axis] = change(parts[axis]) % SIZE[axis]
        pairs.append((source, index_of(parts)))
    return lax.ppermute(value, "par", pairs)


def both_ways(rising, falling, axis):
    return send(rising, axis, lambda at: at + 1), send(falling, axis, lambda at: at - 1)


def mixed(value, axis, bits):
    return send(value, axis, lambda at: at ^ bits)


def ordered(kernel, count, after):
    return lambda *refs: kernel(*refs[:count], *refs[count + len(after) :])


def local(kernel, at, values, shapes, scratch=(), alias=None, after=()):
    lead = [jnp.stack(at)] if at else []
    return pl.pallas_call(
        ordered(kernel, len(lead) + len(values), after),
        in_specs=[SMEM] * len(lead) + [VMEM] * len(values) + [ANY] * len(after),
        out_specs=[VMEM] * len(shapes),
        out_shape=[pltpu.VMEM(shape, jnp.float32) for shape in shapes],
        scratch_shapes=[pltpu.VMEM(shape, jnp.float32) for shape in scratch],
        input_output_aliases=alias or {},
        compiler_params=pltpu.CompilerParams(vmem_limit_bytes=2 * MIB),
    )(*lead, *[pltpu.with_memory_space_constraint(value, pltpu.VMEM) for value in values], *after)


def projections(weight_ref, input_ref, held, buffer, arrived, starts):
    weight = pltpu.make_async_copy(weight_ref, held, arrived.at[len(starts)])
    weight.start()
    copies = []
    for place, begin in enumerate(starts):
        tokens = pl.ds(pl.multiple_of(begin, WIDE), WIDE)
        copies.append(
            pltpu.make_async_copy(input_ref.at[:, tokens], buffer.at[place], arrived.at[place])
        )
        copies[-1].start()
    weight.wait()
    for copy, place in zip(copies, range(len(starts))):
        copy.wait()
        yield jnp.dot(held[...], buffer[place], preferred_element_type=jnp.float32)


def begins(at_ref, steps):
    return [lax.rem(at_ref[0] + step, Z) * WIDE for step in steps]


def left_far_kernel(at_ref, weight_ref, input_ref, rising_ref, falling_ref, *scratch):
    (out,) = projections(weight_ref, input_ref, *scratch, begins(at_ref, FAR))
    rising_ref[...] = out[: ROWS // 2]
    falling_ref[...] = out[ROWS // 2 :]


def left_kernel(at_ref, weight_ref, input_ref, *refs):
    outs = projections(weight_ref, input_ref, *refs[-3:], begins(at_ref, REST))
    for out_ref, out in zip(refs[: len(REST)], outs):
        out_ref[...] = out


def right_kernel(
    at_ref, weight_ref, input_ref, own_ref, next_ref, last_ref, rising_ref, falling_ref, turned, *scratch
):
    y = at_ref[1]
    outs = projections(weight_ref, input_ref, *scratch, begins(at_ref, ALL))
    for step, out in enumerate(outs):
        for sub in range(Y):
            turned[sub] = out[:, sub * SUB : (sub + 1) * SUB]
        own_ref[step] = turned[y]
        next_ref[step] = turned[lax.rem(y + 1, Y)]
        last_ref[step] = turned[lax.rem(y + 3, Y)]
        (rising_ref if step < Z // 2 else falling_ref)[step % (Z // 2)] = turned[lax.rem(y + 2, Y)]


def projected(kernel, at, weight, inputs, blocks, shapes, turned=(), after=()):
    depth = inputs.shape[0]
    distant = lambda value: pltpu.with_memory_space_constraint(value, pltpu.HBM)
    return pl.pallas_call(
        ordered(kernel, 3, after),
        in_specs=[SMEM, *[pl.BlockSpec(memory_space=pltpu.HBM)] * 2] + [ANY] * len(after),
        out_specs=[VMEM] * len(shapes),
        out_shape=[pltpu.VMEM(shape, jnp.float32) for shape in shapes],
        scratch_shapes=[
            *turned,
            pltpu.VMEM((ROWS, depth), jnp.bfloat16),
            pltpu.VMEM((blocks, depth, WIDE), jnp.bfloat16),
            pltpu.SemaphoreType.DMA((blocks + 1,)),
        ],
        compiler_params=pltpu.CompilerParams(vmem_limit_bytes=20 * MIB),
    )(jnp.stack(at), distant(weight.T), distant(inputs), *after)


def half_add_kernel(ahead_ref, behind_ref, rising_ref, falling_ref, up_ref, down_ref):
    half = rising_ref.shape[0]
    up_ref[:half] = ahead_ref[:half] + rising_ref[...]
    down_ref[half:] = behind_ref[half:] + falling_ref[...]


def pair_add_kernel(ahead_ref, behind_ref, rising_ref, falling_ref, up_ref, down_ref):
    up_ref[...] = ahead_ref[...] + rising_ref[...]
    down_ref[...] = behind_ref[...] + falling_ref[...]


def step_add(ahead, behind, moved, after, half=False):
    kernel = half_add_kernel if half else pair_add_kernel
    return local(
        kernel, (), [ahead, behind, *moved], [ahead.shape] * 2, alias={0: 0, 1: 1}, after=after
    )


def left_half_kernel(at_ref, own_ref, rising_ref, falling_ref, keep_ref, give_ref, held):
    total = own_ref[...] + rising_ref[...] + falling_ref[...]
    held[0], held[1] = total[: ROWS // 2], total[ROWS // 2 :]
    keep_ref[...] = held[at_ref[0]]
    give_ref[...] = held[1 - at_ref[0]]


def left_quarter_kernel(at_ref, own_ref, moved_ref, keep_ref, give_ref, held):
    total = own_ref[...] + moved_ref[...]
    held[0], held[1] = total[:LEFT], total[LEFT:]
    keep_ref[...] = held[at_ref[0]]
    give_ref[...] = held[1 - at_ref[0]]


def add_kernel(own_ref, moved_ref, out_ref):
    out_ref[...] = own_ref[...] + moved_ref[...]


def right_chunks_kernel(own_ref, rising_ref, falling_ref, *refs):
    for step in ALL:
        total = own_ref[step] + rising_ref[step] + falling_ref[step]
        if step == FAR[0]:
            refs[-2][...] = total[: ROWS // 2]
            refs[-1][...] = total[ROWS // 2 :]
        else:
            refs[REST.index(step)][...] = total


def right_half_kernel(at_ref, *refs):
    *terms, keep_ref, give_ref, held = refs
    total = terms[0][...]
    for term in terms[1:]:
        total += term[...]
    held[0], held[1] = total[:RIGHT], total[RIGHT:]
    keep_ref[...] = held[at_ref[0]]
    give_ref[...] = held[1 - at_ref[0]]


def feature_kernel(at_ref, left_ref, moved_ref, ids_ref, *refs):
    *pieces, out_ref, held = refs
    left = left_ref[...] + moved_ref[...]
    for sub in range(Y):
        held[sub] = left[:, sub * SUB : (sub + 1) * SUB]
    labels = lax.broadcasted_iota(jnp.int32, (EX_GRP, SUB), 0)
    over = (((1,), (1,)), ((), ()))
    total = jnp.zeros((EX_GRP, LEFT * RIGHT), jnp.float32)
    for bits, piece in enumerate(pieces):
        right = piece[...]
        sub = at_ref[0] ^ bits
        member = (ids_ref[sub] == labels).astype(jnp.float32).astype(jnp.bfloat16)
        part = held[sub]
        product = jnp.concatenate([part[a : a + 1] * right for a in range(LEFT)], axis=0)
        high = product.astype(jnp.bfloat16)
        low = (product - high.astype(jnp.float32)).astype(jnp.bfloat16)
        total += lax.dot_general(member, high, over, preferred_element_type=jnp.float32)
        total += lax.dot_general(member, low, over, preferred_element_type=jnp.float32)
    out_ref[...] = total


def on_device(activations, out_grads, example_ids, train_flags, in_proj, out_proj):
    at = parts_of(lax.axis_index("par"))
    group = lax.axis_index("grp")
    place = (at["z"], at["y"])

    whole, half = (ROWS, WIDE), (ROWS // 2, WIDE)
    quarter = (Z, ROWS, SUB)
    far = projected(left_far_kernel, place, in_proj, activations, 1, [half] * 2)
    left_moved = both_ways(*far, "z")
    *right, rising, falling = projected(
        right_kernel, place, out_proj, out_grads, Z, [quarter] * 3 + [(Z // 2, ROWS, SUB)] * 2,
        [pltpu.VMEM((Y, ROWS, SUB), jnp.float32)], far[:1],
    )
    right_moved = both_ways(rising, falling, "y")
    left = projected(
        left_kernel, place, in_proj, activations, len(REST), [whole] * 7, after=[rising]
    )

    sent = step_add(left[0], left[1], left_moved, [], half=True)
    left_moved = both_ways(*sent, "z")
    sent = step_add(right[1], right[2], right_moved, sent[:1], half=True)
    right_moved = both_ways(*sent, "y")
    sent = step_add(left[2], left[3], left_moved, sent[:1])
    left_moved = both_ways(*sent, "z")
    sent = step_add(left[4], left[5], left_moved, sent[:1])
    left_moved = both_ways(*sent, "z")
    *right, rising, falling = local(
        right_chunks_kernel, (), [right[0], *right_moved],
        [(ROWS, SUB)] * 7 + [(ROWS // 2, SUB)] * 2, after=sent[:1],
    )
    right_moved = both_ways(rising, falling, "z")
    sent = step_add(right[0], right[1], right_moved, [], half=True)
    right_moved = both_ways(*sent, "z")
    first, second = (at["y"] ^ (at["y"] >> 1)) & 1, at["y"] >> 1
    keep, give = local(
        left_half_kernel, (first,), [left[6], *left_moved], [half] * 2, [(2, *half)], after=sent[:1]
    )
    left_moved = mixed(give, "y", 1)
    sent = step_add(right[2], right[3], right_moved, [give])
    right_moved = both_ways(*sent, "z")
    keep, give = local(
        left_quarter_kernel, (second,), [keep, left_moved], [(LEFT, WIDE)] * 2, [(2, LEFT, WIDE)],
        after=sent[:1],
    )
    left_moved = mixed(give, "y", 3)
    sent = step_add(right[4], right[5], right_moved, [give])
    right_moved = both_ways(*sent, "z")
    (left,) = local(add_kernel, (), [keep, left_moved], [(LEFT, WIDE)], after=sent[:1])
    left_moved = mixed(left, "x", 1)
    keep, give = local(
        right_half_kernel, (at["x"],), [right[6], *right_moved], [(RIGHT, SUB)] * 2, [(2, RIGHT, SUB)],
        after=[left],
    )
    (right,) = local(add_kernel, (), [keep, mixed(give, "x", 1)], [(RIGHT, SUB)])
    pieces = [right] + [mixed(right, "y", bits) for bits in range(1, Y)]

    ids = lax.dynamic_slice(example_ids, (0, at["z"] * WIDE), (1, WIDE)).reshape(Y, 1, SUB)
    features = pl.pallas_call(
        feature_kernel,
        in_specs=[SMEM] + [VMEM] * 7,
        out_specs=VMEM,
        out_shape=jax.ShapeDtypeStruct((EX_GRP, LEFT * RIGHT), jnp.float32),
        scratch_shapes=[pltpu.VMEM((Y, LEFT, SUB), jnp.float32)],
        compiler_params=pltpu.CompilerParams(vmem_limit_bytes=8 * MIB),
    )(jnp.stack([at["y"]]), left, left_moved, ids, *pieces)
    for bits in (1, 2, 7):
        features = features + mixed(features, "z", bits)

    flags = train_flags.astype(jnp.float32)
    row_side = features * (flags * (1.0 / TOK_GRP))[:, None]
    cols = (features * (1.0 - flags)[:, None])[None]
    for bit in (1, 2):
        other = lax.ppermute(cols, "grp", [(i, i ^ bit) for i in range(4)])
        late = (group & bit) > 0
        cols = jnp.concatenate([jnp.where(late, other, cols), jnp.where(late, cols, other)])
    cols = cols.reshape(4 * EX_GRP, LEFT * RIGHT)
    kernel = lax.dot_general(
        row_side, cols, (((1,), (1,)), ((), ())), precision=lax.Precision.HIGHEST
    )
    near, opposite, last = (mixed(kernel, "y", bits) for bits in range(1, Y))
    kernel = (kernel + near) + (opposite + last)
    return kernel + mixed(kernel, "x", 1)


def solution(mesh):
    return jax.shard_map(
        on_device,
        mesh=mesh,
        in_specs=(
            P("par", "grp"),
            P("par", "grp"),
            P("grp", None),
            P("grp"),
            P("par", None),
            P("par", None),
        ),
        out_specs=P("grp", None),
        check_vma=False,
    )
```

time: 129 us -> 120 us (0.930)
  waiting for transfers between devices: 67.1 us -> 57.3 us
  starting transfers between devices: 44.5 us -> 50.1 us
  Pallas kernels: 13.5 us -> 10.9 us
  local copies, waits for them, and re-layouts: 1.99 us -> 0.01 us
    ppermute x32 -> x34, waiting for transfers between devices: 63.6 us -> 53.7 us  [send(): return lax.ppermute(value, 'par', pairs)]
    ppermute x32 -> x34, starting transfers between devices: 41.4 us -> 47 us  [send(): return lax.ppermute(value, 'par', pairs)]
    pallas_call x16 -> x17, Pallas kernels: 13.5 us -> 10.9 us  [the longest x3 9.42 us: projected(): pl.pallas_call(ordered(kernel, 3, after), in_specs=[SMEM, *[pl.BlockSpec(...]
    unnamed x12 -> x4, local copies, waits for them, and re-layouts: 1.99 us -> 0.01 us
  transfers between devices with their start and end apart: 34 -> 36, of which waited for: 26 -> 24; matrix products, arithmetic and copies ran while one was open for 0% -> 0% of each run, Pallas kernels for 6% -> 7%
where the time goes in v3:
time: 120 us
  waiting for transfers between devices  57.3 us (48%)
  starting transfers between devices  50.1 us (42%)
  Pallas kernels  10.9 us (9%)
    ppermute x34, waiting for transfers between devices, send(): return lax.ppermute(value, 'par', pairs)  53.7 us
    ppermute x34, starting transfers between devices, send(): return lax.ppermute(value, 'par', pairs)  47 us
    pallas_call x3, Pallas kernels, projected(): pl.pallas_call(ordered(kernel, 3, after), in_specs=[SMEM, *[pl.BlockSpec(...  9.42 us
    ppermute x2, waiting for transfers between devices, on_device(): other = lax.ppermute(cols, 'grp', [(i, i ^ bit) for i in range(4)])  3.53 us
    ppermute x2, starting transfers between devices, on_device(): other = lax.ppermute(cols, 'grp', [(i, i ^ bit) for i in range(4)])  3.16 us
  transfers between devices with their start and end apart: 36, of which 24 were waited for; matrix products, arithmetic and copies ran while one was open for 0% of the time, Pallas kernels for 7%

profile of v3, /device:TPU:32, one launch (start us, length us, event | category | flops | bytes accessed | tf_op | source)
XLA Modules:
  0.0 119.5 jit_solution(376639386707746916)
XLA Ops:
  0.1 1.8 %shard_map.64 = (f32[16,3072]{1,0:T(8,128)S(1)}, f32[16,3072]{1,0:T(8,128)S(1)}) custom-call(s32[2]{0:T(128)S(1)} %pad_add_fusion.refs_0_, bf16[32,64]{1,0:T(8,128)(2,1)} %bitcast.14, bf16[64,24576]{1,0:T(8,128)(2,1)} %refs_2_.5), custom_call_target="tpu_custom_call" | custom-call | tf_op jit(solution)/shard_map/pallas_call | solution.py:115
  1.8 2.0 %collective-permute-start = (f32[16,3072]{1,0:T(8,128)S(1)}, f32[16,3072]{1,0:T(8,128)S(1)}, u32[]{:S(2)}, u32[]{:S(2)}) collective-permute-start(f32[16,3072]{1,0:T(8,128)S(1)} %get-tuple-element.48.refs_3_), channel_id=1, source_target_pairs={{0,8},{1,9},{2,10},{3,11},{4,12},{5,13},{6,14},{7,15},{8,16},{9,17... | collective-permute-start | bytes 589832 | tf_op jit(solution)/shard_map/ppermute | solution.py:38
  4.0 4.7 %shard_map.65 = (f32[8,32,768]{2,1,0:T(8,128)S(1)}, f32[8,32,768]{2,1,0:T(8,128)S(1)}, f32[8,32,768]{2,1,0:T(8,128)S(1)}, f32[4,32,768]{2,1,0:T(8,128)S(1)}, f32[4,32,768]{2,1,0:T(8,128)S(1)}) custom-call(s32[2]{0:T(128)S(1)} %pad_add_fusion.refs_0_, bf16[32,172]{1,0:T(8,128)(2,1)} %bitcast.16, bf16[172,24576]{1,0:T(8,128)(2,1)} %refs_2_.4, ...), custom_call_target="tpu_custom_call" | custom-call | tf_op jit(solution)/shard_map/pallas_call | solution.py:115
  8.6 1.7 %collective-permute-start.4 = (f32[4,32,768]{2,1,0:T(8,128)S(1)}, f32[4,32,768]{2,1,0:T(8,128)S(1)}, u32[]{:S(2)}, u32[]{:S(2)}) collective-permute-start(f32[4,32,768]{2,1,0:T(8,128)S(1)} %get-tuple-element.49.refs_3_), channel_id=1, source_target_pairs={{0,1},{1,2},{2,3},{3,0},{4,5},{5,6},{6,7},{7,4},{8,9},{9,10},{10,1... | collective-permute-start | bytes 1179656 | tf_op jit(solution)/shard_map/ppermute | solution.py:38
  10.3 1.7 %collective-permute-start.5 = (f32[4,32,768]{2,1,0:T(8,128)S(1)}, f32[4,32,768]{2,1,0:T(8,128)S(1)}, u32[]{:S(2)}, u32[]{:S(2)}) collective-permute-start(f32[4,32,768]{2,1,0:T(8,128)S(1)} %get-tuple-element.62), channel_id=1, source_target_pairs={{0,3},{1,0},{2,1},{3,2},{4,7},{5,4},{6,5},{7,6},{8,11},{9,8},{10,9... | collective-permute-start | bytes 1179656 | tf_op jit(solution)/shard_map/ppermute | solution.py:38
  12.0 3.0 %shard_map.66 = (f32[32,3072]{1,0:T(8,128)S(1)}, f32[32,3072]{1,0:T(8,128)S(1)}, f32[32,3072]{1,0:T(8,128)S(1)}, f32[32,3072]{1,0:T(8,128)S(1)}, f32[32,3072]{1,...) custom-call(s32[2]{0:T(128)S(1)} %pad_add_fusion.refs_0_, bf16[32,64]{1,0:T(8,128)(2,1)} %bitcast.15, ...), custom_call_target="tpu_custom_call" | custom-call | tf_op jit(solution)/shard_map/pallas_call | solution.py:115
  15.0 2.0 %collective-permute-start.2 = (f32[32,3072]{1,0:T(8,128)S(1)}, f32[32,3072]{1,0:T(8,128)S(1)}, u32[]{:S(2)}, u32[]{:S(2)}) collective-permute-start(f32[32,3072]{1,0:T(8,128)S(1)} %get-tuple-element.58.refs_4_), channel_id=1, source_target_pairs={{0,8},{1,9},{2,10},{3,11},{4,12},{5,13},{6,14},{7,15},{8,16},{9,17... | collective-permute-start | bytes 1179656 | tf_op jit(solution)/shard_map/ppermute | solution.py:38
  17.0 2.2 %collective-permute-start.3 = (f32[32,3072]{1,0:T(8,128)S(1)}, f32[32,3072]{1,0:T(8,128)S(1)}, u32[]{:S(2)}, u32[]{:S(2)}) collective-permute-start(f32[32,3072]{1,0:T(8,128)S(1)} %get-tuple-element.59), channel_id=1, source_target_pairs={{0,56},{1,57},{2,58},{3,59},{4,60},{5,61},{6,62},{7,63},{8,0},{9,1... | collective-permute-start | bytes 1179656 | tf_op jit(solution)/shard_map/ppermute | solution.py:38
  19.2 1.2 %collective-permute-done.4.refs_2_ = f32[4,32,768]{2,1,0:T(8,128)S(1)} collective-permute-done((f32[4,32,768]{2,1,0:T(8,128)S(1)}, f32[4,32,768]{2,1,0:T(8,128)S(1)}, u32[]{:S(2)}, u32[]{:S(2)}) %collective-permute-start.4) | collective-permute-done | bytes 393248 | tf_op jit(solution)/shard_map/ppermute | solution.py:38
  20.5 0.1 shard_map.68
  20.6 1.7 %collective-permute-start.10 = (f32[8,32,768]{2,1,0:T(8,128)S(1)}, f32[8,32,768]{2,1,0:T(8,128)S(1)}, u32[]{:S(2)}, u32[]{:S(2)}) collective-permute-start(f32[8,32,768]{2,1,0:T(8,128)S(1)} %get-tuple-element.63.refs_4_), channel_id=1, source_target_pairs={{0,1},{1,2},{2,3},{3,0},{4,5},{5,6},{6,7},{7,4},{8,9},{9,10},{10,1... | collective-permute-start | bytes 2359304 | tf_op jit(solution)/shard_map/ppermute | solution.py:38
  22.3 1.7 %collective-permute-start.11 = (f32[8,32,768]{2,1,0:T(8,128)S(1)}, f32[8,32,768]{2,1,0:T(8,128)S(1)}, u32[]{:S(2)}, u32[]{:S(2)}) collective-permute-start(f32[8,32,768]{2,1,0:T(8,128)S(1)} %get-tuple-element.69), channel_id=1, source_target_pairs={{0,3},{1,0},{2,1},{3,2},{4,7},{5,4},{6,5},{7,6},{8,11},{9,8},{10,9... | collective-permute-start | bytes 2359304 | tf_op jit(solution)/shard_map/ppermute | solution.py:38
  23.9 3.6 %collective-permute-done.2.refs_2_ = f32[32,3072]{1,0:T(8,128)S(1)} collective-permute-done((f32[32,3072]{1,0:T(8,128)S(1)}, f32[32,3072]{1,0:T(8,128)S(1)}, u32[]{:S(2)}, u32[]{:S(2)}) %collective-permute-start.2) | collective-permute-done | bytes 393248 | tf_op jit(solution)/shard_map/ppermute | solution.py:38
  27.6 0.6 collective-permute-done.3.refs_3_
  28.2 0.1 shard_map.69
  28.3 3.0 %collective-permute-start.6 = (f32[32,3072]{1,0:T(8,128)S(1)}, f32[32,3072]{1,0:T(8,128)S(1)}, u32[]{:S(2)}, u32[]{:S(2)}) collective-permute-start(f32[32,3072]{1,0:T(8,128)S(1)} %get-tuple-element.64.refs_4_), channel_id=1, source_target_pairs={{0,8},{1,9},{2,10},{3,11},{4,12},{5,13},{6,14},{7,15},{8,16},{9,17... | collective-permute-start | bytes 1179656 | tf_op jit(solution)/shard_map/ppermute | solution.py:38
  31.4 6.8 %collective-permute-done.6.refs_2_ = f32[32,3072]{1,0:T(8,128)S(1)} collective-permute-done((f32[32,3072]{1,0:T(8,128)S(1)}, f32[32,3072]{1,0:T(8,128)S(1)}, u32[]{:S(2)}, u32[]{:S(2)}) %collective-permute-start.6) | collective-permute-done | bytes 393248 | tf_op jit(solution)/shard_map/ppermute | solution.py:38
  38.2 2.7 %collective-permute-done.7.refs_3_ = f32[32,3072]{1,0:T(8,128)S(1)} collective-permute-done((f32[32,3072]{1,0:T(8,128)S(1)}, f32[32,3072]{1,0:T(8,128)S(1)}, u32[]{:S(2)}, u32[]{:S(2)}) %collective-permute-start.7) | collective-permute-done | bytes 393248 | tf_op jit(solution)/shard_map/ppermute | solution.py:38
  41.1 1.8 %collective-permute-start.8 = (f32[32,3072]{1,0:T(8,128)S(1)}, f32[32,3072]{1,0:T(8,128)S(1)}, u32[]{:S(2)}, u32[]{:S(2)}) collective-permute-start(f32[32,3072]{1,0:T(8,128)S(1)} %get-tuple-element.66.refs_3_), channel_id=1, source_target_pairs={{0,8},{1,9},{2,10},{3,11},{4,12},{5,13},{6,14},{7,15},{8,16},{9,17... | collective-permute-start | bytes 1179656 | tf_op jit(solution)/shard_map/ppermute | solution.py:38
  42.9 0.3 collective-permute-start.9
  43.2 0.1 shard_map.71
  43.3 1.8 %collective-permute-start.12 = (f32[16,768]{1,0:T(8,128)S(1)}, f32[16,768]{1,0:T(8,128)S(1)}, u32[]{:S(2)}, u32[]{:S(2)}) collective-permute-start(f32[16,768]{1,0:T(8,128)S(1)} %get-tuple-element.72), channel_id=1, source_target_pairs={{0,8},{1,9},{2,10},{3,11},{4,12},{5,13},{6,14},{7,15},{8,16},{9,17... | collective-permute-start | bytes 147464 | tf_op jit(solution)/shard_map/ppermute | solution.py:38
  45.2 0.3 collective-permute-start.13
  45.4 4.7 %collective-permute-done.12.refs_2_ = f32[16,768]{1,0:T(8,128)S(1)} collective-permute-done((f32[16,768]{1,0:T(8,128)S(1)}, f32[16,768]{1,0:T(8,128)S(1)}, u32[]{:S(2)}, u32[]{:S(2)}) %collective-permute-start.12) | collective-permute-done | bytes 49184 | tf_op jit(solution)/shard_map/ppermute | solution.py:38
  50.1 1.3 %collective-permute-done.13.refs_3_ = f32[16,768]{1,0:T(8,128)S(1)} collective-permute-done((f32[16,768]{1,0:T(8,128)S(1)}, f32[16,768]{1,0:T(8,128)S(1)}, u32[]{:S(2)}, u32[]{:S(2)}) %collective-permute-start.13) | collective-permute-done | bytes 49184 | tf_op jit(solution)/shard_map/ppermute | solution.py:38
  51.5 1.8 %collective-permute-start.15 = (f32[32,768]{1,0:T(8,128)S(1)}, f32[32,768]{1,0:T(8,128)S(1)}, u32[]{:S(2)}, u32[]{:S(2)}) collective-permute-start(f32[32,768]{1,0:T(8,128)S(1)} %get-tuple-element.74.refs_4_), channel_id=1, source_target_pairs={{0,8},{1,9},{2,10},{3,11},{4,12},{5,13},{6,14},{7,15},{8,16},{9,17... | collective-permute-start | bytes 294920 | tf_op jit(solution)/shard_map/ppermute | solution.py:38
  53.3 0.3 collective-permute-start.16
  53.7 0.2 collective-permute-start.14
  53.8 3.3 %collective-permute-done.15.refs_2_ = f32[32,768]{1,0:T(8,128)S(1)} collective-permute-done((f32[32,768]{1,0:T(8,128)S(1)}, f32[32,768]{1,0:T(8,128)S(1)}, u32[]{:S(2)}, u32[]{:S(2)}) %collective-permute-start.15) | collective-permute-done | bytes 98336 | tf_op jit(solution)/shard_map/ppermute | solution.py:38
  57.1 1.5 %collective-permute-done.16.refs_3_ = f32[32,768]{1,0:T(8,128)S(1)} collective-permute-done((f32[32,768]{1,0:T(8,128)S(1)}, f32[32,768]{1,0:T(8,128)S(1)}, u32[]{:S(2)}, u32[]{:S(2)}) %collective-permute-start.16) | collective-permute-done | bytes 98336 | tf_op jit(solution)/shard_map/ppermute | solution.py:38
  58.7 1.8 %collective-permute-start.18 = (f32[32,768]{1,0:T(8,128)S(1)}, f32[32,768]{1,0:T(8,128)S(1)}, u32[]{:S(2)}, u32[]{:S(2)}) collective-permute-start(f32[32,768]{1,0:T(8,128)S(1)} %get-tuple-element.80.refs_3_), channel_id=1, source_target_pairs={{0,8},{1,9},{2,10},{3,11},{4,12},{5,13},{6,14},{7,15},{8,16},{9,17... | collective-permute-start | bytes 294920 | tf_op jit(solution)/shard_map/ppermute | solution.py:38
  60.5 0.3 collective-permute-start.19
  60.8 1.6 %collective-permute-start.17 = (f32[8,3072]{1,0:T(8,128)S(1)}, f32[8,3072]{1,0:T(8,128)S(1)}, u32[]{:S(2)}, u32[]{:S(2)}) collective-permute-start(f32[8,3072]{1,0:T(8,128)S(1)} %get-tuple-element.82.refs_4_), channel_id=1, source_target_pairs={{0,3},{1,2},{2,1},{3,0},{4,7},{5,6},{6,5},{7,4},{8,11},{9,10},{10,... | collective-permute-start | bytes 294920 | tf_op jit(solution)/shard_map/ppermute | solution.py:38
  62.4 0.9 collective-permute-done.18.refs_2_
  63.4 1.7 %collective-permute-done.19.refs_3_ = f32[32,768]{1,0:T(8,128)S(1)} collective-permute-done((f32[32,768]{1,0:T(8,128)S(1)}, f32[32,768]{1,0:T(8,128)S(1)}, u32[]{:S(2)}, u32[]{:S(2)}) %collective-permute-start.19) | collective-permute-done | bytes 98336 | tf_op jit(solution)/shard_map/ppermute | solution.py:38
  65.1 1.7 %collective-permute-start.21 = (f32[32,768]{1,0:T(8,128)S(1)}, f32[32,768]{1,0:T(8,128)S(1)}, u32[]{:S(2)}, u32[]{:S(2)}) collective-permute-start(f32[32,768]{1,0:T(8,128)S(1)} %get-tuple-element.86.refs_2_), channel_id=1, source_target_pairs={{0,8},{1,9},{2,10},{3,11},{4,12},{5,13},{6,14},{7,15},{8,16},{9,17... | collective-permute-start | bytes 294920 | tf_op jit(solution)/shard_map/ppermute | solution.py:38
  66.8 0.4 collective-permute-start.22
  67.3 2.6 %collective-permute-done.21.refs_2_ = f32[32,768]{1,0:T(8,128)S(1)} collective-permute-done((f32[32,768]{1,0:T(8,128)S(1)}, f32[32,768]{1,0:T(8,128)S(1)}, u32[]{:S(2)}, u32[]{:S(2)}) %collective-permute-start.21) | collective-permute-done | bytes 98336 | tf_op jit(solution)/shard_map/ppermute | solution.py:38
  69.8 1.6 %collective-permute-done.22.refs_3_ = f32[32,768]{1,0:T(8,128)S(1)} collective-permute-done((f32[32,768]{1,0:T(8,128)S(1)}, f32[32,768]{1,0:T(8,128)S(1)}, u32[]{:S(2)}, u32[]{:S(2)}) %collective-permute-start.22) | collective-permute-done | bytes 98336 | tf_op jit(solution)/shard_map/ppermute | solution.py:38
  71.4 1.6 %collective-permute-start.23 = (f32[16,768]{1,0:T(8,128)S(1)}, f32[16,768]{1,0:T(8,128)S(1)}, u32[]{:S(2)}, u32[]{:S(2)}) collective-permute-start(f32[16,768]{1,0:T(8,128)S(1)} %get-tuple-element.90), channel_id=1, source_target_pairs={{0,4},{1,5},{2,6},{3,7},{4,0},{5,1},{6,2},{7,3},{8,12},{9,13},{10,... | collective-permute-start | bytes 147464 | tf_op jit(solution)/shard_map/ppermute | solution.py:38
  73.0 0.5 collective-permute-start.20
  73.5 2.1 %collective-permute-done.23.refs_1_ = f32[16,768]{1,0:T(8,128)S(1)} collective-permute-done((f32[16,768]{1,0:T(8,128)S(1)}, f32[16,768]{1,0:T(8,128)S(1)}, u32[]{:S(2)}, u32[]{:S(2)}) %collective-permute-start.23) | collective-permute-done | bytes 49184 | tf_op jit(solution)/shard_map/ppermute | solution.py:38
  75.7 3.0 %collective-permute-start.25 = (f32[16,768]{1,0:T(8,128)S(1)}, f32[16,768]{1,0:T(8,128)S(1)}, u32[]{:S(2)}, u32[]{:S(2)}) collective-permute-start(f32[16,768]{1,0:T(8,128)S(1)} %shard_map.79.refs_0_), channel_id=1, source_target_pairs={{0,2},{1,3},{2,0},{3,1},{4,6},{5,7},{6,4},{7,5},{8,10},{9,11},{10,... | collective-permute-start | bytes 147464 | tf_op jit(solution)/shard_map/ppermute | solution.py:38
  78.8 1.6 %collective-permute-start.26 = (f32[16,768]{1,0:T(8,128)S(1)}, f32[16,768]{1,0:T(8,128)S(1)}, u32[]{:S(2)}, u32[]{:S(2)}) collective-permute-start(f32[16,768]{1,0:T(8,128)S(1)} %shard_map.79.refs_0_), channel_id=1, source_target_pairs={{0,3},{1,2},{2,1},{3,0},{4,7},{5,6},{6,5},{7,4},{8,11},{9,10},{10,... | collective-permute-start | bytes 147464 | tf_op jit(solution)/shard_map/ppermute | solution.py:38
  80.4 1.0 collective-permute-done.25.refs_2_
  81.4 2.7 %collective-permute-done.26.refs_3_ = f32[16,768]{1,0:T(8,128)S(1)} collective-permute-done((f32[16,768]{1,0:T(8,128)S(1)}, f32[16,768]{1,0:T(8,128)S(1)}, u32[]{:S(2)}, u32[]{:S(2)}) %collective-permute-start.26) | collective-permute-done | bytes 49184 | tf_op jit(solution)/shard_map/ppermute | solution.py:38
  84.1 0.6 shard_map.80
  84.7 0.7 collective-permute-start.27
  85.3 3.1 %collective-permute-done.27 = f32[32,128]{1,0:T(8,128)S(1)} collective-permute-done((f32[32,128]{1,0:T(8,128)S(1)}, f32[32,128]{1,0:T(8,128)S(1)}, u32[]{:S(2)}, u32[]{:S(2)}) %collective-permute-start.27) | collective-permute-done | bytes 16416 | tf_op jit(solution)/shard_map/ppermute | solution.py:38
  88.5 2.3 %collective-permute-start.28 = (f32[32,128]{1,0:T(8,128)S(1)}, f32[32,128]{1,0:T(8,128)S(1)}, u32[]{:S(2)}, u32[]{:S(2)}) collective-permute-start(f32[32,128]{1,0:T(8,128)S(1)} %add.36), channel_id=1, source_target_pairs={{0,16},{1,17},{2,18},{3,19},{4,20},{5,21},{6,22},{7,23},{8,24},{9,... | collective-permute-start | bytes 49160 | tf_op jit(solution)/shard_map/ppermute | solution.py:38
  90.8 2.3 %collective-permute-done.28 = f32[32,128]{1,0:T(8,128)S(1)} collective-permute-done((f32[32,128]{1,0:T(8,128)S(1)}, f32[32,128]{1,0:T(8,128)S(1)}, u32[]{:S(2)}, u32[]{:S(2)}) %collective-permute-start.28) | collective-permute-done | bytes 16416 | tf_op jit(solution)/shard_map/ppermute | solution.py:38
  93.1 2.4 %collective-permute-start.29 = (f32[32,128]{1,0:T(8,128)S(1)}, f32[32,128]{1,0:T(8,128)S(1)}, u32[]{:S(2)}, u32[]{:S(2)}) collective-permute-start(f32[32,128]{1,0:T(8,128)S(1)} %add.37), channel_id=1, source_target_pairs={{0,56},{1,57},{2,58},{3,59},{4,60},{5,61},{6,62},{7,63},{8,48},{9,... | collective-permute-start | bytes 49160 | tf_op jit(solution)/shard_map/ppermute | solution.py:38
  95.5 4.3 %collective-permute-done.29 = f32[32,128]{1,0:T(8,128)S(1)} collective-permute-done((f32[32,128]{1,0:T(8,128)S(1)}, f32[32,128]{1,0:T(8,128)S(1)}, u32[]{:S(2)}, u32[]{:S(2)}) %collective-permute-start.29) | collective-permute-done | bytes 16416 | tf_op jit(solution)/shard_map/ppermute | solution.py:38
  100.0 1.2 collective-permute-done.30
  101.1 3.1 %collective-permute-start.31 = (f32[2,32,128]{2,1,0:T(8,128)S(1)}, f32[2,32,128]{2,1,0:T(8,128)S(1)}, u32[]{:S(2)}, u32[]{:S(2)}) collective-permute-start(f32[2,32,128]{2,1,0:T(8,128)S(1)} %pad_maximum_fusion.1), channel_id=1, source_target_pairs={{0,128},{64,192},{128,0},{192,64},{1,129},{65,193},{129,1},{193,65... | collective-permute-start | bytes 98312 | tf_op jit(solution)/shard_map/ppermute | solution.py:279
  104.3 2.4 %collective-permute-done.31 = f32[2,32,128]{2,1,0:T(8,128)S(1)} collective-permute-done((f32[2,32,128]{2,1,0:T(8,128)S(1)}, f32[2,32,128]{2,1,0:T(8,128)S(1)}, u32[]{:S(2)}, u32[]{:S(2)}) %collective-permute-start.31) | collective-permute-done | bytes 32800 | tf_op jit(solution)/shard_map/ppermute | solution.py:279
  106.7 0.2 fusion
  107.0 3.1 %collective-permute-start.33 = (f32[32,128]{1,0:T(8,128)S(1)}, f32[32,128]{1,0:T(8,128)S(1)}, u32[]{:S(2)}, u32[]{:S(2)}) collective-permute-start(f32[32,128]{1,0:T(8,128)S(1)} %fusion), channel_id=1, source_target_pairs={{0,2},{1,3},{2,0},{3,1},{4,6},{5,7},{6,4},{7,5},{8,10},{9,11},{10,... | collective-permute-start | bytes 49160 | tf_op jit(solution)/shard_map/ppermute | solution.py:38
  110.1 1.6 %collective-permute-start.34 = (f32[32,128]{1,0:T(8,128)S(1)}, f32[32,128]{1,0:T(8,128)S(1)}, u32[]{:S(2)}, u32[]{:S(2)}) collective-permute-start(f32[32,128]{1,0:T(8,128)S(1)} %fusion), channel_id=1, source_target_pairs={{0,3},{1,2},{2,1},{3,0},{4,7},{5,6},{6,5},{7,4},{8,11},{9,10},{10,... | collective-permute-start | bytes 49160 | tf_op jit(solution)/shard_map/ppermute | solution.py:38
  111.7 0.6 collective-permute-done.33
  112.3 2.7 %collective-permute-done.34 = f32[32,128]{1,0:T(8,128)S(1)} collective-permute-done((f32[32,128]{1,0:T(8,128)S(1)}, f32[32,128]{1,0:T(8,128)S(1)}, u32[]{:S(2)}, u32[]{:S(2)}) %collective-permute-start.34) | collective-permute-done | bytes 16416 | tf_op jit(solution)/shard_map/ppermute | solution.py:38
  115.1 1.6 %collective-permute-start.35 = (f32[32,128]{1,0:T(8,128)S(1)}, f32[32,128]{1,0:T(8,128)S(1)}, u32[]{:S(2)}, u32[]{:S(2)}) collective-permute-start(f32[32,128]{1,0:T(8,128)S(1)} %add_add_fusion), channel_id=1, source_target_pairs={{0,4},{1,5},{2,6},{3,7},{4,0},{5,1},{6,2},{7,3},{8,12},{9,13},{10,... | collective-permute-start | bytes 49160 | tf_op jit(solution)/shard_map/ppermute | solution.py:38
  116.7 2.2 %collective-permute-done.35 = f32[32,128]{1,0:T(8,128)S(1)} collective-permute-done((f32[32,128]{1,0:T(8,128)S(1)}, f32[32,128]{1,0:T(8,128)S(1)}, u32[]{:S(2)}, u32[]{:S(2)}) %collective-permute-start.35) | collective-permute-done | bytes 16416 | tf_op jit(solution)/shard_map/ppermute | solution.py:38
  118.9 0.6 add.42
  (42 shorter events, 1.1 us)
Async XLA Ops:
  0.0 80.4 %copy-start = (s32[1,24576]{1,0:T(1,128)S(1)}, s32[1,24576]{1,0:T(1,128)}, u32[]{:S(2)}) copy-start(s32[1,24576]{1,0:T(1,128)} %param.8) | copy-start | bytes 294916
  1.8 13.1 %collective-permute-start = (f32[16,3072]{1,0:T(8,128)S(1)}, f32[16,3072]{1,0:T(8,128)S(1)}, u32[]{:S(2)}, u32[]{:S(2)}) collective-permute-start(f32[16,3072]{1,0:T(8,128)S(1)} %get-tuple-element.48.refs_3_), channel_id=1, source_target_pairs={{0,8},{1,9},{2,10},{3,11},{4,12},{5,13},{6,14},{7,15},{8,16},{9,17... | collective-permute-start | bytes 589832 | tf_op jit(solution)/shard_map/ppermute | solution.py:38
  3.8 11.1 %collective-permute-start.1 = (f32[16,3072]{1,0:T(8,128)S(1)}, f32[16,3072]{1,0:T(8,128)S(1)}, u32[]{:S(2)}, u32[]{:S(2)}) collective-permute-start(f32[16,3072]{1,0:T(8,128)S(1)} %get-tuple-element.57), channel_id=1, source_target_pairs={{0,56},{1,57},{2,58},{3,59},{4,60},{5,61},{6,62},{7,63},{8,0},{9,1... | collective-permute-start | bytes 589832 | tf_op jit(solution)/shard_map/ppermute | solution.py:38
  8.6 11.8 %collective-permute-start.4 = (f32[4,32,768]{2,1,0:T(8,128)S(1)}, f32[4,32,768]{2,1,0:T(8,128)S(1)}, u32[]{:S(2)}, u32[]{:S(2)}) collective-permute-start(f32[4,32,768]{2,1,0:T(8,128)S(1)} %get-tuple-element.49.refs_3_), channel_id=1, source_target_pairs={{0,1},{1,2},{2,3},{3,0},{4,5},{5,6},{6,7},{7,4},{8,9},{9,10},{10,1... | collective-permute-start | bytes 1179656 | tf_op jit(solution)/shard_map/ppermute | solution.py:38
  10.3 10.2 %collective-permute-start.5 = (f32[4,32,768]{2,1,0:T(8,128)S(1)}, f32[4,32,768]{2,1,0:T(8,128)S(1)}, u32[]{:S(2)}, u32[]{:S(2)}) collective-permute-start(f32[4,32,768]{2,1,0:T(8,128)S(1)} %get-tuple-element.62), channel_id=1, source_target_pairs={{0,3},{1,0},{2,1},{3,2},{4,7},{5,4},{6,5},{7,6},{8,11},{9,8},{10,9... | collective-permute-start | bytes 1179656 | tf_op jit(solution)/shard_map/ppermute | solution.py:38
  14.9 80.6 %copy-start.1 = (s32[32]{0:T(128)S(1)}, s32[32]{0:T(128)}, u32[]{:S(2)}) copy-start(s32[32]{0:T(128)} %param.9) | copy-start | bytes 388
  15.0 12.5 %collective-permute-start.2 = (f32[32,3072]{1,0:T(8,128)S(1)}, f32[32,3072]{1,0:T(8,128)S(1)}, u32[]{:S(2)}, u32[]{:S(2)}) collective-permute-start(f32[32,3072]{1,0:T(8,128)S(1)} %get-tuple-element.58.refs_4_), channel_id=1, source_target_pairs={{0,8},{1,9},{2,10},{3,11},{4,12},{5,13},{6,14},{7,15},{8,16},{9,17... | collective-permute-start | bytes 1179656 | tf_op jit(solution)/shard_map/ppermute | solution.py:38
  17.0 11.1 %collective-permute-start.3 = (f32[32,3072]{1,0:T(8,128)S(1)}, f32[32,3072]{1,0:T(8,128)S(1)}, u32[]{:S(2)}, u32[]{:S(2)}) collective-permute-start(f32[32,3072]{1,0:T(8,128)S(1)} %get-tuple-element.59), channel_id=1, source_target_pairs={{0,56},{1,57},{2,58},{3,59},{4,60},{5,61},{6,62},{7,63},{8,0},{9,1... | collective-permute-start | bytes 1179656 | tf_op jit(solution)/shard_map/ppermute | solution.py:38
  20.6 22.6 %collective-permute-start.10 = (f32[8,32,768]{2,1,0:T(8,128)S(1)}, f32[8,32,768]{2,1,0:T(8,128)S(1)}, u32[]{:S(2)}, u32[]{:S(2)}) collective-permute-start(f32[8,32,768]{2,1,0:T(8,128)S(1)} %get-tuple-element.63.refs_4_), channel_id=1, source_target_pairs={{0,1},{1,2},{2,3},{3,0},{4,5},{5,6},{6,7},{7,4},{8,9},{9,10},{10,1... | collective-permute-start | bytes 2359304 | tf_op jit(solution)/shard_map/ppermute | solution.py:38
  22.3 20.9 %collective-permute-start.11 = (f32[8,32,768]{2,1,0:T(8,128)S(1)}, f32[8,32,768]{2,1,0:T(8,128)S(1)}, u32[]{:S(2)}, u32[]{:S(2)}) collective-permute-start(f32[8,32,768]{2,1,0:T(8,128)S(1)} %get-tuple-element.69), channel_id=1, source_target_pairs={{0,3},{1,0},{2,1},{3,2},{4,7},{5,4},{6,5},{7,6},{8,11},{9,8},{10,9... | collective-permute-start | bytes 2359304 | tf_op jit(solution)/shard_map/ppermute | solution.py:38
  28.3 9.9 %collective-permute-start.6 = (f32[32,3072]{1,0:T(8,128)S(1)}, f32[32,3072]{1,0:T(8,128)S(1)}, u32[]{:S(2)}, u32[]{:S(2)}) collective-permute-start(f32[32,3072]{1,0:T(8,128)S(1)} %get-tuple-element.64.refs_4_), channel_id=1, source_target_pairs={{0,8},{1,9},{2,10},{3,11},{4,12},{5,13},{6,14},{7,15},{8,16},{9,17... | collective-permute-start | bytes 1179656 | tf_op jit(solution)/shard_map/ppermute | solution.py:38
  31.4 9.6 %collective-permute-start.7 = (f32[32,3072]{1,0:T(8,128)S(1)}, f32[32,3072]{1,0:T(8,128)S(1)}, u32[]{:S(2)}, u32[]{:S(2)}) collective-permute-start(f32[32,3072]{1,0:T(8,128)S(1)} %get-tuple-element.65), channel_id=1, source_target_pairs={{0,56},{1,57},{2,58},{3,59},{4,60},{5,61},{6,62},{7,63},{8,0},{9,1... | collective-permute-start | bytes 1179656 | tf_op jit(solution)/shard_map/ppermute | solution.py:38
  41.1 12.5 %collective-permute-start.8 = (f32[32,3072]{1,0:T(8,128)S(1)}, f32[32,3072]{1,0:T(8,128)S(1)}, u32[]{:S(2)}, u32[]{:S(2)}) collective-permute-start(f32[32,3072]{1,0:T(8,128)S(1)} %get-tuple-element.66.refs_3_), channel_id=1, source_target_pairs={{0,8},{1,9},{2,10},{3,11},{4,12},{5,13},{6,14},{7,15},{8,16},{9,17... | collective-permute-start | bytes 1179656 | tf_op jit(solution)/shard_map/ppermute | solution.py:38
  42.9 10.7 %collective-permute-start.9 = (f32[32,3072]{1,0:T(8,128)S(1)}, f32[32,3072]{1,0:T(8,128)S(1)}, u32[]{:S(2)}, u32[]{:S(2)}) collective-permute-start(f32[32,3072]{1,0:T(8,128)S(1)} %get-tuple-element.67), channel_id=1, source_target_pairs={{0,56},{1,57},{2,58},{3,59},{4,60},{5,61},{6,62},{7,63},{8,0},{9,1... | collective-permute-start | bytes 1179656 | tf_op jit(solution)/shard_map/ppermute | solution.py:38
  43.3 6.8 %collective-permute-start.12 = (f32[16,768]{1,0:T(8,128)S(1)}, f32[16,768]{1,0:T(8,128)S(1)}, u32[]{:S(2)}, u32[]{:S(2)}) collective-permute-start(f32[16,768]{1,0:T(8,128)S(1)} %get-tuple-element.72), channel_id=1, source_target_pairs={{0,8},{1,9},{2,10},{3,11},{4,12},{5,13},{6,14},{7,15},{8,16},{9,17... | collective-permute-start | bytes 147464 | tf_op jit(solution)/shard_map/ppermute | solution.py:38
  45.2 6.3 %collective-permute-start.13 = (f32[16,768]{1,0:T(8,128)S(1)}, f32[16,768]{1,0:T(8,128)S(1)}, u32[]{:S(2)}, u32[]{:S(2)}) collective-permute-start(f32[16,768]{1,0:T(8,128)S(1)} %get-tuple-element.73), channel_id=1, source_target_pairs={{0,56},{1,57},{2,58},{3,59},{4,60},{5,61},{6,62},{7,63},{8,0},{9,1... | collective-permute-start | bytes 147464 | tf_op jit(solution)/shard_map/ppermute | solution.py:38
  51.5 5.7 %collective-permute-start.15 = (f32[32,768]{1,0:T(8,128)S(1)}, f32[32,768]{1,0:T(8,128)S(1)}, u32[]{:S(2)}, u32[]{:S(2)}) collective-permute-start(f32[32,768]{1,0:T(8,128)S(1)} %get-tuple-element.74.refs_4_), channel_id=1, source_target_pairs={{0,8},{1,9},{2,10},{3,11},{4,12},{5,13},{6,14},{7,15},{8,16},{9,17... | collective-permute-start | bytes 294920 | tf_op jit(solution)/shard_map/ppermute | solution.py:38
  53.3 5.3 %collective-permute-start.16 = (f32[32,768]{1,0:T(8,128)S(1)}, f32[32,768]{1,0:T(8,128)S(1)}, u32[]{:S(2)}, u32[]{:S(2)}) collective-permute-start(f32[32,768]{1,0:T(8,128)S(1)} %get-tuple-element.79), channel_id=1, source_target_pairs={{0,56},{1,57},{2,58},{3,59},{4,60},{5,61},{6,62},{7,63},{8,0},{9,1... | collective-permute-start | bytes 294920 | tf_op jit(solution)/shard_map/ppermute | solution.py:38
  53.7 7.1 %collective-permute-start.14 = (f32[16,3072]{1,0:T(8,128)S(1)}, f32[16,3072]{1,0:T(8,128)S(1)}, u32[]{:S(2)}, u32[]{:S(2)}) collective-permute-start(f32[16,3072]{1,0:T(8,128)S(1)} %get-tuple-element.76.refs_4_), channel_id=1, source_target_pairs={{0,1},{1,0},{2,3},{3,2},{4,5},{5,4},{6,7},{7,6},{8,9},{9,8},{10,11... | collective-permute-start | bytes 589832 | tf_op jit(solution)/shard_map/ppermute | solution.py:38
  58.7 4.7 %collective-permute-start.18 = (f32[32,768]{1,0:T(8,128)S(1)}, f32[32,768]{1,0:T(8,128)S(1)}, u32[]{:S(2)}, u32[]{:S(2)}) collective-permute-start(f32[32,768]{1,0:T(8,128)S(1)} %get-tuple-element.80.refs_3_), channel_id=1, source_target_pairs={{0,8},{1,9},{2,10},{3,11},{4,12},{5,13},{6,14},{7,15},{8,16},{9,17... | collective-permute-start | bytes 294920 | tf_op jit(solution)/shard_map/ppermute | solution.py:38
  60.5 4.6 %collective-permute-start.19 = (f32[32,768]{1,0:T(8,128)S(1)}, f32[32,768]{1,0:T(8,128)S(1)}, u32[]{:S(2)}, u32[]{:S(2)}) collective-permute-start(f32[32,768]{1,0:T(8,128)S(1)} %get-tuple-element.85), channel_id=1, source_target_pairs={{0,56},{1,57},{2,58},{3,59},{4,60},{5,61},{6,62},{7,63},{8,0},{9,1... | collective-permute-start | bytes 294920 | tf_op jit(solution)/shard_map/ppermute | solution.py:38
  60.8 6.4 %collective-permute-start.17 = (f32[8,3072]{1,0:T(8,128)S(1)}, f32[8,3072]{1,0:T(8,128)S(1)}, u32[]{:S(2)}, u32[]{:S(2)}) collective-permute-start(f32[8,3072]{1,0:T(8,128)S(1)} %get-tuple-element.82.refs_4_), channel_id=1, source_target_pairs={{0,3},{1,2},{2,1},{3,0},{4,7},{5,6},{6,5},{7,4},{8,11},{9,10},{10,... | collective-permute-start | bytes 294920 | tf_op jit(solution)/shard_map/ppermute | solution.py:38
  65.1 4.7 %collective-permute-start.21 = (f32[32,768]{1,0:T(8,128)S(1)}, f32[32,768]{1,0:T(8,128)S(1)}, u32[]{:S(2)}, u32[]{:S(2)}) collective-permute-start(f32[32,768]{1,0:T(8,128)S(1)} %get-tuple-element.86.refs_2_), channel_id=1, source_target_pairs={{0,8},{1,9},{2,10},{3,11},{4,12},{5,13},{6,14},{7,15},{8,16},{9,17... | collective-permute-start | bytes 294920 | tf_op jit(solution)/shard_map/ppermute | solution.py:38
  66.8 4.6 %collective-permute-start.22 = (f32[32,768]{1,0:T(8,128)S(1)}, f32[32,768]{1,0:T(8,128)S(1)}, u32[]{:S(2)}, u32[]{:S(2)}) collective-permute-start(f32[32,768]{1,0:T(8,128)S(1)} %get-tuple-element.88), channel_id=1, source_target_pairs={{0,56},{1,57},{2,58},{3,59},{4,60},{5,61},{6,62},{7,63},{8,0},{9,1... | collective-permute-start | bytes 294920 | tf_op jit(solution)/shard_map/ppermute | solution.py:38
  71.4 4.2 %collective-permute-start.23 = (f32[16,768]{1,0:T(8,128)S(1)}, f32[16,768]{1,0:T(8,128)S(1)}, u32[]{:S(2)}, u32[]{:S(2)}) collective-permute-start(f32[16,768]{1,0:T(8,128)S(1)} %get-tuple-element.90), channel_id=1, source_target_pairs={{0,4},{1,5},{2,6},{3,7},{4,0},{5,1},{6,2},{7,3},{8,12},{9,13},{10,... | collective-permute-start | bytes 147464 | tf_op jit(solution)/shard_map/ppermute | solution.py:38
  73.0 11.0 %collective-permute-start.20 = (f32[8,3072]{1,0:T(8,128)S(1)}, f32[8,3072]{1,0:T(8,128)S(1)}, u32[]{:S(2)}, u32[]{:S(2)}) collective-permute-start(f32[8,3072]{1,0:T(8,128)S(1)} %shard_map.77.refs_4_.left_ref), channel_id=1, source_target_pairs={{0,4},{1,5},{2,6},{3,7},{4,0},{5,1},{6,2},{7,3},{8,12},{9,13},{10,... | collective-permute-start | bytes 294920 | tf_op jit(solution)/shard_map/ppermute | solution.py:38
  75.6 4.8 %collective-permute-start.24 = (f32[16,768]{1,0:T(8,128)S(1)}, f32[16,768]{1,0:T(8,128)S(1)}, u32[]{:S(2)}, u32[]{:S(2)}) collective-permute-start(f32[16,768]{1,0:T(8,128)S(1)} %shard_map.79.refs_0_), channel_id=1, source_target_pairs={{0,1},{1,0},{2,3},{3,2},{4,5},{5,4},{6,7},{7,6},{8,9},{9,8},{10,11... | collective-permute-start | bytes 147464 | tf_op jit(solution)/shard_map/ppermute | solution.py:38
  75.7 5.7 %collective-permute-start.25 = (f32[16,768]{1,0:T(8,128)S(1)}, f32[16,768]{1,0:T(8,128)S(1)}, u32[]{:S(2)}, u32[]{:S(2)}) collective-permute-start(f32[16,768]{1,0:T(8,128)S(1)} %shard_map.79.refs_0_), channel_id=1, source_target_pairs={{0,2},{1,3},{2,0},{3,1},{4,6},{5,7},{6,4},{7,5},{8,10},{9,11},{10,... | collective-permute-start | bytes 147464 | tf_op jit(solution)/shard_map/ppermute | solution.py:38
  78.8 5.3 %collective-permute-start.26 = (f32[16,768]{1,0:T(8,128)S(1)}, f32[16,768]{1,0:T(8,128)S(1)}, u32[]{:S(2)}, u32[]{:S(2)}) collective-permute-start(f32[16,768]{1,0:T(8,128)S(1)} %shard_map.79.refs_0_), channel_id=1, source_target_pairs={{0,3},{1,2},{2,1},{3,0},{4,7},{5,6},{6,5},{7,4},{8,11},{9,10},{10,... | collective-permute-start | bytes 147464 | tf_op jit(solution)/shard_map/ppermute | solution.py:38
  84.7 3.8 %collective-permute-start.27 = (f32[32,128]{1,0:T(8,128)S(1)}, f32[32,128]{1,0:T(8,128)S(1)}, u32[]{:S(2)}, u32[]{:S(2)}) collective-permute-start(f32[32,128]{1,0:T(8,128)S(1)} %shard_map.80), channel_id=1, source_target_pairs={{0,8},{1,9},{2,10},{3,11},{4,12},{5,13},{6,14},{7,15},{8,0},{9,1},... | collective-permute-start | bytes 49160 | tf_op jit(solution)/shard_map/ppermute | solution.py:38
  88.5 4.6 %collective-permute-start.28 = (f32[32,128]{1,0:T(8,128)S(1)}, f32[32,128]{1,0:T(8,128)S(1)}, u32[]{:S(2)}, u32[]{:S(2)}) collective-permute-start(f32[32,128]{1,0:T(8,128)S(1)} %add.36), channel_id=1, source_target_pairs={{0,16},{1,17},{2,18},{3,19},{4,20},{5,21},{6,22},{7,23},{8,24},{9,... | collective-permute-start | bytes 49160 | tf_op jit(solution)/shard_map/ppermute | solution.py:38
  93.1 6.7 %collective-permute-start.29 = (f32[32,128]{1,0:T(8,128)S(1)}, f32[32,128]{1,0:T(8,128)S(1)}, u32[]{:S(2)}, u32[]{:S(2)}) collective-permute-start(f32[32,128]{1,0:T(8,128)S(1)} %add.37), channel_id=1, source_target_pairs={{0,56},{1,57},{2,58},{3,59},{4,60},{5,61},{6,62},{7,63},{8,48},{9,... | collective-permute-start | bytes 49160 | tf_op jit(solution)/shard_map/ppermute | solution.py:38
  99.9 1.2 %collective-permute-start.30 = (f32[1,32,128]{2,1,0:T(8,128)S(1)}, f32[1,32,128]{2,1,0:T(8,128)S(1)}, u32[]{:S(2)}, u32[]{:S(2)}) collective-permute-start(f32[1,32,128]{2,1,0:T(8,128)S(1)} %multiply_bitcast_fusion), channel_id=1, source_target_pairs={{0,64},{64,0},{128,192},{192,128},{1,65},{65,1},{129,193},{193,129... | collective-permute-start | bytes 49160 | tf_op jit(solution)/shard_map/ppermute | solution.py:279
  101.1 5.5 %collective-permute-start.31 = (f32[2,32,128]{2,1,0:T(8,128)S(1)}, f32[2,32,128]{2,1,0:T(8,128)S(1)}, u32[]{:S(2)}, u32[]{:S(2)}) collective-permute-start(f32[2,32,128]{2,1,0:T(8,128)S(1)} %pad_maximum_fusion.1), channel_id=1, source_target_pairs={{0,128},{64,192},{128,0},{192,64},{1,129},{65,193},{129,1},{193,65... | collective-permute-start | bytes 98312 | tf_op jit(solution)/shard_map/ppermute | solution.py:279
  106.9 4.8 %collective-permute-start.32 = (f32[32,128]{1,0:T(8,128)S(1)}, f32[32,128]{1,0:T(8,128)S(1)}, u32[]{:S(2)}, u32[]{:S(2)}) collective-permute-start(f32[32,128]{1,0:T(8,128)S(1)} %fusion), channel_id=1, source_target_pairs={{0,1},{1,0},{2,3},{3,2},{4,5},{5,4},{6,7},{7,6},{8,9},{9,8},{10,11... | collective-permute-start | bytes 49160 | tf_op jit(solution)/shard_map/ppermute | solution.py:38
  107.0 5.3 %collective-permute-start.33 = (f32[32,128]{1,0:T(8,128)S(1)}, f32[32,128]{1,0:T(8,128)S(1)}, u32[]{:S(2)}, u32[]{:S(2)}) collective-permute-start(f32[32,128]{1,0:T(8,128)S(1)} %fusion), channel_id=1, source_target_pairs={{0,2},{1,3},{2,0},{3,1},{4,6},{5,7},{6,4},{7,5},{8,10},{9,11},{10,... | collective-permute-start | bytes 49160 | tf_op jit(solution)/shard_map/ppermute | solution.py:38
  110.1 4.9 %collective-permute-start.34 = (f32[32,128]{1,0:T(8,128)S(1)}, f32[32,128]{1,0:T(8,128)S(1)}, u32[]{:S(2)}, u32[]{:S(2)}) collective-permute-start(f32[32,128]{1,0:T(8,128)S(1)} %fusion), channel_id=1, source_target_pairs={{0,3},{1,2},{2,1},{3,0},{4,7},{5,6},{6,5},{7,4},{8,11},{9,10},{10,... | collective-permute-start | bytes 49160 | tf_op jit(solution)/shard_map/ppermute | solution.py:38
  115.1 3.8 %collective-permute-start.35 = (f32[32,128]{1,0:T(8,128)S(1)}, f32[32,128]{1,0:T(8,128)S(1)}, u32[]{:S(2)}, u32[]{:S(2)}) collective-permute-start(f32[32,128]{1,0:T(8,128)S(1)} %add_add_fusion), channel_id=1, source_target_pairs={{0,4},{1,5},{2,6},{3,7},{4,0},{5,1},{6,2},{7,3},{8,12},{9,13},{10,... | collective-permute-start | bytes 49160 | tf_op jit(solution)/shard_map/ppermute | solution.py:38

commit v4 on v3

--- a/solution.py
+++ b/solution.py
@@ -9,10 +9,10 @@
 TOK_GRP = 24576
 EX_GRP = 32
 Z, X, Y = 8, 2, 4
-LEFT = ROWS // Y
-RIGHT = ROWS // X
+LEFT = ROWS // X
+RIGHT = ROWS // Y
 WIDE = TOK_GRP // Z
-SUB = WIDE // Y
+HALF = WIDE // 2
 FAR, REST, ALL = (4,), (3, 5, 2, 6, 1, 7, 0), tuple(range(Z))
 SIZE = {"z": Z, "x": X, "y": Y}
 MIB = 1024 * 1024
@@ -101,8 +101,10 @@
     y = at_ref[1]
     outs = projections(weight_ref, input_ref, *scratch, begins(at_ref, ALL))
     for step, out in enumerate(outs):
-        for sub in range(Y):
-            turned[sub] = out[:, sub * SUB : (sub + 1) * SUB]
+        for row in range(Y):
+            for side in range(2):
+                tokens = out[row * RIGHT : (row + 1) * RIGHT, side * HALF : (side + 1) * HALF]
+                turned[row, side] = tokens
         own_ref[step] = turned[y]
         next_ref[step] = turned[lax.rem(y + 1, Y)]
         last_ref[step] = turned[lax.rem(y + 3, Y)]
@@ -147,13 +149,6 @@
 
 def left_half_kernel(at_ref, own_ref, rising_ref, falling_ref, keep_ref, give_ref, held):
     total = own_ref[...] + rising_ref[...] + falling_ref[...]
-    held[0], held[1] = total[: ROWS // 2], total[ROWS // 2 :]
-    keep_ref[...] = held[at_ref[0]]
-    give_ref[...] = held[1 - at_ref[0]]
-
-
-def left_quarter_kernel(at_ref, own_ref, moved_ref, keep_ref, give_ref, held):
-    total = own_ref[...] + moved_ref[...]
     held[0], held[1] = total[:LEFT], total[LEFT:]
     keep_ref[...] = held[at_ref[0]]
     give_ref[...] = held[1 - at_ref[0]]
@@ -167,35 +162,26 @@
     for step in ALL:
         total = own_ref[step] + rising_ref[step] + falling_ref[step]
         if step == FAR[0]:
-            refs[-2][...] = total[: ROWS // 2]
-            refs[-1][...] = total[ROWS // 2 :]
+            refs[-2][...] = total[:1]
+            refs[-1][...] = total[1:]
         else:
             refs[REST.index(step)][...] = total
 
 
-def right_half_kernel(at_ref, *refs):
-    *terms, keep_ref, give_ref, held = refs
-    total = terms[0][...]
-    for term in terms[1:]:
-        total += term[...]
-    held[0], held[1] = total[:RIGHT], total[RIGHT:]
-    keep_ref[...] = held[at_ref[0]]
-    give_ref[...] = held[1 - at_ref[0]]
-
-
-def feature_kernel(at_ref, left_ref, moved_ref, ids_ref, *refs):
-    *pieces, out_ref, held = refs
-    left = left_ref[...] + moved_ref[...]
-    for sub in range(Y):
-        held[sub] = left[:, sub * SUB : (sub + 1) * SUB]
-    labels = lax.broadcasted_iota(jnp.int32, (EX_GRP, SUB), 0)
+def right_sum_kernel(own_ref, rising_ref, falling_ref, out_ref):
+    out_ref[...] = own_ref[...] + rising_ref[...] + falling_ref[...]
+
+
+def feature_kernel(own_ref, near_ref, opposite_ref, last_ref, right_ref, moved_ref, ids_ref, out_ref):
+    left = (own_ref[...] + near_ref[...]) + (opposite_ref[...] + last_ref[...])
+    labels = lax.broadcasted_iota(jnp.int32, (EX_GRP, HALF), 0)
     over = (((1,), (1,)), ((), ()))
     total = jnp.zeros((EX_GRP, LEFT * RIGHT), jnp.float32)
-    for bits, piece in enumerate(pieces):
-        right = piece[...]
-        sub = at_ref[0] ^ bits
-        member = (ids_ref[sub] == labels).astype(jnp.float32).astype(jnp.bfloat16)
-        part = held[sub]
+    for side in range(2):
+        tokens = slice(side * HALF, (side + 1) * HALF)
+        member = (ids_ref[:, tokens] == labels).astype(jnp.float32).astype(jnp.bfloat16)
+        right = right_ref[side] + moved_ref[side]
+        part = left[:, tokens]
         product = jnp.concatenate([part[a : a + 1] * right for a in range(LEFT)], axis=0)
         high = product.astype(jnp.bfloat16)
         low = (product - high.astype(jnp.float32)).astype(jnp.bfloat16)
@@ -210,12 +196,12 @@
     place = (at["z"], at["y"])
 
     whole, half = (ROWS, WIDE), (ROWS // 2, WIDE)
-    quarter = (Z, ROWS, SUB)
+    chunk = (2, RIGHT, HALF)
     far = projected(left_far_kernel, place, in_proj, activations, 1, [half] * 2)
     left_moved = both_ways(*far, "z")
     *right, rising, falling = projected(
-        right_kernel, place, out_proj, out_grads, Z, [quarter] * 3 + [(Z // 2, ROWS, SUB)] * 2,
-        [pltpu.VMEM((Y, ROWS, SUB), jnp.float32)], far[:1],
+        right_kernel, place, out_proj, out_grads, Z, [(Z, *chunk)] * 3 + [(Z // 2, *chunk)] * 2,
+        [pltpu.VMEM((Y, *chunk), jnp.float32)], far[:1],
     )
     right_moved = both_ways(rising, falling, "y")
     left = projected(
@@ -232,43 +218,32 @@
     left_moved = both_ways(*sent, "z")
     *right, rising, falling = local(
         right_chunks_kernel, (), [right[0], *right_moved],
-        [(ROWS, SUB)] * 7 + [(ROWS // 2, SUB)] * 2, after=sent[:1],
+        [chunk] * 7 + [(1, RIGHT, HALF)] * 2, after=sent[:1],
     )
     right_moved = both_ways(rising, falling, "z")
     sent = step_add(right[0], right[1], right_moved, [], half=True)
     right_moved = both_ways(*sent, "z")
-    first, second = (at["y"] ^ (at["y"] >> 1)) & 1, at["y"] >> 1
     keep, give = local(
-        left_half_kernel, (first,), [left[6], *left_moved], [half] * 2, [(2, *half)], after=sent[:1]
-    )
-    left_moved = mixed(give, "y", 1)
+        left_half_kernel, (at["x"],), [left[6], *left_moved], [half] * 2, [(2, *half)], after=sent[:1]
+    )
+    left_moved = mixed(give, "x", 1)
     sent = step_add(right[2], right[3], right_moved, [give])
     right_moved = both_ways(*sent, "z")
-    keep, give = local(
-        left_quarter_kernel, (second,), [keep, left_moved], [(LEFT, WIDE)] * 2, [(2, LEFT, WIDE)],
-        after=sent[:1],
-    )
-    left_moved = mixed(give, "y", 3)
-    sent = step_add(right[4], right[5], right_moved, [give])
+    (left,) = local(add_kernel, (), [keep, left_moved], [half], after=sent[:1])
+    sent = step_add(right[4], right[5], right_moved, [])
     right_moved = both_ways(*sent, "z")
-    (left,) = local(add_kernel, (), [keep, left_moved], [(LEFT, WIDE)], after=sent[:1])
-    left_moved = mixed(left, "x", 1)
-    keep, give = local(
-        right_half_kernel, (at["x"],), [right[6], *right_moved], [(RIGHT, SUB)] * 2, [(2, RIGHT, SUB)],
-        after=[left],
-    )
-    (right,) = local(add_kernel, (), [keep, mixed(give, "x", 1)], [(RIGHT, SUB)])
-    pieces = [right] + [mixed(right, "y", bits) for bits in range(1, Y)]
-
-    ids = lax.dynamic_slice(example_ids, (0, at["z"] * WIDE), (1, WIDE)).reshape(Y, 1, SUB)
+    lefts = [left] + [mixed(left, "y", bits) for bits in range(1, Y)]
+    (right,) = local(right_sum_kernel, (), [right[6], *right_moved], [chunk])
+    right_moved = mixed(right, "x", 1)
+
+    ids = lax.dynamic_slice(example_ids, (0, at["z"] * WIDE), (1, WIDE))
     features = pl.pallas_call(
         feature_kernel,
-        in_specs=[SMEM] + [VMEM] * 7,
+        in_specs=[VMEM] * 7,
         out_specs=VMEM,
         out_shape=jax.ShapeDtypeStruct((EX_GRP, LEFT * RIGHT), jnp.float32),
-        scratch_shapes=[pltpu.VMEM((Y, LEFT, SUB), jnp.float32)],
-        compiler_params=pltpu.CompilerParams(vmem_limit_bytes=8 * MIB),
-    )(jnp.stack([at["y"]]), left, left_moved, ids, *pieces)
+        compiler_params=pltpu.CompilerParams(vmem_limit_bytes=12 * MIB),
+    )(*lefts, right, right_moved, ids)
     for bits in (1, 2, 7):
         features = features + mixed(features, "z", bits)
 

time: 120 us -> 114 us (0.950)
  waiting for transfers between devices: 57.3 us -> 51.6 us
    ppermute x34 -> x32, waiting for transfers between devices: 53.7 us -> 48.1 us  [send(): return lax.ppermute(value, 'par', pairs)]
    ppermute x34 -> x32, starting transfers between devices: 47 us -> 46.9 us  [send(): return lax.ppermute(value, 'par', pairs)]
  transfers between devices with their start and end apart: 36 -> 34, of which waited for: 24 -> 21; matrix products, arithmetic and copies ran while one was open for 0% -> 0% of each run, Pallas kernels for 7% -> 7%
where the time goes in v4:
time: 114 us
  waiting for transfers between devices  51.6 us (45%)
  starting transfers between devices  50.3 us (44%)
  Pallas kernels  10.7 us (9%)
    ppermute x32, waiting for transfers between devices, send(): return lax.ppermute(value, 'par', pairs)  48.1 us
    ppermute x32, starting transfers between devices, send(): return lax.ppermute(value, 'par', pairs)  46.9 us
    pallas_call x3, Pallas kernels, projected(): pl.pallas_call(ordered(kernel, 3, after), in_specs=[SMEM, *[pl.BlockSpec(...  9.26 us
    ppermute x2, waiting for transfers between devices, on_device(): other = lax.ppermute(cols, 'grp', [(i, i ^ bit) for i in range(4)])  3.54 us
    ppermute x2, starting transfers between devices, on_device(): other = lax.ppermute(cols, 'grp', [(i, i ^ bit) for i in range(4)])  3.37 us
  transfers between devices with their start and end apart: 34, of which 21 were waited for; matrix products, arithmetic and copies ran while one was open for 0% of the time, Pallas kernels for 7%

profile of v4, /device:TPU:32, one launch (start us, length us, event | category | flops | bytes accessed | tf_op | source)
XLA Modules:
  0.0 113.8 jit_solution(1904884775196826968)
XLA Ops:
  0.1 1.8 %shard_map.64 = (f32[16,3072]{1,0:T(8,128)S(1)}, f32[16,3072]{1,0:T(8,128)S(1)}) custom-call(s32[2]{0:T(128)S(1)} %pad_add_fusion.refs_0_, bf16[32,64]{1,0:T(8,128)(2,1)} %bitcast.10, bf16[64,24576]{1,0:T(8,128)(2,1)} %refs_2_.5), custom_call_target="tpu_custom_call" | custom-call | tf_op jit(solution)/shard_map/pallas_call | solution.py:117
  1.8 2.0 %collective-permute-start = (f32[16,3072]{1,0:T(8,128)S(1)}, f32[16,3072]{1,0:T(8,128)S(1)}, u32[]{:S(2)}, u32[]{:S(2)}) collective-permute-start(f32[16,3072]{1,0:T(8,128)S(1)} %get-tuple-element.44.refs_3_), channel_id=1, source_target_pairs={{0,8},{1,9},{2,10},{3,11},{4,12},{5,13},{6,14},{7,15},{8,16},{9,17... | collective-permute-start | bytes 589832 | tf_op jit(solution)/shard_map/ppermute | solution.py:38
  3.8 0.1 collective-permute-start.1
  4.0 4.5 %shard_map.65 = (f32[8,2,8,1536]{3,2,1,0:T(8,128)S(1)}, f32[8,2,8,1536]{3,2,1,0:T(8,128)S(1)}, f32[8,2,8,1536]{3,2,1,0:T(8,128)S(1)}, f32[4,2,8,1536]{3,2,1,0:T(8,128)S(1)}, f32[4,2,8,1536]{3,2,1,0:T(8,128)S(1)}) custom-call(s32[2]{0:T(128)S(1)} %pad_add_fusion.refs_0_, bf16[32,172]{1,0:T(8,128)(2,1)} %bitcast.12, bf16[172,24576]{1,0:T(8,128)(2,1)} %refs_2_.4, ...), custom_call_target="tpu_custom_call" | custom-call | tf_op jit(solution)/shard_map/pallas_call | solution.py:117
  8.5 1.6 %collective-permute-start.4 = (f32[4,2,8,1536]{3,2,1,0:T(8,128)S(1)}, f32[4,2,8,1536]{3,2,1,0:T(8,128)S(1)}, u32[]{:S(2)}, u32[]{:S(2)}) collective-permute-start(f32[4,2,8,1536]{3,2,1,0:T(8,128)S(1)} %get-tuple-element.45.refs_3_), channel_id=1, source_target_pairs={{0,1},{1,2},{2,3},{3,0},{4,5},{5,6},{6,7},{7,4},{8,9},{9,10},{10,1... | collective-permute-start | bytes 1179656 | tf_op jit(solution)/shard_map/ppermute | solution.py:38
  10.1 1.7 %collective-permute-start.5 = (f32[4,2,8,1536]{3,2,1,0:T(8,128)S(1)}, f32[4,2,8,1536]{3,2,1,0:T(8,128)S(1)}, u32[]{:S(2)}, u32[]{:S(2)}) collective-permute-start(f32[4,2,8,1536]{3,2,1,0:T(8,128)S(1)} %get-tuple-element.58), channel_id=1, source_target_pairs={{0,3},{1,0},{2,1},{3,2},{4,7},{5,4},{6,5},{7,6},{8,11},{9,8},{10,9... | collective-permute-start | bytes 1179656 | tf_op jit(solution)/shard_map/ppermute | solution.py:38
  11.8 3.0 %shard_map.66 = (f32[32,3072]{1,0:T(8,128)S(1)}, f32[32,3072]{1,0:T(8,128)S(1)}, f32[32,3072]{1,0:T(8,128)S(1)}, f32[32,3072]{1,0:T(8,128)S(1)}, f32[32,3072]{1,...) custom-call(s32[2]{0:T(128)S(1)} %pad_add_fusion.refs_0_, bf16[32,64]{1,0:T(8,128)(2,1)} %bitcast.11, ...), custom_call_target="tpu_custom_call" | custom-call | tf_op jit(solution)/shard_map/pallas_call | solution.py:117
  14.9 2.0 %collective-permute-start.2 = (f32[32,3072]{1,0:T(8,128)S(1)}, f32[32,3072]{1,0:T(8,128)S(1)}, u32[]{:S(2)}, u32[]{:S(2)}) collective-permute-start(f32[32,3072]{1,0:T(8,128)S(1)} %get-tuple-element.54.refs_4_), channel_id=1, source_target_pairs={{0,8},{1,9},{2,10},{3,11},{4,12},{5,13},{6,14},{7,15},{8,16},{9,17... | collective-permute-start | bytes 1179656 | tf_op jit(solution)/shard_map/ppermute | solution.py:38
  16.9 2.2 %collective-permute-start.3 = (f32[32,3072]{1,0:T(8,128)S(1)}, f32[32,3072]{1,0:T(8,128)S(1)}, u32[]{:S(2)}, u32[]{:S(2)}) collective-permute-start(f32[32,3072]{1,0:T(8,128)S(1)} %get-tuple-element.55), channel_id=1, source_target_pairs={{0,56},{1,57},{2,58},{3,59},{4,60},{5,61},{6,62},{7,63},{8,0},{9,1... | collective-permute-start | bytes 1179656 | tf_op jit(solution)/shard_map/ppermute | solution.py:38
  19.1 1.2 %collective-permute-done.4.refs_2_ = f32[4,2,8,1536]{3,2,1,0:T(8,128)S(1)} collective-permute-done((f32[4,2,8,1536]{3,2,1,0:T(8,128)S(1)}, f32[4,2,8,1536]{3,2,1,0:T(8,128)S(1)}, u32[]{:S(2)}, u32[]{:S(2)}) %collective-permute-start.4) | collective-permute-done | bytes 393248 | tf_op jit(solution)/shard_map/ppermute | solution.py:38
  20.3 0.1 shard_map.68
  20.5 1.7 %collective-permute-start.10 = (f32[8,2,8,1536]{3,2,1,0:T(8,128)S(1)}, f32[8,2,8,1536]{3,2,1,0:T(8,128)S(1)}, u32[]{:S(2)}, u32[]{:S(2)}) collective-permute-start(f32[8,2,8,1536]{3,2,1,0:T(8,128)S(1)} %get-tuple-element.59.refs_4_), channel_id=1, source_target_pairs={{0,1},{1,2},{2,3},{3,0},{4,5},{5,6},{6,7},{7,4},{8,9},{9,10},{10,1... | collective-permute-start | bytes 2359304 | tf_op jit(solution)/shard_map/ppermute | solution.py:38
  22.1 1.6 %collective-permute-start.11 = (f32[8,2,8,1536]{3,2,1,0:T(8,128)S(1)}, f32[8,2,8,1536]{3,2,1,0:T(8,128)S(1)}, u32[]{:S(2)}, u32[]{:S(2)}) collective-permute-start(f32[8,2,8,1536]{3,2,1,0:T(8,128)S(1)} %get-tuple-element.65), channel_id=1, source_target_pairs={{0,3},{1,0},{2,1},{3,2},{4,7},{5,4},{6,5},{7,6},{8,11},{9,8},{10,9... | collective-permute-start | bytes 2359304 | tf_op jit(solution)/shard_map/ppermute | solution.py:38
  23.8 3.6 %collective-permute-done.2.refs_2_ = f32[32,3072]{1,0:T(8,128)S(1)} collective-permute-done((f32[32,3072]{1,0:T(8,128)S(1)}, f32[32,3072]{1,0:T(8,128)S(1)}, u32[]{:S(2)}, u32[]{:S(2)}) %collective-permute-start.2) | collective-permute-done | bytes 393248 | tf_op jit(solution)/shard_map/ppermute | solution.py:38
  27.4 0.6 collective-permute-done.3.refs_3_
  28.0 0.1 shard_map.69
  28.2 3.0 %collective-permute-start.6 = (f32[32,3072]{1,0:T(8,128)S(1)}, f32[32,3072]{1,0:T(8,128)S(1)}, u32[]{:S(2)}, u32[]{:S(2)}) collective-permute-start(f32[32,3072]{1,0:T(8,128)S(1)} %get-tuple-element.60.refs_4_), channel_id=1, source_target_pairs={{0,8},{1,9},{2,10},{3,11},{4,12},{5,13},{6,14},{7,15},{8,16},{9,17... | collective-permute-start | bytes 1179656 | tf_op jit(solution)/shard_map/ppermute | solution.py:38
  31.2 6.9 %collective-permute-done.6.refs_2_ = f32[32,3072]{1,0:T(8,128)S(1)} collective-permute-done((f32[32,3072]{1,0:T(8,128)S(1)}, f32[32,3072]{1,0:T(8,128)S(1)}, u32[]{:S(2)}, u32[]{:S(2)}) %collective-permute-start.6) | collective-permute-done | bytes 393248 | tf_op jit(solution)/shard_map/ppermute | solution.py:38
  38.1 2.7 %collective-permute-done.7.refs_3_ = f32[32,3072]{1,0:T(8,128)S(1)} collective-permute-done((f32[32,3072]{1,0:T(8,128)S(1)}, f32[32,3072]{1,0:T(8,128)S(1)}, u32[]{:S(2)}, u32[]{:S(2)}) %collective-permute-start.7) | collective-permute-done | bytes 393248 | tf_op jit(solution)/shard_map/ppermute | solution.py:38
  40.8 0.1 shard_map.70
  40.9 1.8 %collective-permute-start.8 = (f32[32,3072]{1,0:T(8,128)S(1)}, f32[32,3072]{1,0:T(8,128)S(1)}, u32[]{:S(2)}, u32[]{:S(2)}) collective-permute-start(f32[32,3072]{1,0:T(8,128)S(1)} %get-tuple-element.62.refs_3_), channel_id=1, source_target_pairs={{0,8},{1,9},{2,10},{3,11},{4,12},{5,13},{6,14},{7,15},{8,16},{9,17... | collective-permute-start | bytes 1179656 | tf_op jit(solution)/shard_map/ppermute | solution.py:38
  42.7 0.3 collective-permute-start.9
  43.0 0.1 shard_map.71
  43.2 1.8 %collective-permute-start.12 = (f32[1,8,1536]{2,1,0:T(8,128)S(1)}, f32[1,8,1536]{2,1,0:T(8,128)S(1)}, u32[]{:S(2)}, u32[]{:S(2)}) collective-permute-start(f32[1,8,1536]{2,1,0:T(8,128)S(1)} %get-tuple-element.68), channel_id=1, source_target_pairs={{0,8},{1,9},{2,10},{3,11},{4,12},{5,13},{6,14},{7,15},{8,16},{9,17... | collective-permute-start | bytes 147464 | tf_op jit(solution)/shard_map/ppermute | solution.py:38
  45.0 0.3 collective-permute-start.13
  45.3 4.7 %collective-permute-done.12.refs_2_ = f32[1,8,1536]{2,1,0:T(8,128)S(1)} collective-permute-done((f32[1,8,1536]{2,1,0:T(8,128)S(1)}, f32[1,8,1536]{2,1,0:T(8,128)S(1)}, u32[]{:S(2)}, u32[]{:S(2)}) %collective-permute-start.12) | collective-permute-done | bytes 49184 | tf_op jit(solution)/shard_map/ppermute | solution.py:38
  50.0 1.3 %collective-permute-done.13.refs_3_ = f32[1,8,1536]{2,1,0:T(8,128)S(1)} collective-permute-done((f32[1,8,1536]{2,1,0:T(8,128)S(1)}, f32[1,8,1536]{2,1,0:T(8,128)S(1)}, u32[]{:S(2)}, u32[]{:S(2)}) %collective-permute-start.13) | collective-permute-done | bytes 49184 | tf_op jit(solution)/shard_map/ppermute | solution.py:38
  51.3 1.8 %collective-permute-start.15 = (f32[2,8,1536]{2,1,0:T(8,128)S(1)}, f32[2,8,1536]{2,1,0:T(8,128)S(1)}, u32[]{:S(2)}, u32[]{:S(2)}) collective-permute-start(f32[2,8,1536]{2,1,0:T(8,128)S(1)} %get-tuple-element.70.refs_4_), channel_id=1, source_target_pairs={{0,8},{1,9},{2,10},{3,11},{4,12},{5,13},{6,14},{7,15},{8,16},{9,17... | collective-permute-start | bytes 294920 | tf_op jit(solution)/shard_map/ppermute | solution.py:38
  53.1 0.3 collective-permute-start.16
  53.4 0.1 shard_map.73
  53.5 1.6 %collective-permute-start.14 = (f32[16,3072]{1,0:T(8,128)S(1)}, f32[16,3072]{1,0:T(8,128)S(1)}, u32[]{:S(2)}, u32[]{:S(2)}) collective-permute-start(f32[16,3072]{1,0:T(8,128)S(1)} %get-tuple-element.72.refs_4_), channel_id=1, source_target_pairs={{0,4},{1,5},{2,6},{3,7},{4,0},{5,1},{6,2},{7,3},{8,12},{9,13},{10,... | collective-permute-start | bytes 589832 | tf_op jit(solution)/shard_map/ppermute | solution.py:38
  55.1 1.9 %collective-permute-done.15.refs_2_ = f32[2,8,1536]{2,1,0:T(8,128)S(1)} collective-permute-done((f32[2,8,1536]{2,1,0:T(8,128)S(1)}, f32[2,8,1536]{2,1,0:T(8,128)S(1)}, u32[]{:S(2)}, u32[]{:S(2)}) %collective-permute-start.15) | collective-permute-done | bytes 98336 | tf_op jit(solution)/shard_map/ppermute | solution.py:38
  57.0 1.5 %collective-permute-done.16.refs_3_ = f32[2,8,1536]{2,1,0:T(8,128)S(1)} collective-permute-done((f32[2,8,1536]{2,1,0:T(8,128)S(1)}, f32[2,8,1536]{2,1,0:T(8,128)S(1)}, u32[]{:S(2)}, u32[]{:S(2)}) %collective-permute-start.16) | collective-permute-done | bytes 98336 | tf_op jit(solution)/shard_map/ppermute | solution.py:38
  58.5 1.8 %collective-permute-start.20 = (f32[2,8,1536]{2,1,0:T(8,128)S(1)}, f32[2,8,1536]{2,1,0:T(8,128)S(1)}, u32[]{:S(2)}, u32[]{:S(2)}) collective-permute-start(f32[2,8,1536]{2,1,0:T(8,128)S(1)} %get-tuple-element.76.refs_2_), channel_id=1, source_target_pairs={{0,8},{1,9},{2,10},{3,11},{4,12},{5,13},{6,14},{7,15},{8,16},{9,17... | collective-permute-start | bytes 294920 | tf_op jit(solution)/shard_map/ppermute | solution.py:38
  60.3 0.3 collective-permute-start.21
  60.6 2.6 %collective-permute-done.20.refs_2_ = f32[2,8,1536]{2,1,0:T(8,128)S(1)} collective-permute-done((f32[2,8,1536]{2,1,0:T(8,128)S(1)}, f32[2,8,1536]{2,1,0:T(8,128)S(1)}, u32[]{:S(2)}, u32[]{:S(2)}) %collective-permute-start.20) | collective-permute-done | bytes 98336 | tf_op jit(solution)/shard_map/ppermute | solution.py:38
  63.2 1.7 %collective-permute-done.21.refs_3_ = f32[2,8,1536]{2,1,0:T(8,128)S(1)} collective-permute-done((f32[2,8,1536]{2,1,0:T(8,128)S(1)}, f32[2,8,1536]{2,1,0:T(8,128)S(1)}, u32[]{:S(2)}, u32[]{:S(2)}) %collective-permute-start.21) | collective-permute-done | bytes 98336 | tf_op jit(solution)/shard_map/ppermute | solution.py:38
  65.0 1.7 %collective-permute-start.22 = (f32[2,8,1536]{2,1,0:T(8,128)S(1)}, f32[2,8,1536]{2,1,0:T(8,128)S(1)}, u32[]{:S(2)}, u32[]{:S(2)}) collective-permute-start(f32[2,8,1536]{2,1,0:T(8,128)S(1)} %get-tuple-element.81), channel_id=1, source_target_pairs={{0,8},{1,9},{2,10},{3,11},{4,12},{5,13},{6,14},{7,15},{8,16},{9,17... | collective-permute-start | bytes 294920 | tf_op jit(solution)/shard_map/ppermute | solution.py:38
  66.6 0.4 collective-permute-start.23
  67.1 0.1 collective-permute-start.17
  67.2 3.2 %collective-permute-start.18 = (f32[16,3072]{1,0:T(8,128)S(1)}, f32[16,3072]{1,0:T(8,128)S(1)}, u32[]{:S(2)}, u32[]{:S(2)}) collective-permute-start(f32[16,3072]{1,0:T(8,128)S(1)} %shard_map.75.own_ref), channel_id=1, source_target_pairs={{0,2},{1,3},{2,0},{3,1},{4,6},{5,7},{6,4},{7,5},{8,10},{9,11},{10,... | collective-permute-start | bytes 589832 | tf_op jit(solution)/shard_map/ppermute | solution.py:38
  70.4 1.5 %collective-permute-start.19 = (f32[16,3072]{1,0:T(8,128)S(1)}, f32[16,3072]{1,0:T(8,128)S(1)}, u32[]{:S(2)}, u32[]{:S(2)}) collective-permute-start(f32[16,3072]{1,0:T(8,128)S(1)} %shard_map.75.own_ref), channel_id=1, source_target_pairs={{0,3},{1,2},{2,1},{3,0},{4,7},{5,6},{6,5},{7,4},{8,11},{9,10},{10,... | collective-permute-start | bytes 589832 | tf_op jit(solution)/shard_map/ppermute | solution.py:38
  71.9 1.6 %collective-permute-start.24 = (f32[2,8,1536]{2,1,0:T(8,128)S(1)}, f32[2,8,1536]{2,1,0:T(8,128)S(1)}, u32[]{:S(2)}, u32[]{:S(2)}) collective-permute-start(f32[2,8,1536]{2,1,0:T(8,128)S(1)} %shard_map.77.right_ref), channel_id=1, source_target_pairs={{0,4},{1,5},{2,6},{3,7},{4,0},{5,1},{6,2},{7,3},{8,12},{9,13},{10,... | collective-permute-start | bytes 294920 | tf_op jit(solution)/shard_map/ppermute | solution.py:38
  73.5 3.1 %collective-permute-done.24.moved_ref = f32[2,8,1536]{2,1,0:T(8,128)S(1)} collective-permute-done((f32[2,8,1536]{2,1,0:T(8,128)S(1)}, f32[2,8,1536]{2,1,0:T(8,128)S(1)}, u32[]{:S(2)}, u32[]{:S(2)}) %collective-permute-start.24) | collective-permute-done | bytes 98336 | tf_op jit(solution)/shard_map/ppermute | solution.py:38
  76.6 1.6 %collective-permute-done.19.last_ref = f32[16,3072]{1,0:T(8,128)S(1)} collective-permute-done((f32[16,3072]{1,0:T(8,128)S(1)}, f32[16,3072]{1,0:T(8,128)S(1)}, u32[]{:S(2)}, u32[]{:S(2)}) %collective-permute-start.19) | collective-permute-done | bytes 196640 | tf_op jit(solution)/shard_map/ppermute | solution.py:38
  78.3 0.6 shard_map.78
  78.9 1.5 %collective-permute-start.25 = (f32[32,128]{1,0:T(8,128)S(1)}, f32[32,128]{1,0:T(8,128)S(1)}, u32[]{:S(2)}, u32[]{:S(2)}) collective-permute-start(f32[32,128]{1,0:T(8,128)S(1)} %shard_map.78), channel_id=1, source_target_pairs={{0,8},{1,9},{2,10},{3,11},{4,12},{5,13},{6,14},{7,15},{8,0},{9,1},... | collective-permute-start | bytes 49160 | tf_op jit(solution)/shard_map/ppermute | solution.py:38
  80.4 2.4 %collective-permute-done.25 = f32[32,128]{1,0:T(8,128)S(1)} collective-permute-done((f32[32,128]{1,0:T(8,128)S(1)}, f32[32,128]{1,0:T(8,128)S(1)}, u32[]{:S(2)}, u32[]{:S(2)}) %collective-permute-start.25) | collective-permute-done | bytes 16416 | tf_op jit(solution)/shard_map/ppermute | solution.py:38
  82.7 2.3 %collective-permute-start.26 = (f32[32,128]{1,0:T(8,128)S(1)}, f32[32,128]{1,0:T(8,128)S(1)}, u32[]{:S(2)}, u32[]{:S(2)}) collective-permute-start(f32[32,128]{1,0:T(8,128)S(1)} %add.36), channel_id=1, source_target_pairs={{0,16},{1,17},{2,18},{3,19},{4,20},{5,21},{6,22},{7,23},{8,24},{9,... | collective-permute-start | bytes 49160 | tf_op jit(solution)/shard_map/ppermute | solution.py:38
  85.1 2.4 %collective-permute-done.26 = f32[32,128]{1,0:T(8,128)S(1)} collective-permute-done((f32[32,128]{1,0:T(8,128)S(1)}, f32[32,128]{1,0:T(8,128)S(1)}, u32[]{:S(2)}, u32[]{:S(2)}) %collective-permute-start.26) | collective-permute-done | bytes 16416 | tf_op jit(solution)/shard_map/ppermute | solution.py:38
  87.5 2.3 %collective-permute-start.27 = (f32[32,128]{1,0:T(8,128)S(1)}, f32[32,128]{1,0:T(8,128)S(1)}, u32[]{:S(2)}, u32[]{:S(2)}) collective-permute-start(f32[32,128]{1,0:T(8,128)S(1)} %add.37), channel_id=1, source_target_pairs={{0,56},{1,57},{2,58},{3,59},{4,60},{5,61},{6,62},{7,63},{8,48},{9,... | collective-permute-start | bytes 49160 | tf_op jit(solution)/shard_map/ppermute | solution.py:38
  89.8 4.4 %collective-permute-done.27 = f32[32,128]{1,0:T(8,128)S(1)} collective-permute-done((f32[32,128]{1,0:T(8,128)S(1)}, f32[32,128]{1,0:T(8,128)S(1)}, u32[]{:S(2)}, u32[]{:S(2)}) %collective-permute-start.27) | collective-permute-done | bytes 16416 | tf_op jit(solution)/shard_map/ppermute | solution.py:38
  94.3 1.2 %collective-permute-done.28 = f32[1,32,128]{2,1,0:T(8,128)S(1)} collective-permute-done((f32[1,32,128]{2,1,0:T(8,128)S(1)}, f32[1,32,128]{2,1,0:T(8,128)S(1)}, u32[]{:S(2)}, u32[]{:S(2)}) %collective-permute-start.28) | collective-permute-done | bytes 16416 | tf_op jit(solution)/shard_map/ppermute | solution.py:254
  95.5 3.3 %collective-permute-start.29 = (f32[2,32,128]{2,1,0:T(8,128)S(1)}, f32[2,32,128]{2,1,0:T(8,128)S(1)}, u32[]{:S(2)}, u32[]{:S(2)}) collective-permute-start(f32[2,32,128]{2,1,0:T(8,128)S(1)} %pad_maximum_fusion.1), channel_id=1, source_target_pairs={{0,128},{64,192},{128,0},{192,64},{1,129},{65,193},{129,1},{193,65... | collective-permute-start | bytes 98312 | tf_op jit(solution)/shard_map/ppermute | solution.py:254
  98.8 2.4 %collective-permute-done.29 = f32[2,32,128]{2,1,0:T(8,128)S(1)} collective-permute-done((f32[2,32,128]{2,1,0:T(8,128)S(1)}, f32[2,32,128]{2,1,0:T(8,128)S(1)}, u32[]{:S(2)}, u32[]{:S(2)}) %collective-permute-start.29) | collective-permute-done | bytes 32800 | tf_op jit(solution)/shard_map/ppermute | solution.py:254
  101.3 0.2 fusion
  101.5 0.1 collective-permute-start.30
  101.6 2.8 %collective-permute-start.31 = (f32[32,128]{1,0:T(8,128)S(1)}, f32[32,128]{1,0:T(8,128)S(1)}, u32[]{:S(2)}, u32[]{:S(2)}) collective-permute-start(f32[32,128]{1,0:T(8,128)S(1)} %fusion), channel_id=1, source_target_pairs={{0,2},{1,3},{2,0},{3,1},{4,6},{5,7},{6,4},{7,5},{8,10},{9,11},{10,... | collective-permute-start | bytes 49160 | tf_op jit(solution)/shard_map/ppermute | solution.py:38
  104.4 1.8 %collective-permute-start.32 = (f32[32,128]{1,0:T(8,128)S(1)}, f32[32,128]{1,0:T(8,128)S(1)}, u32[]{:S(2)}, u32[]{:S(2)}) collective-permute-start(f32[32,128]{1,0:T(8,128)S(1)} %fusion), channel_id=1, source_target_pairs={{0,3},{1,2},{2,1},{3,0},{4,7},{5,6},{6,5},{7,4},{8,11},{9,10},{10,... | collective-permute-start | bytes 49160 | tf_op jit(solution)/shard_map/ppermute | solution.py:38
  106.3 0.7 collective-permute-done.31
  107.0 2.3 %collective-permute-done.32 = f32[32,128]{1,0:T(8,128)S(1)} collective-permute-done((f32[32,128]{1,0:T(8,128)S(1)}, f32[32,128]{1,0:T(8,128)S(1)}, u32[]{:S(2)}, u32[]{:S(2)}) %collective-permute-start.32) | collective-permute-done | bytes 16416 | tf_op jit(solution)/shard_map/ppermute | solution.py:38
  109.4 1.6 %collective-permute-start.33 = (f32[32,128]{1,0:T(8,128)S(1)}, f32[32,128]{1,0:T(8,128)S(1)}, u32[]{:S(2)}, u32[]{:S(2)}) collective-permute-start(f32[32,128]{1,0:T(8,128)S(1)} %add_add_fusion), channel_id=1, source_target_pairs={{0,4},{1,5},{2,6},{3,7},{4,0},{5,1},{6,2},{7,3},{8,12},{9,13},{10,... | collective-permute-start | bytes 49160 | tf_op jit(solution)/shard_map/ppermute | solution.py:38
  111.0 2.2 %collective-permute-done.33 = f32[32,128]{1,0:T(8,128)S(1)} collective-permute-done((f32[32,128]{1,0:T(8,128)S(1)}, f32[32,128]{1,0:T(8,128)S(1)}, u32[]{:S(2)}, u32[]{:S(2)}) %collective-permute-start.33) | collective-permute-done | bytes 16416 | tf_op jit(solution)/shard_map/ppermute | solution.py:38
  113.2 0.6 add.42
  (36 shorter events, 0.5 us)
Async XLA Ops:
  0.0 73.5 %copy-start = (s32[1,24576]{1,0:T(1,128)S(1)}, s32[1,24576]{1,0:T(1,128)}, u32[]{:S(2)}) copy-start(s32[1,24576]{1,0:T(1,128)} %param.8) | copy-start | bytes 294916
  1.8 12.9 %collective-permute-start = (f32[16,3072]{1,0:T(8,128)S(1)}, f32[16,3072]{1,0:T(8,128)S(1)}, u32[]{:S(2)}, u32[]{:S(2)}) collective-permute-start(f32[16,3072]{1,0:T(8,128)S(1)} %get-tuple-element.44.refs_3_), channel_id=1, source_target_pairs={{0,8},{1,9},{2,10},{3,11},{4,12},{5,13},{6,14},{7,15},{8,16},{9,17... | collective-permute-start | bytes 589832 | tf_op jit(solution)/shard_map/ppermute | solution.py:38
  3.8 11.0 %collective-permute-start.1 = (f32[16,3072]{1,0:T(8,128)S(1)}, f32[16,3072]{1,0:T(8,128)S(1)}, u32[]{:S(2)}, u32[]{:S(2)}) collective-permute-start(f32[16,3072]{1,0:T(8,128)S(1)} %get-tuple-element.53), channel_id=1, source_target_pairs={{0,56},{1,57},{2,58},{3,59},{4,60},{5,61},{6,62},{7,63},{8,0},{9,1... | collective-permute-start | bytes 589832 | tf_op jit(solution)/shard_map/ppermute | solution.py:38
  8.5 11.8 %collective-permute-start.4 = (f32[4,2,8,1536]{3,2,1,0:T(8,128)S(1)}, f32[4,2,8,1536]{3,2,1,0:T(8,128)S(1)}, u32[]{:S(2)}, u32[]{:S(2)}) collective-permute-start(f32[4,2,8,1536]{3,2,1,0:T(8,128)S(1)} %get-tuple-element.45.refs_3_), channel_id=1, source_target_pairs={{0,1},{1,2},{2,3},{3,0},{4,5},{5,6},{6,7},{7,4},{8,9},{9,10},{10,1... | collective-permute-start | bytes 1179656 | tf_op jit(solution)/shard_map/ppermute | solution.py:38
  10.1 10.2 %collective-permute-start.5 = (f32[4,2,8,1536]{3,2,1,0:T(8,128)S(1)}, f32[4,2,8,1536]{3,2,1,0:T(8,128)S(1)}, u32[]{:S(2)}, u32[]{:S(2)}) collective-permute-start(f32[4,2,8,1536]{3,2,1,0:T(8,128)S(1)} %get-tuple-element.58), channel_id=1, source_target_pairs={{0,3},{1,0},{2,1},{3,2},{4,7},{5,4},{6,5},{7,6},{8,11},{9,8},{10,9... | collective-permute-start | bytes 1179656 | tf_op jit(solution)/shard_map/ppermute | solution.py:38
  14.8 75.0 %copy-start.1 = (s32[32]{0:T(128)S(1)}, s32[32]{0:T(128)}, u32[]{:S(2)}) copy-start(s32[32]{0:T(128)} %param.9) | copy-start | bytes 388
  14.9 12.5 %collective-permute-start.2 = (f32[32,3072]{1,0:T(8,128)S(1)}, f32[32,3072]{1,0:T(8,128)S(1)}, u32[]{:S(2)}, u32[]{:S(2)}) collective-permute-start(f32[32,3072]{1,0:T(8,128)S(1)} %get-tuple-element.54.refs_4_), channel_id=1, source_target_pairs={{0,8},{1,9},{2,10},{3,11},{4,12},{5,13},{6,14},{7,15},{8,16},{9,17... | collective-permute-start | bytes 1179656 | tf_op jit(solution)/shard_map/ppermute | solution.py:38
  16.9 11.1 %collective-permute-start.3 = (f32[32,3072]{1,0:T(8,128)S(1)}, f32[32,3072]{1,0:T(8,128)S(1)}, u32[]{:S(2)}, u32[]{:S(2)}) collective-permute-start(f32[32,3072]{1,0:T(8,128)S(1)} %get-tuple-element.55), channel_id=1, source_target_pairs={{0,56},{1,57},{2,58},{3,59},{4,60},{5,61},{6,62},{7,63},{8,0},{9,1... | collective-permute-start | bytes 1179656 | tf_op jit(solution)/shard_map/ppermute | solution.py:38
  20.5 22.6 %collective-permute-start.10 = (f32[8,2,8,1536]{3,2,1,0:T(8,128)S(1)}, f32[8,2,8,1536]{3,2,1,0:T(8,128)S(1)}, u32[]{:S(2)}, u32[]{:S(2)}) collective-permute-start(f32[8,2,8,1536]{3,2,1,0:T(8,128)S(1)} %get-tuple-element.59.refs_4_), channel_id=1, source_target_pairs={{0,1},{1,2},{2,3},{3,0},{4,5},{5,6},{6,7},{7,4},{8,9},{9,10},{10,1... | collective-permute-start | bytes 2359304 | tf_op jit(solution)/shard_map/ppermute | solution.py:38
  22.1 20.9 %collective-permute-start.11 = (f32[8,2,8,1536]{3,2,1,0:T(8,128)S(1)}, f32[8,2,8,1536]{3,2,1,0:T(8,128)S(1)}, u32[]{:S(2)}, u32[]{:S(2)}) collective-permute-start(f32[8,2,8,1536]{3,2,1,0:T(8,128)S(1)} %get-tuple-element.65), channel_id=1, source_target_pairs={{0,3},{1,0},{2,1},{3,2},{4,7},{5,4},{6,5},{7,6},{8,11},{9,8},{10,9... | collective-permute-start | bytes 2359304 | tf_op jit(solution)/shard_map/ppermute | solution.py:38
  28.2 9.9 %collective-permute-start.6 = (f32[32,3072]{1,0:T(8,128)S(1)}, f32[32,3072]{1,0:T(8,128)S(1)}, u32[]{:S(2)}, u32[]{:S(2)}) collective-permute-start(f32[32,3072]{1,0:T(8,128)S(1)} %get-tuple-element.60.refs_4_), channel_id=1, source_target_pairs={{0,8},{1,9},{2,10},{3,11},{4,12},{5,13},{6,14},{7,15},{8,16},{9,17... | collective-permute-start | bytes 1179656 | tf_op jit(solution)/shard_map/ppermute | solution.py:38
  31.2 9.6 %collective-permute-start.7 = (f32[32,3072]{1,0:T(8,128)S(1)}, f32[32,3072]{1,0:T(8,128)S(1)}, u32[]{:S(2)}, u32[]{:S(2)}) collective-permute-start(f32[32,3072]{1,0:T(8,128)S(1)} %get-tuple-element.61), channel_id=1, source_target_pairs={{0,56},{1,57},{2,58},{3,59},{4,60},{5,61},{6,62},{7,63},{8,0},{9,1... | collective-permute-start | bytes 1179656 | tf_op jit(solution)/shard_map/ppermute | solution.py:38
  40.9 12.5 %collective-permute-start.8 = (f32[32,3072]{1,0:T(8,128)S(1)}, f32[32,3072]{1,0:T(8,128)S(1)}, u32[]{:S(2)}, u32[]{:S(2)}) collective-permute-start(f32[32,3072]{1,0:T(8,128)S(1)} %get-tuple-element.62.refs_3_), channel_id=1, source_target_pairs={{0,8},{1,9},{2,10},{3,11},{4,12},{5,13},{6,14},{7,15},{8,16},{9,17... | collective-permute-start | bytes 1179656 | tf_op jit(solution)/shard_map/ppermute | solution.py:38
  42.7 10.7 %collective-permute-start.9 = (f32[32,3072]{1,0:T(8,128)S(1)}, f32[32,3072]{1,0:T(8,128)S(1)}, u32[]{:S(2)}, u32[]{:S(2)}) collective-permute-start(f32[32,3072]{1,0:T(8,128)S(1)} %get-tuple-element.63), channel_id=1, source_target_pairs={{0,56},{1,57},{2,58},{3,59},{4,60},{5,61},{6,62},{7,63},{8,0},{9,1... | collective-permute-start | bytes 1179656 | tf_op jit(solution)/shard_map/ppermute | solution.py:38
  43.2 6.8 %collective-permute-start.12 = (f32[1,8,1536]{2,1,0:T(8,128)S(1)}, f32[1,8,1536]{2,1,0:T(8,128)S(1)}, u32[]{:S(2)}, u32[]{:S(2)}) collective-permute-start(f32[1,8,1536]{2,1,0:T(8,128)S(1)} %get-tuple-element.68), channel_id=1, source_target_pairs={{0,8},{1,9},{2,10},{3,11},{4,12},{5,13},{6,14},{7,15},{8,16},{9,17... | collective-permute-start | bytes 147464 | tf_op jit(solution)/shard_map/ppermute | solution.py:38
  45.0 6.3 %collective-permute-start.13 = (f32[1,8,1536]{2,1,0:T(8,128)S(1)}, f32[1,8,1536]{2,1,0:T(8,128)S(1)}, u32[]{:S(2)}, u32[]{:S(2)}) collective-permute-start(f32[1,8,1536]{2,1,0:T(8,128)S(1)} %get-tuple-element.69), channel_id=1, source_target_pairs={{0,56},{1,57},{2,58},{3,59},{4,60},{5,61},{6,62},{7,63},{8,0},{9,1... | collective-permute-start | bytes 147464 | tf_op jit(solution)/shard_map/ppermute | solution.py:38
  51.3 5.7 %collective-permute-start.15 = (f32[2,8,1536]{2,1,0:T(8,128)S(1)}, f32[2,8,1536]{2,1,0:T(8,128)S(1)}, u32[]{:S(2)}, u32[]{:S(2)}) collective-permute-start(f32[2,8,1536]{2,1,0:T(8,128)S(1)} %get-tuple-element.70.refs_4_), channel_id=1, source_target_pairs={{0,8},{1,9},{2,10},{3,11},{4,12},{5,13},{6,14},{7,15},{8,16},{9,17... | collective-permute-start | bytes 294920 | tf_op jit(solution)/shard_map/ppermute | solution.py:38
  53.1 5.3 %collective-permute-start.16 = (f32[2,8,1536]{2,1,0:T(8,128)S(1)}, f32[2,8,1536]{2,1,0:T(8,128)S(1)}, u32[]{:S(2)}, u32[]{:S(2)}) collective-permute-start(f32[2,8,1536]{2,1,0:T(8,128)S(1)} %get-tuple-element.75), channel_id=1, source_target_pairs={{0,56},{1,57},{2,58},{3,59},{4,60},{5,61},{6,62},{7,63},{8,0},{9,1... | collective-permute-start | bytes 294920 | tf_op jit(solution)/shard_map/ppermute | solution.py:38
  53.5 13.6 %collective-permute-start.14 = (f32[16,3072]{1,0:T(8,128)S(1)}, f32[16,3072]{1,0:T(8,128)S(1)}, u32[]{:S(2)}, u32[]{:S(2)}) collective-permute-start(f32[16,3072]{1,0:T(8,128)S(1)} %get-tuple-element.72.refs_4_), channel_id=1, source_target_pairs={{0,4},{1,5},{2,6},{3,7},{4,0},{5,1},{6,2},{7,3},{8,12},{9,13},{10,... | collective-permute-start | bytes 589832 | tf_op jit(solution)/shard_map/ppermute | solution.py:38
  58.5 4.7 %collective-permute-start.20 = (f32[2,8,1536]{2,1,0:T(8,128)S(1)}, f32[2,8,1536]{2,1,0:T(8,128)S(1)}, u32[]{:S(2)}, u32[]{:S(2)}) collective-permute-start(f32[2,8,1536]{2,1,0:T(8,128)S(1)} %get-tuple-element.76.refs_2_), channel_id=1, source_target_pairs={{0,8},{1,9},{2,10},{3,11},{4,12},{5,13},{6,14},{7,15},{8,16},{9,17... | collective-permute-start | bytes 294920 | tf_op jit(solution)/shard_map/ppermute | solution.py:38
  60.3 4.6 %collective-permute-start.21 = (f32[2,8,1536]{2,1,0:T(8,128)S(1)}, f32[2,8,1536]{2,1,0:T(8,128)S(1)}, u32[]{:S(2)}, u32[]{:S(2)}) collective-permute-start(f32[2,8,1536]{2,1,0:T(8,128)S(1)} %get-tuple-element.80), channel_id=1, source_target_pairs={{0,56},{1,57},{2,58},{3,59},{4,60},{5,61},{6,62},{7,63},{8,0},{9,1... | collective-permute-start | bytes 294920 | tf_op jit(solution)/shard_map/ppermute | solution.py:38
  65.0 6.9 %collective-permute-start.22 = (f32[2,8,1536]{2,1,0:T(8,128)S(1)}, f32[2,8,1536]{2,1,0:T(8,128)S(1)}, u32[]{:S(2)}, u32[]{:S(2)}) collective-permute-start(f32[2,8,1536]{2,1,0:T(8,128)S(1)} %get-tuple-element.81), channel_id=1, source_target_pairs={{0,8},{1,9},{2,10},{3,11},{4,12},{5,13},{6,14},{7,15},{8,16},{9,17... | collective-permute-start | bytes 294920 | tf_op jit(solution)/shard_map/ppermute | solution.py:38
  66.6 5.3 %collective-permute-start.23 = (f32[2,8,1536]{2,1,0:T(8,128)S(1)}, f32[2,8,1536]{2,1,0:T(8,128)S(1)}, u32[]{:S(2)}, u32[]{:S(2)}) collective-permute-start(f32[2,8,1536]{2,1,0:T(8,128)S(1)} %get-tuple-element.82), channel_id=1, source_target_pairs={{0,56},{1,57},{2,58},{3,59},{4,60},{5,61},{6,62},{7,63},{8,0},{9,1... | collective-permute-start | bytes 294920 | tf_op jit(solution)/shard_map/ppermute | solution.py:38
  67.1 9.5 %collective-permute-start.17 = (f32[16,3072]{1,0:T(8,128)S(1)}, f32[16,3072]{1,0:T(8,128)S(1)}, u32[]{:S(2)}, u32[]{:S(2)}) collective-permute-start(f32[16,3072]{1,0:T(8,128)S(1)} %shard_map.75.own_ref), channel_id=1, source_target_pairs={{0,1},{1,0},{2,3},{3,2},{4,5},{5,4},{6,7},{7,6},{8,9},{9,8},{10,11... | collective-permute-start | bytes 589832 | tf_op jit(solution)/shard_map/ppermute | solution.py:38
  67.2 9.4 %collective-permute-start.18 = (f32[16,3072]{1,0:T(8,128)S(1)}, f32[16,3072]{1,0:T(8,128)S(1)}, u32[]{:S(2)}, u32[]{:S(2)}) collective-permute-start(f32[16,3072]{1,0:T(8,128)S(1)} %shard_map.75.own_ref), channel_id=1, source_target_pairs={{0,2},{1,3},{2,0},{3,1},{4,6},{5,7},{6,4},{7,5},{8,10},{9,11},{10,... | collective-permute-start | bytes 589832 | tf_op jit(solution)/shard_map/ppermute | solution.py:38
  70.4 7.9 %collective-permute-start.19 = (f32[16,3072]{1,0:T(8,128)S(1)}, f32[16,3072]{1,0:T(8,128)S(1)}, u32[]{:S(2)}, u32[]{:S(2)}) collective-permute-start(f32[16,3072]{1,0:T(8,128)S(1)} %shard_map.75.own_ref), channel_id=1, source_target_pairs={{0,3},{1,2},{2,1},{3,0},{4,7},{5,6},{6,5},{7,4},{8,11},{9,10},{10,... | collective-permute-start | bytes 589832 | tf_op jit(solution)/shard_map/ppermute | solution.py:38
  71.9 4.7 %collective-permute-start.24 = (f32[2,8,1536]{2,1,0:T(8,128)S(1)}, f32[2,8,1536]{2,1,0:T(8,128)S(1)}, u32[]{:S(2)}, u32[]{:S(2)}) collective-permute-start(f32[2,8,1536]{2,1,0:T(8,128)S(1)} %shard_map.77.right_ref), channel_id=1, source_target_pairs={{0,4},{1,5},{2,6},{3,7},{4,0},{5,1},{6,2},{7,3},{8,12},{9,13},{10,... | collective-permute-start | bytes 294920 | tf_op jit(solution)/shard_map/ppermute | solution.py:38
  78.9 3.8 %collective-permute-start.25 = (f32[32,128]{1,0:T(8,128)S(1)}, f32[32,128]{1,0:T(8,128)S(1)}, u32[]{:S(2)}, u32[]{:S(2)}) collective-permute-start(f32[32,128]{1,0:T(8,128)S(1)} %shard_map.78), channel_id=1, source_target_pairs={{0,8},{1,9},{2,10},{3,11},{4,12},{5,13},{6,14},{7,15},{8,0},{9,1},... | collective-permute-start | bytes 49160 | tf_op jit(solution)/shard_map/ppermute | solution.py:38
  82.7 4.7 %collective-permute-start.26 = (f32[32,128]{1,0:T(8,128)S(1)}, f32[32,128]{1,0:T(8,128)S(1)}, u32[]{:S(2)}, u32[]{:S(2)}) collective-permute-start(f32[32,128]{1,0:T(8,128)S(1)} %add.36), channel_id=1, source_target_pairs={{0,16},{1,17},{2,18},{3,19},{4,20},{5,21},{6,22},{7,23},{8,24},{9,... | collective-permute-start | bytes 49160 | tf_op jit(solution)/shard_map/ppermute | solution.py:38
  87.5 6.7 %collective-permute-start.27 = (f32[32,128]{1,0:T(8,128)S(1)}, f32[32,128]{1,0:T(8,128)S(1)}, u32[]{:S(2)}, u32[]{:S(2)}) collective-permute-start(f32[32,128]{1,0:T(8,128)S(1)} %add.37), channel_id=1, source_target_pairs={{0,56},{1,57},{2,58},{3,59},{4,60},{5,61},{6,62},{7,63},{8,48},{9,... | collective-permute-start | bytes 49160 | tf_op jit(solution)/shard_map/ppermute | solution.py:38
  94.3 1.2 %collective-permute-start.28 = (f32[1,32,128]{2,1,0:T(8,128)S(1)}, f32[1,32,128]{2,1,0:T(8,128)S(1)}, u32[]{:S(2)}, u32[]{:S(2)}) collective-permute-start(f32[1,32,128]{2,1,0:T(8,128)S(1)} %multiply_bitcast_fusion), channel_id=1, source_target_pairs={{0,64},{64,0},{128,192},{192,128},{1,65},{65,1},{129,193},{193,129... | collective-permute-start | bytes 49160 | tf_op jit(solution)/shard_map/ppermute | solution.py:254
  95.5 5.7 %collective-permute-start.29 = (f32[2,32,128]{2,1,0:T(8,128)S(1)}, f32[2,32,128]{2,1,0:T(8,128)S(1)}, u32[]{:S(2)}, u32[]{:S(2)}) collective-permute-start(f32[2,32,128]{2,1,0:T(8,128)S(1)} %pad_maximum_fusion.1), channel_id=1, source_target_pairs={{0,128},{64,192},{128,0},{192,64},{1,129},{65,193},{129,1},{193,65... | collective-permute-start | bytes 98312 | tf_op jit(solution)/shard_map/ppermute | solution.py:254
  101.5 4.8 %collective-permute-start.30 = (f32[32,128]{1,0:T(8,128)S(1)}, f32[32,128]{1,0:T(8,128)S(1)}, u32[]{:S(2)}, u32[]{:S(2)}) collective-permute-start(f32[32,128]{1,0:T(8,128)S(1)} %fusion), channel_id=1, source_target_pairs={{0,1},{1,0},{2,3},{3,2},{4,5},{5,4},{6,7},{7,6},{8,9},{9,8},{10,11... | collective-permute-start | bytes 49160 | tf_op jit(solution)/shard_map/ppermute | solution.py:38
  101.6 5.4 %collective-permute-start.31 = (f32[32,128]{1,0:T(8,128)S(1)}, f32[32,128]{1,0:T(8,128)S(1)}, u32[]{:S(2)}, u32[]{:S(2)}) collective-permute-start(f32[32,128]{1,0:T(8,128)S(1)} %fusion), channel_id=1, source_target_pairs={{0,2},{1,3},{2,0},{3,1},{4,6},{5,7},{6,4},{7,5},{8,10},{9,11},{10,... | collective-permute-start | bytes 49160 | tf_op jit(solution)/shard_map/ppermute | solution.py:38
  104.4 4.9 %collective-permute-start.32 = (f32[32,128]{1,0:T(8,128)S(1)}, f32[32,128]{1,0:T(8,128)S(1)}, u32[]{:S(2)}, u32[]{:S(2)}) collective-permute-start(f32[32,128]{1,0:T(8,128)S(1)} %fusion), channel_id=1, source_target_pairs={{0,3},{1,2},{2,1},{3,0},{4,7},{5,6},{6,5},{7,4},{8,11},{9,10},{10,... | collective-permute-start | bytes 49160 | tf_op jit(solution)/shard_map/ppermute | solution.py:38
  109.4 3.8 %collective-permute-start.33 = (f32[32,128]{1,0:T(8,128)S(1)}, f32[32,128]{1,0:T(8,128)S(1)}, u32[]{:S(2)}, u32[]{:S(2)}) collective-permute-start(f32[32,128]{1,0:T(8,128)S(1)} %add_add_fusion), channel_id=1, source_target_pairs={{0,4},{1,5},{2,6},{3,7},{4,0},{5,1},{6,2},{7,3},{8,12},{9,13},{10,... | collective-permute-start | bytes 49160 | tf_op jit(solution)/shard_map/ppermute | solution.py:38

commit v5 on v4

--- a/solution.py
+++ b/solution.py
@@ -159,21 +159,16 @@
 
 
 def right_chunks_kernel(own_ref, rising_ref, falling_ref, *refs):
-    for step in ALL:
-        total = own_ref[step] + rising_ref[step] + falling_ref[step]
-        if step == FAR[0]:
-            refs[-2][...] = total[:1]
-            refs[-1][...] = total[1:]
-        else:
-            refs[REST.index(step)][...] = total
+    for step, out_ref in enumerate(refs):
+        out_ref[...] = own_ref[step] + rising_ref[step] + falling_ref[step]
 
 
 def right_sum_kernel(own_ref, rising_ref, falling_ref, out_ref):
     out_ref[...] = own_ref[...] + rising_ref[...] + falling_ref[...]
 
 
-def feature_kernel(own_ref, near_ref, opposite_ref, last_ref, right_ref, moved_ref, ids_ref, out_ref):
-    left = (own_ref[...] + near_ref[...]) + (opposite_ref[...] + last_ref[...])
+def feature_kernel(own_ref, other_ref, right_ref, moved_ref, ids_ref, out_ref):
+    left = own_ref[...] + other_ref[...]
     labels = lax.broadcasted_iota(jnp.int32, (EX_GRP, HALF), 0)
     over = (((1,), (1,)), ((), ()))
     total = jnp.zeros((EX_GRP, LEFT * RIGHT), jnp.float32)
@@ -216,34 +211,33 @@
     left_moved = both_ways(*sent, "z")
     sent = step_add(left[4], left[5], left_moved, sent[:1])
     left_moved = both_ways(*sent, "z")
-    *right, rising, falling = local(
-        right_chunks_kernel, (), [right[0], *right_moved],
-        [chunk] * 7 + [(1, RIGHT, HALF)] * 2, after=sent[:1],
-    )
-    right_moved = both_ways(rising, falling, "z")
-    sent = step_add(right[0], right[1], right_moved, [], half=True)
+    right = local(right_chunks_kernel, (), [right[0], *right_moved], [chunk] * Z, after=sent[:1])
+    right_moved = both_ways(right[4], right[5], "z")
+    sent = step_add(right[3], right[6], right_moved, [])
     right_moved = both_ways(*sent, "z")
     keep, give = local(
         left_half_kernel, (at["x"],), [left[6], *left_moved], [half] * 2, [(2, *half)], after=sent[:1]
     )
     left_moved = mixed(give, "x", 1)
-    sent = step_add(right[2], right[3], right_moved, [give])
+    sent = step_add(right[2], right[7], right_moved, [give])
     right_moved = both_ways(*sent, "z")
     (left,) = local(add_kernel, (), [keep, left_moved], [half], after=sent[:1])
-    sent = step_add(right[4], right[5], right_moved, [])
-    right_moved = both_ways(*sent, "z")
-    lefts = [left] + [mixed(left, "y", bits) for bits in range(1, Y)]
-    (right,) = local(right_sum_kernel, (), [right[6], *right_moved], [chunk])
+    left_moved = mixed(left, "y", 1)
+    (rising,) = local(add_kernel, (), [right[1], right_moved[0]], [chunk], after=[left])
+    right_moved = [send(rising, "z", lambda at: at + 1), right_moved[1]]
+    (left,) = local(add_kernel, (), [left, left_moved], [half], after=[rising])
+    left_moved = mixed(left, "y", 3)
+    (right,) = local(right_sum_kernel, (), [right[0], *right_moved], [chunk], after=[left])
     right_moved = mixed(right, "x", 1)
 
     ids = lax.dynamic_slice(example_ids, (0, at["z"] * WIDE), (1, WIDE))
     features = pl.pallas_call(
         feature_kernel,
-        in_specs=[VMEM] * 7,
+        in_specs=[VMEM] * 5,
         out_specs=VMEM,
         out_shape=jax.ShapeDtypeStruct((EX_GRP, LEFT * RIGHT), jnp.float32),
         compiler_params=pltpu.CompilerParams(vmem_limit_bytes=12 * MIB),
-    )(*lefts, right, right_moved, ids)
+    )(left, left_moved, right, right_moved, ids)
     for bits in (1, 2, 7):
         features = features + mixed(features, "z", bits)
 

time: 114 us -> 112 us (0.982)
  starting transfers between devices: 50.3 us -> 46.2 us
  waiting for transfers between devices: 51.6 us -> 53.6 us
    ppermute x32 -> x30, starting transfers between devices: 46.9 us -> 43.4 us  [send(): return lax.ppermute(value, 'par', pairs)]
    ppermute x32 -> x30, waiting for transfers between devices: 48.1 us -> 49.7 us  [send(): return lax.ppermute(value, 'par', pairs)]
  transfers between devices with their start and end apart: 34 -> 32, of which waited for: 21 -> 20; matrix products, arithmetic and copies ran while one was open for 0% -> 0% of each run, Pallas kernels for 7% -> 7%
where the time goes in v5:
time: 112 us
  waiting for transfers between devices  53.6 us (48%)
  starting transfers between devices  46.2 us (41%)
  Pallas kernels  10.7 us (10%)
    ppermute x30, waiting for transfers between devices, send(): return lax.ppermute(value, 'par', pairs)  49.7 us
    ppermute x30, starting transfers between devices, send(): return lax.ppermute(value, 'par', pairs)  43.4 us
    pallas_call x3, Pallas kernels, projected(): pl.pallas_call(ordered(kernel, 3, after), in_specs=[SMEM, *[pl.BlockSpec(...  9.26 us
    ppermute x2, waiting for transfers between devices, on_device(): other = lax.ppermute(cols, 'grp', [(i, i ^ bit) for i in range(4)])  3.86 us
    ppermute x2, starting transfers between devices, on_device(): other = lax.ppermute(cols, 'grp', [(i, i ^ bit) for i in range(4)])  2.84 us
  transfers between devices with their start and end apart: 32, of which 20 were waited for; matrix products, arithmetic and copies ran while one was open for 0% of the time, Pallas kernels for 7%

profile of v5, /device:TPU:32, one launch (start us, length us, event | category | flops | bytes accessed | tf_op | source)
XLA Modules:
  0.0 111.8 jit_solution(8965134792311684226)
XLA Ops:
  0.0 0.1 pad_add_fusion.refs_0_
  0.1 1.8 %shard_map.64 = (f32[16,3072]{1,0:T(8,128)S(1)}, f32[16,3072]{1,0:T(8,128)S(1)}) custom-call(s32[2]{0:T(128)S(1)} %pad_add_fusion.refs_0_, bf16[32,64]{1,0:T(8,128)(2,1)} %bitcast.10, bf16[64,24576]{1,0:T(8,128)(2,1)} %refs_2_.5), custom_call_target="tpu_custom_call" | custom-call | tf_op jit(solution)/shard_map/pallas_call | solution.py:117
  1.8 2.0 %collective-permute-start = (f32[16,3072]{1,0:T(8,128)S(1)}, f32[16,3072]{1,0:T(8,128)S(1)}, u32[]{:S(2)}, u32[]{:S(2)}) collective-permute-start(f32[16,3072]{1,0:T(8,128)S(1)} %get-tuple-element.41.refs_3_), channel_id=1, source_target_pairs={{0,8},{1,9},{2,10},{3,11},{4,12},{5,13},{6,14},{7,15},{8,16},{9,17... | collective-permute-start | bytes 589832 | tf_op jit(solution)/shard_map/ppermute | solution.py:38
  3.8 0.1 collective-permute-start.1
  4.0 4.5 %shard_map.65 = (f32[8,2,8,1536]{3,2,1,0:T(8,128)S(1)}, f32[8,2,8,1536]{3,2,1,0:T(8,128)S(1)}, f32[8,2,8,1536]{3,2,1,0:T(8,128)S(1)}, f32[4,2,8,1536]{3,2,1,0:T(8,128)S(1)}, f32[4,2,8,1536]{3,2,1,0:T(8,128)S(1)}) custom-call(s32[2]{0:T(128)S(1)} %pad_add_fusion.refs_0_, bf16[32,172]{1,0:T(8,128)(2,1)} %bitcast.12, bf16[172,24576]{1,0:T(8,128)(2,1)} %refs_2_.4, ...), custom_call_target="tpu_custom_call" | custom-call | tf_op jit(solution)/shard_map/pallas_call | solution.py:117
  8.5 1.6 %collective-permute-start.4 = (f32[4,2,8,1536]{3,2,1,0:T(8,128)S(1)}, f32[4,2,8,1536]{3,2,1,0:T(8,128)S(1)}, u32[]{:S(2)}, u32[]{:S(2)}) collective-permute-start(f32[4,2,8,1536]{3,2,1,0:T(8,128)S(1)} %get-tuple-element.42.refs_3_), channel_id=1, source_target_pairs={{0,1},{1,2},{2,3},{3,0},{4,5},{5,6},{6,7},{7,4},{8,9},{9,10},{10,1... | collective-permute-start | bytes 1179656 | tf_op jit(solution)/shard_map/ppermute | solution.py:38
  10.1 1.7 %collective-permute-start.5 = (f32[4,2,8,1536]{3,2,1,0:T(8,128)S(1)}, f32[4,2,8,1536]{3,2,1,0:T(8,128)S(1)}, u32[]{:S(2)}, u32[]{:S(2)}) collective-permute-start(f32[4,2,8,1536]{3,2,1,0:T(8,128)S(1)} %get-tuple-element.55), channel_id=1, source_target_pairs={{0,3},{1,0},{2,1},{3,2},{4,7},{5,4},{6,5},{7,6},{8,11},{9,8},{10,9... | collective-permute-start | bytes 1179656 | tf_op jit(solution)/shard_map/ppermute | solution.py:38
  11.8 3.0 %shard_map.66 = (f32[32,3072]{1,0:T(8,128)S(1)}, f32[32,3072]{1,0:T(8,128)S(1)}, f32[32,3072]{1,0:T(8,128)S(1)}, f32[32,3072]{1,0:T(8,128)S(1)}, f32[32,3072]{1,...) custom-call(s32[2]{0:T(128)S(1)} %pad_add_fusion.refs_0_, bf16[32,64]{1,0:T(8,128)(2,1)} %bitcast.11, ...), custom_call_target="tpu_custom_call" | custom-call | tf_op jit(solution)/shard_map/pallas_call | solution.py:117
  14.8 0.1 shard_map.67
  14.9 2.0 %collective-permute-start.2 = (f32[32,3072]{1,0:T(8,128)S(1)}, f32[32,3072]{1,0:T(8,128)S(1)}, u32[]{:S(2)}, u32[]{:S(2)}) collective-permute-start(f32[32,3072]{1,0:T(8,128)S(1)} %get-tuple-element.51.refs_4_), channel_id=1, source_target_pairs={{0,8},{1,9},{2,10},{3,11},{4,12},{5,13},{6,14},{7,15},{8,16},{9,17... | collective-permute-start | bytes 1179656 | tf_op jit(solution)/shard_map/ppermute | solution.py:38
  16.9 2.2 %collective-permute-start.3 = (f32[32,3072]{1,0:T(8,128)S(1)}, f32[32,3072]{1,0:T(8,128)S(1)}, u32[]{:S(2)}, u32[]{:S(2)}) collective-permute-start(f32[32,3072]{1,0:T(8,128)S(1)} %get-tuple-element.52), channel_id=1, source_target_pairs={{0,56},{1,57},{2,58},{3,59},{4,60},{5,61},{6,62},{7,63},{8,0},{9,1... | collective-permute-start | bytes 1179656 | tf_op jit(solution)/shard_map/ppermute | solution.py:38
  19.1 1.2 %collective-permute-done.4.refs_2_ = f32[4,2,8,1536]{3,2,1,0:T(8,128)S(1)} collective-permute-done((f32[4,2,8,1536]{3,2,1,0:T(8,128)S(1)}, f32[4,2,8,1536]{3,2,1,0:T(8,128)S(1)}, u32[]{:S(2)}, u32[]{:S(2)}) %collective-permute-start.4) | collective-permute-done | bytes 393248 | tf_op jit(solution)/shard_map/ppermute | solution.py:38
  20.3 0.1 shard_map.68
  20.5 1.7 %collective-permute-start.10 = (f32[8,2,8,1536]{3,2,1,0:T(8,128)S(1)}, f32[8,2,8,1536]{3,2,1,0:T(8,128)S(1)}, u32[]{:S(2)}, u32[]{:S(2)}) collective-permute-start(f32[8,2,8,1536]{3,2,1,0:T(8,128)S(1)} %get-tuple-element.56.refs_4_), channel_id=1, source_target_pairs={{0,1},{1,2},{2,3},{3,0},{4,5},{5,6},{6,7},{7,4},{8,9},{9,10},{10,1... | collective-permute-start | bytes 2359304 | tf_op jit(solution)/shard_map/ppermute | solution.py:38
  22.1 1.6 %collective-permute-start.11 = (f32[8,2,8,1536]{3,2,1,0:T(8,128)S(1)}, f32[8,2,8,1536]{3,2,1,0:T(8,128)S(1)}, u32[]{:S(2)}, u32[]{:S(2)}) collective-permute-start(f32[8,2,8,1536]{3,2,1,0:T(8,128)S(1)} %get-tuple-element.62), channel_id=1, source_target_pairs={{0,3},{1,0},{2,1},{3,2},{4,7},{5,4},{6,5},{7,6},{8,11},{9,8},{10,9... | collective-permute-start | bytes 2359304 | tf_op jit(solution)/shard_map/ppermute | solution.py:38
  23.8 3.6 %collective-permute-done.2.refs_2_ = f32[32,3072]{1,0:T(8,128)S(1)} collective-permute-done((f32[32,3072]{1,0:T(8,128)S(1)}, f32[32,3072]{1,0:T(8,128)S(1)}, u32[]{:S(2)}, u32[]{:S(2)}) %collective-permute-start.2) | collective-permute-done | bytes 393248 | tf_op jit(solution)/shard_map/ppermute | solution.py:38
  27.4 0.6 collective-permute-done.3.refs_3_
  28.0 0.1 shard_map.69
  28.2 3.0 %collective-permute-start.6 = (f32[32,3072]{1,0:T(8,128)S(1)}, f32[32,3072]{1,0:T(8,128)S(1)}, u32[]{:S(2)}, u32[]{:S(2)}) collective-permute-start(f32[32,3072]{1,0:T(8,128)S(1)} %get-tuple-element.57.refs_4_), channel_id=1, source_target_pairs={{0,8},{1,9},{2,10},{3,11},{4,12},{5,13},{6,14},{7,15},{8,16},{9,17... | collective-permute-start | bytes 1179656 | tf_op jit(solution)/shard_map/ppermute | solution.py:38
  31.2 6.9 %collective-permute-done.6.refs_2_ = f32[32,3072]{1,0:T(8,128)S(1)} collective-permute-done((f32[32,3072]{1,0:T(8,128)S(1)}, f32[32,3072]{1,0:T(8,128)S(1)}, u32[]{:S(2)}, u32[]{:S(2)}) %collective-permute-start.6) | collective-permute-done | bytes 393248 | tf_op jit(solution)/shard_map/ppermute | solution.py:38
  38.1 2.7 %collective-permute-done.7.refs_3_ = f32[32,3072]{1,0:T(8,128)S(1)} collective-permute-done((f32[32,3072]{1,0:T(8,128)S(1)}, f32[32,3072]{1,0:T(8,128)S(1)}, u32[]{:S(2)}, u32[]{:S(2)}) %collective-permute-start.7) | collective-permute-done | bytes 393248 | tf_op jit(solution)/shard_map/ppermute | solution.py:38
  40.8 0.1 shard_map.70
  40.9 1.8 %collective-permute-start.8 = (f32[32,3072]{1,0:T(8,128)S(1)}, f32[32,3072]{1,0:T(8,128)S(1)}, u32[]{:S(2)}, u32[]{:S(2)}) collective-permute-start(f32[32,3072]{1,0:T(8,128)S(1)} %get-tuple-element.59.refs_3_), channel_id=1, source_target_pairs={{0,8},{1,9},{2,10},{3,11},{4,12},{5,13},{6,14},{7,15},{8,16},{9,17... | collective-permute-start | bytes 1179656 | tf_op jit(solution)/shard_map/ppermute | solution.py:38
  42.7 0.3 collective-permute-start.9
  43.0 0.1 shard_map.71
  43.2 1.8 %collective-permute-start.12 = (f32[2,8,1536]{2,1,0:T(8,128)S(1)}, f32[2,8,1536]{2,1,0:T(8,128)S(1)}, u32[]{:S(2)}, u32[]{:S(2)}) collective-permute-start(f32[2,8,1536]{2,1,0:T(8,128)S(1)} %get-tuple-element.65), channel_id=1, source_target_pairs={{0,8},{1,9},{2,10},{3,11},{4,12},{5,13},{6,14},{7,15},{8,16},{9,17... | collective-permute-start | bytes 294920 | tf_op jit(solution)/shard_map/ppermute | solution.py:38
  45.0 0.3 collective-permute-start.13
  45.3 5.6 %collective-permute-done.12.refs_2_ = f32[2,8,1536]{2,1,0:T(8,128)S(1)} collective-permute-done((f32[2,8,1536]{2,1,0:T(8,128)S(1)}, f32[2,8,1536]{2,1,0:T(8,128)S(1)}, u32[]{:S(2)}, u32[]{:S(2)}) %collective-permute-start.12) | collective-permute-done | bytes 98336 | tf_op jit(solution)/shard_map/ppermute | solution.py:38
  50.8 1.5 %collective-permute-done.13.refs_3_ = f32[2,8,1536]{2,1,0:T(8,128)S(1)} collective-permute-done((f32[2,8,1536]{2,1,0:T(8,128)S(1)}, f32[2,8,1536]{2,1,0:T(8,128)S(1)}, u32[]{:S(2)}, u32[]{:S(2)}) %collective-permute-start.13) | collective-permute-done | bytes 98336 | tf_op jit(solution)/shard_map/ppermute | solution.py:38
  52.4 0.1 shard_map.73
  52.5 1.6 %collective-permute-start.14 = (f32[16,3072]{1,0:T(8,128)S(1)}, f32[16,3072]{1,0:T(8,128)S(1)}, u32[]{:S(2)}, u32[]{:S(2)}) collective-permute-start(f32[16,3072]{1,0:T(8,128)S(1)} %get-tuple-element.69.refs_4_), channel_id=1, source_target_pairs={{0,4},{1,5},{2,6},{3,7},{4,0},{5,1},{6,2},{7,3},{8,12},{9,13},{10,... | collective-permute-start | bytes 589832 | tf_op jit(solution)/shard_map/ppermute | solution.py:38
  54.1 1.7 %collective-permute-start.15 = (f32[2,8,1536]{2,1,0:T(8,128)S(1)}, f32[2,8,1536]{2,1,0:T(8,128)S(1)}, u32[]{:S(2)}, u32[]{:S(2)}) collective-permute-start(f32[2,8,1536]{2,1,0:T(8,128)S(1)} %get-tuple-element.67.refs_4_), channel_id=1, source_target_pairs={{0,8},{1,9},{2,10},{3,11},{4,12},{5,13},{6,14},{7,15},{8,16},{9,17... | collective-permute-start | bytes 294920 | tf_op jit(solution)/shard_map/ppermute | solution.py:38
  55.8 0.3 collective-permute-start.16
  56.1 3.4 %collective-permute-done.15.refs_2_ = f32[2,8,1536]{2,1,0:T(8,128)S(1)} collective-permute-done((f32[2,8,1536]{2,1,0:T(8,128)S(1)}, f32[2,8,1536]{2,1,0:T(8,128)S(1)}, u32[]{:S(2)}, u32[]{:S(2)}) %collective-permute-start.15) | collective-permute-done | bytes 98336 | tf_op jit(solution)/shard_map/ppermute | solution.py:38
  59.5 1.5 %collective-permute-done.16.refs_3_ = f32[2,8,1536]{2,1,0:T(8,128)S(1)} collective-permute-done((f32[2,8,1536]{2,1,0:T(8,128)S(1)}, f32[2,8,1536]{2,1,0:T(8,128)S(1)}, u32[]{:S(2)}, u32[]{:S(2)}) %collective-permute-start.16) | collective-permute-done | bytes 98336 | tf_op jit(solution)/shard_map/ppermute | solution.py:38
  61.1 0.1 collective-permute-start.17
  61.2 1.8 %collective-permute-start.18 = (f32[2,8,1536]{2,1,0:T(8,128)S(1)}, f32[2,8,1536]{2,1,0:T(8,128)S(1)}, u32[]{:S(2)}, u32[]{:S(2)}) collective-permute-start(f32[2,8,1536]{2,1,0:T(8,128)S(1)} %get-tuple-element.73.refs_2_), channel_id=1, source_target_pairs={{0,8},{1,9},{2,10},{3,11},{4,12},{5,13},{6,14},{7,15},{8,16},{9,17... | collective-permute-start | bytes 294920 | tf_op jit(solution)/shard_map/ppermute | solution.py:38
  63.0 0.3 collective-permute-start.21
  63.3 2.6 %collective-permute-done.18.refs_1_ = f32[2,8,1536]{2,1,0:T(8,128)S(1)} collective-permute-done((f32[2,8,1536]{2,1,0:T(8,128)S(1)}, f32[2,8,1536]{2,1,0:T(8,128)S(1)}, u32[]{:S(2)}, u32[]{:S(2)}) %collective-permute-start.18) | collective-permute-done | bytes 98336 | tf_op jit(solution)/shard_map/ppermute | solution.py:38
  65.9 1.8 %collective-permute-start.20 = (f32[2,8,1536]{2,1,0:T(8,128)S(1)}, f32[2,8,1536]{2,1,0:T(8,128)S(1)}, u32[]{:S(2)}, u32[]{:S(2)}) collective-permute-start(f32[2,8,1536]{2,1,0:T(8,128)S(1)} %shard_map.76.refs_2_), channel_id=1, source_target_pairs={{0,8},{1,9},{2,10},{3,11},{4,12},{5,13},{6,14},{7,15},{8,16},{9,17... | collective-permute-start | bytes 294920 | tf_op jit(solution)/shard_map/ppermute | solution.py:38
  67.8 2.1 %collective-permute-start.19 = (f32[16,3072]{1,0:T(8,128)S(1)}, f32[16,3072]{1,0:T(8,128)S(1)}, u32[]{:S(2)}, u32[]{:S(2)}) collective-permute-start(f32[16,3072]{1,0:T(8,128)S(1)} %shard_map.77.refs_3_.own_ref), channel_id=1, source_target_pairs={{0,3},{1,2},{2,1},{3,0},{4,7},{5,6},{6,5},{7,4},{8,11},{9,10},{10,... | collective-permute-start | bytes 589832 | tf_op jit(solution)/shard_map/ppermute | solution.py:38
  69.8 0.8 collective-permute-done.20.refs_1_
  70.6 0.6 collective-permute-start.22
  71.2 4.1 %collective-permute-done.22.moved_ref = f32[2,8,1536]{2,1,0:T(8,128)S(1)} collective-permute-done((f32[2,8,1536]{2,1,0:T(8,128)S(1)}, f32[2,8,1536]{2,1,0:T(8,128)S(1)}, u32[]{:S(2)}, u32[]{:S(2)}) %collective-permute-start.22) | collective-permute-done | bytes 98336 | tf_op jit(solution)/shard_map/ppermute | solution.py:38
  75.3 0.6 shard_map.79
  75.9 2.9 %collective-permute-start.23 = (f32[32,128]{1,0:T(8,128)S(1)}, f32[32,128]{1,0:T(8,128)S(1)}, u32[]{:S(2)}, u32[]{:S(2)}) collective-permute-start(f32[32,128]{1,0:T(8,128)S(1)} %shard_map.79), channel_id=1, source_target_pairs={{0,8},{1,9},{2,10},{3,11},{4,12},{5,13},{6,14},{7,15},{8,0},{9,1},... | collective-permute-start | bytes 49160 | tf_op jit(solution)/shard_map/ppermute | solution.py:38
  78.9 1.7 %collective-permute-done.23 = f32[32,128]{1,0:T(8,128)S(1)} collective-permute-done((f32[32,128]{1,0:T(8,128)S(1)}, f32[32,128]{1,0:T(8,128)S(1)}, u32[]{:S(2)}, u32[]{:S(2)}) %collective-permute-start.23) | collective-permute-done | bytes 16416 | tf_op jit(solution)/shard_map/ppermute | solution.py:38
  80.6 2.1 %collective-permute-start.24 = (f32[32,128]{1,0:T(8,128)S(1)}, f32[32,128]{1,0:T(8,128)S(1)}, u32[]{:S(2)}, u32[]{:S(2)}) collective-permute-start(f32[32,128]{1,0:T(8,128)S(1)} %add.36), channel_id=1, source_target_pairs={{0,16},{1,17},{2,18},{3,19},{4,20},{5,21},{6,22},{7,23},{8,24},{9,... | collective-permute-start | bytes 49160 | tf_op jit(solution)/shard_map/ppermute | solution.py:38
  82.7 2.5 %collective-permute-done.24 = f32[32,128]{1,0:T(8,128)S(1)} collective-permute-done((f32[32,128]{1,0:T(8,128)S(1)}, f32[32,128]{1,0:T(8,128)S(1)}, u32[]{:S(2)}, u32[]{:S(2)}) %collective-permute-start.24) | collective-permute-done | bytes 16416 | tf_op jit(solution)/shard_map/ppermute | solution.py:38
  85.2 2.5 %collective-permute-start.25 = (f32[32,128]{1,0:T(8,128)S(1)}, f32[32,128]{1,0:T(8,128)S(1)}, u32[]{:S(2)}, u32[]{:S(2)}) collective-permute-start(f32[32,128]{1,0:T(8,128)S(1)} %add.37), channel_id=1, source_target_pairs={{0,56},{1,57},{2,58},{3,59},{4,60},{5,61},{6,62},{7,63},{8,48},{9,... | collective-permute-start | bytes 49160 | tf_op jit(solution)/shard_map/ppermute | solution.py:38
  87.7 4.2 %collective-permute-done.25 = f32[32,128]{1,0:T(8,128)S(1)} collective-permute-done((f32[32,128]{1,0:T(8,128)S(1)}, f32[32,128]{1,0:T(8,128)S(1)}, u32[]{:S(2)}, u32[]{:S(2)}) %collective-permute-start.25) | collective-permute-done | bytes 16416 | tf_op jit(solution)/shard_map/ppermute | solution.py:38
  92.0 0.1 multiply_bitcast_fusion
  92.1 1.2 %collective-permute-done.26 = f32[1,32,128]{2,1,0:T(8,128)S(1)} collective-permute-done((f32[1,32,128]{2,1,0:T(8,128)S(1)}, f32[1,32,128]{2,1,0:T(8,128)S(1)}, u32[]{:S(2)}, u32[]{:S(2)}) %collective-permute-start.26) | collective-permute-done | bytes 16416 | tf_op jit(solution)/shard_map/ppermute | solution.py:248
  93.3 2.8 %collective-permute-start.27 = (f32[2,32,128]{2,1,0:T(8,128)S(1)}, f32[2,32,128]{2,1,0:T(8,128)S(1)}, u32[]{:S(2)}, u32[]{:S(2)}) collective-permute-start(f32[2,32,128]{2,1,0:T(8,128)S(1)} %pad_maximum_fusion.1), channel_id=1, source_target_pairs={{0,128},{64,192},{128,0},{192,64},{1,129},{65,193},{129,1},{193,65... | collective-permute-start | bytes 98312 | tf_op jit(solution)/shard_map/ppermute | solution.py:248
  96.1 2.7 %collective-permute-done.27 = f32[2,32,128]{2,1,0:T(8,128)S(1)} collective-permute-done((f32[2,32,128]{2,1,0:T(8,128)S(1)}, f32[2,32,128]{2,1,0:T(8,128)S(1)}, u32[]{:S(2)}, u32[]{:S(2)}) %collective-permute-start.27) | collective-permute-done | bytes 32800 | tf_op jit(solution)/shard_map/ppermute | solution.py:248
  98.8 0.2 fusion
  99.0 2.0 %collective-permute-start.28 = (f32[32,128]{1,0:T(8,128)S(1)}, f32[32,128]{1,0:T(8,128)S(1)}, u32[]{:S(2)}, u32[]{:S(2)}) collective-permute-start(f32[32,128]{1,0:T(8,128)S(1)} %fusion), channel_id=1, source_target_pairs={{0,1},{1,0},{2,3},{3,2},{4,5},{5,4},{6,7},{7,6},{8,9},{9,8},{10,11... | collective-permute-start | bytes 49160 | tf_op jit(solution)/shard_map/ppermute | solution.py:38
  101.0 1.4 %collective-permute-start.29 = (f32[32,128]{1,0:T(8,128)S(1)}, f32[32,128]{1,0:T(8,128)S(1)}, u32[]{:S(2)}, u32[]{:S(2)}) collective-permute-start(f32[32,128]{1,0:T(8,128)S(1)} %fusion), channel_id=1, source_target_pairs={{0,2},{1,3},{2,0},{3,1},{4,6},{5,7},{6,4},{7,5},{8,10},{9,11},{10,... | collective-permute-start | bytes 49160 | tf_op jit(solution)/shard_map/ppermute | solution.py:38
  102.4 1.4 %collective-permute-start.30 = (f32[32,128]{1,0:T(8,128)S(1)}, f32[32,128]{1,0:T(8,128)S(1)}, u32[]{:S(2)}, u32[]{:S(2)}) collective-permute-start(f32[32,128]{1,0:T(8,128)S(1)} %fusion), channel_id=1, source_target_pairs={{0,3},{1,2},{2,1},{3,0},{4,7},{5,6},{6,5},{7,4},{8,11},{9,10},{10,... | collective-permute-start | bytes 49160 | tf_op jit(solution)/shard_map/ppermute | solution.py:38
  103.8 2.4 %collective-permute-done.29 = f32[32,128]{1,0:T(8,128)S(1)} collective-permute-done((f32[32,128]{1,0:T(8,128)S(1)}, f32[32,128]{1,0:T(8,128)S(1)}, u32[]{:S(2)}, u32[]{:S(2)}) %collective-permute-start.29) | collective-permute-done | bytes 16416 | tf_op jit(solution)/shard_map/ppermute | solution.py:38
  106.3 1.1 collective-permute-done.30
  107.4 0.6 collective-permute-start.31
  108.0 3.2 %collective-permute-done.31 = f32[32,128]{1,0:T(8,128)S(1)} collective-permute-done((f32[32,128]{1,0:T(8,128)S(1)}, f32[32,128]{1,0:T(8,128)S(1)}, u32[]{:S(2)}, u32[]{:S(2)}) %collective-permute-start.31) | collective-permute-done | bytes 16416 | tf_op jit(solution)/shard_map/ppermute | solution.py:38
  111.2 0.6 add.42
  (33 shorter events, 0.3 us)
Async XLA Ops:
  0.0 71.2 %copy-start = (s32[1,24576]{1,0:T(1,128)S(1)}, s32[1,24576]{1,0:T(1,128)}, u32[]{:S(2)}) copy-start(s32[1,24576]{1,0:T(1,128)} %param.8) | copy-start | bytes 294916
  1.8 12.9 %collective-permute-start = (f32[16,3072]{1,0:T(8,128)S(1)}, f32[16,3072]{1,0:T(8,128)S(1)}, u32[]{:S(2)}, u32[]{:S(2)}) collective-permute-start(f32[16,3072]{1,0:T(8,128)S(1)} %get-tuple-element.41.refs_3_), channel_id=1, source_target_pairs={{0,8},{1,9},{2,10},{3,11},{4,12},{5,13},{6,14},{7,15},{8,16},{9,17... | collective-permute-start | bytes 589832 | tf_op jit(solution)/shard_map/ppermute | solution.py:38
  3.8 11.0 %collective-permute-start.1 = (f32[16,3072]{1,0:T(8,128)S(1)}, f32[16,3072]{1,0:T(8,128)S(1)}, u32[]{:S(2)}, u32[]{:S(2)}) collective-permute-start(f32[16,3072]{1,0:T(8,128)S(1)} %get-tuple-element.50), channel_id=1, source_target_pairs={{0,56},{1,57},{2,58},{3,59},{4,60},{5,61},{6,62},{7,63},{8,0},{9,1... | collective-permute-start | bytes 589832 | tf_op jit(solution)/shard_map/ppermute | solution.py:38
  8.5 11.8 %collective-permute-start.4 = (f32[4,2,8,1536]{3,2,1,0:T(8,128)S(1)}, f32[4,2,8,1536]{3,2,1,0:T(8,128)S(1)}, u32[]{:S(2)}, u32[]{:S(2)}) collective-permute-start(f32[4,2,8,1536]{3,2,1,0:T(8,128)S(1)} %get-tuple-element.42.refs_3_), channel_id=1, source_target_pairs={{0,1},{1,2},{2,3},{3,0},{4,5},{5,6},{6,7},{7,4},{8,9},{9,10},{10,1... | collective-permute-start | bytes 1179656 | tf_op jit(solution)/shard_map/ppermute | solution.py:38
  10.1 10.2 %collective-permute-start.5 = (f32[4,2,8,1536]{3,2,1,0:T(8,128)S(1)}, f32[4,2,8,1536]{3,2,1,0:T(8,128)S(1)}, u32[]{:S(2)}, u32[]{:S(2)}) collective-permute-start(f32[4,2,8,1536]{3,2,1,0:T(8,128)S(1)} %get-tuple-element.55), channel_id=1, source_target_pairs={{0,3},{1,0},{2,1},{3,2},{4,7},{5,4},{6,5},{7,6},{8,11},{9,8},{10,9... | collective-permute-start | bytes 1179656 | tf_op jit(solution)/shard_map/ppermute | solution.py:38
  14.8 73.0 %copy-start.1 = (s32[32]{0:T(128)S(1)}, s32[32]{0:T(128)}, u32[]{:S(2)}) copy-start(s32[32]{0:T(128)} %param.9) | copy-start | bytes 388
  14.9 12.5 %collective-permute-start.2 = (f32[32,3072]{1,0:T(8,128)S(1)}, f32[32,3072]{1,0:T(8,128)S(1)}, u32[]{:S(2)}, u32[]{:S(2)}) collective-permute-start(f32[32,3072]{1,0:T(8,128)S(1)} %get-tuple-element.51.refs_4_), channel_id=1, source_target_pairs={{0,8},{1,9},{2,10},{3,11},{4,12},{5,13},{6,14},{7,15},{8,16},{9,17... | collective-permute-start | bytes 1179656 | tf_op jit(solution)/shard_map/ppermute | solution.py:38
  16.9 11.1 %collective-permute-start.3 = (f32[32,3072]{1,0:T(8,128)S(1)}, f32[32,3072]{1,0:T(8,128)S(1)}, u32[]{:S(2)}, u32[]{:S(2)}) collective-permute-start(f32[32,3072]{1,0:T(8,128)S(1)} %get-tuple-element.52), channel_id=1, source_target_pairs={{0,56},{1,57},{2,58},{3,59},{4,60},{5,61},{6,62},{7,63},{8,0},{9,1... | collective-permute-start | bytes 1179656 | tf_op jit(solution)/shard_map/ppermute | solution.py:38
  20.5 22.6 %collective-permute-start.10 = (f32[8,2,8,1536]{3,2,1,0:T(8,128)S(1)}, f32[8,2,8,1536]{3,2,1,0:T(8,128)S(1)}, u32[]{:S(2)}, u32[]{:S(2)}) collective-permute-start(f32[8,2,8,1536]{3,2,1,0:T(8,128)S(1)} %get-tuple-element.56.refs_4_), channel_id=1, source_target_pairs={{0,1},{1,2},{2,3},{3,0},{4,5},{5,6},{6,7},{7,4},{8,9},{9,10},{10,1... | collective-permute-start | bytes 2359304 | tf_op jit(solution)/shard_map/ppermute | solution.py:38
  22.1 20.9 %collective-permute-start.11 = (f32[8,2,8,1536]{3,2,1,0:T(8,128)S(1)}, f32[8,2,8,1536]{3,2,1,0:T(8,128)S(1)}, u32[]{:S(2)}, u32[]{:S(2)}) collective-permute-start(f32[8,2,8,1536]{3,2,1,0:T(8,128)S(1)} %get-tuple-element.62), channel_id=1, source_target_pairs={{0,3},{1,0},{2,1},{3,2},{4,7},{5,4},{6,5},{7,6},{8,11},{9,8},{10,9... | collective-permute-start | bytes 2359304 | tf_op jit(solution)/shard_map/ppermute | solution.py:38
  28.2 9.9 %collective-permute-start.6 = (f32[32,3072]{1,0:T(8,128)S(1)}, f32[32,3072]{1,0:T(8,128)S(1)}, u32[]{:S(2)}, u32[]{:S(2)}) collective-permute-start(f32[32,3072]{1,0:T(8,128)S(1)} %get-tuple-element.57.refs_4_), channel_id=1, source_target_pairs={{0,8},{1,9},{2,10},{3,11},{4,12},{5,13},{6,14},{7,15},{8,16},{9,17... | collective-permute-start | bytes 1179656 | tf_op jit(solution)/shard_map/ppermute | solution.py:38
  31.2 9.6 %collective-permute-start.7 = (f32[32,3072]{1,0:T(8,128)S(1)}, f32[32,3072]{1,0:T(8,128)S(1)}, u32[]{:S(2)}, u32[]{:S(2)}) collective-permute-start(f32[32,3072]{1,0:T(8,128)S(1)} %get-tuple-element.58), channel_id=1, source_target_pairs={{0,56},{1,57},{2,58},{3,59},{4,60},{5,61},{6,62},{7,63},{8,0},{9,1... | collective-permute-start | bytes 1179656 | tf_op jit(solution)/shard_map/ppermute | solution.py:38
  40.9 11.5 %collective-permute-start.8 = (f32[32,3072]{1,0:T(8,128)S(1)}, f32[32,3072]{1,0:T(8,128)S(1)}, u32[]{:S(2)}, u32[]{:S(2)}) collective-permute-start(f32[32,3072]{1,0:T(8,128)S(1)} %get-tuple-element.59.refs_3_), channel_id=1, source_target_pairs={{0,8},{1,9},{2,10},{3,11},{4,12},{5,13},{6,14},{7,15},{8,16},{9,17... | collective-permute-start | bytes 1179656 | tf_op jit(solution)/shard_map/ppermute | solution.py:38
  42.7 9.6 %collective-permute-start.9 = (f32[32,3072]{1,0:T(8,128)S(1)}, f32[32,3072]{1,0:T(8,128)S(1)}, u32[]{:S(2)}, u32[]{:S(2)}) collective-permute-start(f32[32,3072]{1,0:T(8,128)S(1)} %get-tuple-element.60), channel_id=1, source_target_pairs={{0,56},{1,57},{2,58},{3,59},{4,60},{5,61},{6,62},{7,63},{8,0},{9,1... | collective-permute-start | bytes 1179656 | tf_op jit(solution)/shard_map/ppermute | solution.py:38
  43.2 7.7 %collective-permute-start.12 = (f32[2,8,1536]{2,1,0:T(8,128)S(1)}, f32[2,8,1536]{2,1,0:T(8,128)S(1)}, u32[]{:S(2)}, u32[]{:S(2)}) collective-permute-start(f32[2,8,1536]{2,1,0:T(8,128)S(1)} %get-tuple-element.65), channel_id=1, source_target_pairs={{0,8},{1,9},{2,10},{3,11},{4,12},{5,13},{6,14},{7,15},{8,16},{9,17... | collective-permute-start | bytes 294920 | tf_op jit(solution)/shard_map/ppermute | solution.py:38
  45.0 7.3 %collective-permute-start.13 = (f32[2,8,1536]{2,1,0:T(8,128)S(1)}, f32[2,8,1536]{2,1,0:T(8,128)S(1)}, u32[]{:S(2)}, u32[]{:S(2)}) collective-permute-start(f32[2,8,1536]{2,1,0:T(8,128)S(1)} %get-tuple-element.66), channel_id=1, source_target_pairs={{0,56},{1,57},{2,58},{3,59},{4,60},{5,61},{6,62},{7,63},{8,0},{9,1... | collective-permute-start | bytes 294920 | tf_op jit(solution)/shard_map/ppermute | solution.py:38
  52.5 8.6 %collective-permute-start.14 = (f32[16,3072]{1,0:T(8,128)S(1)}, f32[16,3072]{1,0:T(8,128)S(1)}, u32[]{:S(2)}, u32[]{:S(2)}) collective-permute-start(f32[16,3072]{1,0:T(8,128)S(1)} %get-tuple-element.69.refs_4_), channel_id=1, source_target_pairs={{0,4},{1,5},{2,6},{3,7},{4,0},{5,1},{6,2},{7,3},{8,12},{9,13},{10,... | collective-permute-start | bytes 589832 | tf_op jit(solution)/shard_map/ppermute | solution.py:38
  54.1 5.4 %collective-permute-start.15 = (f32[2,8,1536]{2,1,0:T(8,128)S(1)}, f32[2,8,1536]{2,1,0:T(8,128)S(1)}, u32[]{:S(2)}, u32[]{:S(2)}) collective-permute-start(f32[2,8,1536]{2,1,0:T(8,128)S(1)} %get-tuple-element.67.refs_4_), channel_id=1, source_target_pairs={{0,8},{1,9},{2,10},{3,11},{4,12},{5,13},{6,14},{7,15},{8,16},{9,17... | collective-permute-start | bytes 294920 | tf_op jit(solution)/shard_map/ppermute | solution.py:38
  55.8 5.2 %collective-permute-start.16 = (f32[2,8,1536]{2,1,0:T(8,128)S(1)}, f32[2,8,1536]{2,1,0:T(8,128)S(1)}, u32[]{:S(2)}, u32[]{:S(2)}) collective-permute-start(f32[2,8,1536]{2,1,0:T(8,128)S(1)} %get-tuple-element.72), channel_id=1, source_target_pairs={{0,56},{1,57},{2,58},{3,59},{4,60},{5,61},{6,62},{7,63},{8,0},{9,1... | collective-permute-start | bytes 294920 | tf_op jit(solution)/shard_map/ppermute | solution.py:38
  61.1 6.6 %collective-permute-start.17 = (f32[16,3072]{1,0:T(8,128)S(1)}, f32[16,3072]{1,0:T(8,128)S(1)}, u32[]{:S(2)}, u32[]{:S(2)}) collective-permute-start(f32[16,3072]{1,0:T(8,128)S(1)} %shard_map.75.refs_2_.refs_0_), channel_id=1, source_target_pairs={{0,1},{1,0},{2,3},{3,2},{4,5},{5,4},{6,7},{7,6},{8,9},{9,8},{10,11... | collective-permute-start | bytes 589832 | tf_op jit(solution)/shard_map/ppermute | solution.py:38
  61.2 4.7 %collective-permute-start.18 = (f32[2,8,1536]{2,1,0:T(8,128)S(1)}, f32[2,8,1536]{2,1,0:T(8,128)S(1)}, u32[]{:S(2)}, u32[]{:S(2)}) collective-permute-start(f32[2,8,1536]{2,1,0:T(8,128)S(1)} %get-tuple-element.73.refs_2_), channel_id=1, source_target_pairs={{0,8},{1,9},{2,10},{3,11},{4,12},{5,13},{6,14},{7,15},{8,16},{9,17... | collective-permute-start | bytes 294920 | tf_op jit(solution)/shard_map/ppermute | solution.py:38
  63.0 6.8 %collective-permute-start.21 = (f32[2,8,1536]{2,1,0:T(8,128)S(1)}, f32[2,8,1536]{2,1,0:T(8,128)S(1)}, u32[]{:S(2)}, u32[]{:S(2)}) collective-permute-start(f32[2,8,1536]{2,1,0:T(8,128)S(1)} %get-tuple-element.76), channel_id=1, source_target_pairs={{0,56},{1,57},{2,58},{3,59},{4,60},{5,61},{6,62},{7,63},{8,0},{9,1... | collective-permute-start | bytes 294920 | tf_op jit(solution)/shard_map/ppermute | solution.py:38
  65.9 4.7 %collective-permute-start.20 = (f32[2,8,1536]{2,1,0:T(8,128)S(1)}, f32[2,8,1536]{2,1,0:T(8,128)S(1)}, u32[]{:S(2)}, u32[]{:S(2)}) collective-permute-start(f32[2,8,1536]{2,1,0:T(8,128)S(1)} %shard_map.76.refs_2_), channel_id=1, source_target_pairs={{0,8},{1,9},{2,10},{3,11},{4,12},{5,13},{6,14},{7,15},{8,16},{9,17... | collective-permute-start | bytes 294920 | tf_op jit(solution)/shard_map/ppermute | solution.py:38
  67.8 7.6 %collective-permute-start.19 = (f32[16,3072]{1,0:T(8,128)S(1)}, f32[16,3072]{1,0:T(8,128)S(1)}, u32[]{:S(2)}, u32[]{:S(2)}) collective-permute-start(f32[16,3072]{1,0:T(8,128)S(1)} %shard_map.77.refs_3_.own_ref), channel_id=1, source_target_pairs={{0,3},{1,2},{2,1},{3,0},{4,7},{5,6},{6,5},{7,4},{8,11},{9,10},{10,... | collective-permute-start | bytes 589832 | tf_op jit(solution)/shard_map/ppermute | solution.py:38
  70.6 4.7 %collective-permute-start.22 = (f32[2,8,1536]{2,1,0:T(8,128)S(1)}, f32[2,8,1536]{2,1,0:T(8,128)S(1)}, u32[]{:S(2)}, u32[]{:S(2)}) collective-permute-start(f32[2,8,1536]{2,1,0:T(8,128)S(1)} %shard_map.78.right_ref), channel_id=1, source_target_pairs={{0,4},{1,5},{2,6},{3,7},{4,0},{5,1},{6,2},{7,3},{8,12},{9,13},{10,... | collective-permute-start | bytes 294920 | tf_op jit(solution)/shard_map/ppermute | solution.py:38
  75.9 4.7 %collective-permute-start.23 = (f32[32,128]{1,0:T(8,128)S(1)}, f32[32,128]{1,0:T(8,128)S(1)}, u32[]{:S(2)}, u32[]{:S(2)}) collective-permute-start(f32[32,128]{1,0:T(8,128)S(1)} %shard_map.79), channel_id=1, source_target_pairs={{0,8},{1,9},{2,10},{3,11},{4,12},{5,13},{6,14},{7,15},{8,0},{9,1},... | collective-permute-start | bytes 49160 | tf_op jit(solution)/shard_map/ppermute | solution.py:38
  80.6 4.6 %collective-permute-start.24 = (f32[32,128]{1,0:T(8,128)S(1)}, f32[32,128]{1,0:T(8,128)S(1)}, u32[]{:S(2)}, u32[]{:S(2)}) collective-permute-start(f32[32,128]{1,0:T(8,128)S(1)} %add.36), channel_id=1, source_target_pairs={{0,16},{1,17},{2,18},{3,19},{4,20},{5,21},{6,22},{7,23},{8,24},{9,... | collective-permute-start | bytes 49160 | tf_op jit(solution)/shard_map/ppermute | solution.py:38
  85.2 6.7 %collective-permute-start.25 = (f32[32,128]{1,0:T(8,128)S(1)}, f32[32,128]{1,0:T(8,128)S(1)}, u32[]{:S(2)}, u32[]{:S(2)}) collective-permute-start(f32[32,128]{1,0:T(8,128)S(1)} %add.37), channel_id=1, source_target_pairs={{0,56},{1,57},{2,58},{3,59},{4,60},{5,61},{6,62},{7,63},{8,48},{9,... | collective-permute-start | bytes 49160 | tf_op jit(solution)/shard_map/ppermute | solution.py:38
  92.0 1.2 %collective-permute-start.26 = (f32[1,32,128]{2,1,0:T(8,128)S(1)}, f32[1,32,128]{2,1,0:T(8,128)S(1)}, u32[]{:S(2)}, u32[]{:S(2)}) collective-permute-start(f32[1,32,128]{2,1,0:T(8,128)S(1)} %multiply_bitcast_fusion), channel_id=1, source_target_pairs={{0,64},{64,0},{128,192},{192,128},{1,65},{65,1},{129,193},{193,129... | collective-permute-start | bytes 49160 | tf_op jit(solution)/shard_map/ppermute | solution.py:248
  93.3 5.5 %collective-permute-start.27 = (f32[2,32,128]{2,1,0:T(8,128)S(1)}, f32[2,32,128]{2,1,0:T(8,128)S(1)}, u32[]{:S(2)}, u32[]{:S(2)}) collective-permute-start(f32[2,32,128]{2,1,0:T(8,128)S(1)} %pad_maximum_fusion.1), channel_id=1, source_target_pairs={{0,128},{64,192},{128,0},{192,64},{1,129},{65,193},{129,1},{193,65... | collective-permute-start | bytes 98312 | tf_op jit(solution)/shard_map/ppermute | solution.py:248
  99.0 4.8 %collective-permute-start.28 = (f32[32,128]{1,0:T(8,128)S(1)}, f32[32,128]{1,0:T(8,128)S(1)}, u32[]{:S(2)}, u32[]{:S(2)}) collective-permute-start(f32[32,128]{1,0:T(8,128)S(1)} %fusion), channel_id=1, source_target_pairs={{0,1},{1,0},{2,3},{3,2},{4,5},{5,4},{6,7},{7,6},{8,9},{9,8},{10,11... | collective-permute-start | bytes 49160 | tf_op jit(solution)/shard_map/ppermute | solution.py:38
  101.0 5.2 %collective-permute-start.29 = (f32[32,128]{1,0:T(8,128)S(1)}, f32[32,128]{1,0:T(8,128)S(1)}, u32[]{:S(2)}, u32[]{:S(2)}) collective-permute-start(f32[32,128]{1,0:T(8,128)S(1)} %fusion), channel_id=1, source_target_pairs={{0,2},{1,3},{2,0},{3,1},{4,6},{5,7},{6,4},{7,5},{8,10},{9,11},{10,... | collective-permute-start | bytes 49160 | tf_op jit(solution)/shard_map/ppermute | solution.py:38
  102.4 4.9 %collective-permute-start.30 = (f32[32,128]{1,0:T(8,128)S(1)}, f32[32,128]{1,0:T(8,128)S(1)}, u32[]{:S(2)}, u32[]{:S(2)}) collective-permute-start(f32[32,128]{1,0:T(8,128)S(1)} %fusion), channel_id=1, source_target_pairs={{0,3},{1,2},{2,1},{3,0},{4,7},{5,6},{6,5},{7,4},{8,11},{9,10},{10,... | collective-permute-start | bytes 49160 | tf_op jit(solution)/shard_map/ppermute | solution.py:38
  107.4 3.8 %collective-permute-start.31 = (f32[32,128]{1,0:T(8,128)S(1)}, f32[32,128]{1,0:T(8,128)S(1)}, u32[]{:S(2)}, u32[]{:S(2)}) collective-permute-start(f32[32,128]{1,0:T(8,128)S(1)} %add_add_fusion), channel_id=1, source_target_pairs={{0,4},{1,5},{2,6},{3,7},{4,0},{5,1},{6,2},{7,3},{8,12},{9,13},{10,... | collective-permute-start | bytes 49160 | tf_op jit(solution)/shard_map/ppermute | solution.py:38

commit v6 on v5

--- a/solution.py
+++ b/solution.py
@@ -13,7 +13,7 @@
 RIGHT = ROWS // Y
 WIDE = TOK_GRP // Z
 HALF = WIDE // 2
-FAR, REST, ALL = (4,), (3, 5, 2, 6, 1, 7, 0), tuple(range(Z))
+FAR, REST, ALL = (4, 5), (3, 6, 2, 7, 1, 0), tuple(range(Z))
 SIZE = {"z": Z, "x": X, "y": Y}
 MIB = 1024 * 1024
 SMEM = pl.BlockSpec(memory_space=pltpu.SMEM)
@@ -83,10 +83,10 @@
     return [lax.rem(at_ref[0] + step, Z) * WIDE for step in steps]
 
 
-def left_far_kernel(at_ref, weight_ref, input_ref, rising_ref, falling_ref, *scratch):
-    (out,) = projections(weight_ref, input_ref, *scratch, begins(at_ref, FAR))
-    rising_ref[...] = out[: ROWS // 2]
-    falling_ref[...] = out[ROWS // 2 :]
+def left_far_kernel(at_ref, weight_ref, input_ref, *refs):
+    outs = projections(weight_ref, input_ref, *refs[-3:], begins(at_ref, FAR))
+    for out_ref, out in zip(refs[: len(FAR)], outs):
+        out_ref[...] = out
 
 
 def left_kernel(at_ref, weight_ref, input_ref, *refs):
@@ -192,7 +192,7 @@
 
     whole, half = (ROWS, WIDE), (ROWS // 2, WIDE)
     chunk = (2, RIGHT, HALF)
-    far = projected(left_far_kernel, place, in_proj, activations, 1, [half] * 2)
+    far = projected(left_far_kernel, place, in_proj, activations, len(FAR), [whole] * 2)
     left_moved = both_ways(*far, "z")
     *right, rising, falling = projected(
         right_kernel, place, out_proj, out_grads, Z, [(Z, *chunk)] * 3 + [(Z // 2, *chunk)] * 2,
@@ -200,23 +200,23 @@
     )
     right_moved = both_ways(rising, falling, "y")
     left = projected(
-        left_kernel, place, in_proj, activations, len(REST), [whole] * 7, after=[rising]
-    )
-
-    sent = step_add(left[0], left[1], left_moved, [], half=True)
+        left_kernel, place, in_proj, activations, len(REST), [whole] * 6, after=[rising]
+    )
+
+    sent = step_add(left[0], left[1], left_moved, [])
     left_moved = both_ways(*sent, "z")
     sent = step_add(right[1], right[2], right_moved, sent[:1], half=True)
     right_moved = both_ways(*sent, "y")
     sent = step_add(left[2], left[3], left_moved, sent[:1])
     left_moved = both_ways(*sent, "z")
-    sent = step_add(left[4], left[5], left_moved, sent[:1])
-    left_moved = both_ways(*sent, "z")
-    right = local(right_chunks_kernel, (), [right[0], *right_moved], [chunk] * Z, after=sent[:1])
+    (rising,) = local(add_kernel, (), [left[4], left_moved[0]], [whole], after=sent[:1])
+    left_moved = [send(rising, "z", lambda at: at + 1), left_moved[1]]
+    right = local(right_chunks_kernel, (), [right[0], *right_moved], [chunk] * Z, after=[rising])
     right_moved = both_ways(right[4], right[5], "z")
     sent = step_add(right[3], right[6], right_moved, [])
     right_moved = both_ways(*sent, "z")
     keep, give = local(
-        left_half_kernel, (at["x"],), [left[6], *left_moved], [half] * 2, [(2, *half)], after=sent[:1]
+        left_half_kernel, (at["x"],), [left[5], *left_moved], [half] * 2, [(2, *half)], after=sent[:1]
     )
     left_moved = mixed(give, "x", 1)
     sent = step_add(right[2], right[7], right_moved, [give])

time: 112 us -> 111 us (level)
  waiting for transfers between devices: 53.6 us -> 50.8 us
  starting transfers between devices: 46.2 us -> 48.4 us
    ppermute x30 -> x29, waiting for transfers between devices: 49.7 us -> 46.9 us  [send(): return lax.ppermute(value, 'par', pairs)]
    ppermute x30 -> x29, starting transfers between devices: 43.4 us -> 45.6 us  [send(): return lax.ppermute(value, 'par', pairs)]
  transfers between devices with their start and end apart: 32 -> 31, of which waited for: 20 -> 20; matrix products, arithmetic and copies ran while one was open for 0% -> 0% of each run, Pallas kernels for 7% -> 7%
where the time goes in v6:
time: 111 us
  waiting for transfers between devices  50.8 us (46%)
  starting transfers between devices  48.4 us (44%)
  Pallas kernels  10.7 us (10%)
    ppermute x29, waiting for transfers between devices, send(): return lax.ppermute(value, 'par', pairs)  46.9 us
    ppermute x29, starting transfers between devices, send(): return lax.ppermute(value, 'par', pairs)  45.6 us
    pallas_call x3, Pallas kernels, projected(): pl.pallas_call(ordered(kernel, 3, after), in_specs=[SMEM, *[pl.BlockSpec(...  9.26 us
    ppermute x2, waiting for transfers between devices, on_device(): other = lax.ppermute(cols, 'grp', [(i, i ^ bit) for i in range(4)])  3.85 us
    ppermute x2, starting transfers between devices, on_device(): other = lax.ppermute(cols, 'grp', [(i, i ^ bit) for i in range(4)])  2.84 us
  transfers between devices with their start and end apart: 31, of which 20 were waited for; matrix products, arithmetic and copies ran while one was open for 0% of the time, Pallas kernels for 7%

profile of v6, /device:TPU:32, one launch (start us, length us, event | category | flops | bytes accessed | tf_op | source)
XLA Modules:
  0.0 111.1 jit_solution(18176053064644498892)
XLA Ops:
  0.0 0.1 pad_add_fusion.refs_0_
  0.1 2.0 %shard_map.64 = (f32[32,3072]{1,0:T(8,128)S(1)}, f32[32,3072]{1,0:T(8,128)S(1)}) custom-call(s32[2]{0:T(128)S(1)} %pad_add_fusion.refs_0_, bf16[32,64]{1,0:T(8,128)(2,1)} %bitcast.10, bf16[64,24576]{1,0:T(8,128)(2,1)} %refs_2_.5), custom_call_target="tpu_custom_call" | custom-call | tf_op jit(solution)/shard_map/pallas_call | solution.py:117
  2.0 2.0 %collective-permute-start = (f32[32,3072]{1,0:T(8,128)S(1)}, f32[32,3072]{1,0:T(8,128)S(1)}, u32[]{:S(2)}, u32[]{:S(2)}) collective-permute-start(f32[32,3072]{1,0:T(8,128)S(1)} %get-tuple-element.38.refs_3_), channel_id=1, source_target_pairs={{0,8},{1,9},{2,10},{3,11},{4,12},{5,13},{6,14},{7,15},{8,16},{9,17... | collective-permute-start | bytes 1179656 | tf_op jit(solution)/shard_map/ppermute | solution.py:38
  4.0 0.1 collective-permute-start.1
  4.2 4.5 %shard_map.65 = (f32[8,2,8,1536]{3,2,1,0:T(8,128)S(1)}, f32[8,2,8,1536]{3,2,1,0:T(8,128)S(1)}, f32[8,2,8,1536]{3,2,1,0:T(8,128)S(1)}, f32[4,2,8,1536]{3,2,1,0:T(8,128)S(1)}, f32[4,2,8,1536]{3,2,1,0:T(8,128)S(1)}) custom-call(s32[2]{0:T(128)S(1)} %pad_add_fusion.refs_0_, bf16[32,172]{1,0:T(8,128)(2,1)} %bitcast.12, bf16[172,24576]{1,0:T(8,128)(2,1)} %refs_2_.4, ...), custom_call_target="tpu_custom_call" | custom-call | tf_op jit(solution)/shard_map/pallas_call | solution.py:117
  8.7 1.6 %collective-permute-start.4 = (f32[4,2,8,1536]{3,2,1,0:T(8,128)S(1)}, f32[4,2,8,1536]{3,2,1,0:T(8,128)S(1)}, u32[]{:S(2)}, u32[]{:S(2)}) collective-permute-start(f32[4,2,8,1536]{3,2,1,0:T(8,128)S(1)} %get-tuple-element.39.refs_3_), channel_id=1, source_target_pairs={{0,1},{1,2},{2,3},{3,0},{4,5},{5,6},{6,7},{7,4},{8,9},{9,10},{10,1... | collective-permute-start | bytes 1179656 | tf_op jit(solution)/shard_map/ppermute | solution.py:38
  10.3 1.7 %collective-permute-start.5 = (f32[4,2,8,1536]{3,2,1,0:T(8,128)S(1)}, f32[4,2,8,1536]{3,2,1,0:T(8,128)S(1)}, u32[]{:S(2)}, u32[]{:S(2)}) collective-permute-start(f32[4,2,8,1536]{3,2,1,0:T(8,128)S(1)} %get-tuple-element.51), channel_id=1, source_target_pairs={{0,3},{1,0},{2,1},{3,2},{4,7},{5,4},{6,5},{7,6},{8,11},{9,8},{10,9... | collective-permute-start | bytes 1179656 | tf_op jit(solution)/shard_map/ppermute | solution.py:38
  12.0 2.8 %shard_map.66 = (f32[32,3072]{1,0:T(8,128)S(1)}, f32[32,3072]{1,0:T(8,128)S(1)}, f32[32,3072]{1,0:T(8,128)S(1)}, f32[32,3072]{1,0:T(8,128)S(1)}, f32[32,3072]{1,0:T(8,128)S(1)}, /*index=5*/f32[32,3072]{1,0:T(8,128)S(1)}) custom-call(s32[2]{0:T(128)S(1)} %pad_add_fusion.refs_0_, bf16[32,64]{1,0:T(8,128)(2,1)} %bitcast.11, bf16[64,24576]{1,0:T(8,128)(2,1)} %refs_2_.5, ...), custom_call_target="tpu_custom_call" | custom-call | tf_op jit(solution)/shard_map/pallas_call | solution.py:117
  14.8 0.0 copy-start.1
  14.8 0.0 collective-permute-done.refs_2_
  14.8 0.0 collective-permute-done.1.refs_3_
  14.8 0.1 shard_map.67
  15.0 3.2 %collective-permute-start.2 = (f32[32,3072]{1,0:T(8,128)S(1)}, f32[32,3072]{1,0:T(8,128)S(1)}, u32[]{:S(2)}, u32[]{:S(2)}) collective-permute-start(f32[32,3072]{1,0:T(8,128)S(1)} %get-tuple-element.47.refs_4_), channel_id=1, source_target_pairs={{0,8},{1,9},{2,10},{3,11},{4,12},{5,13},{6,14},{7,15},{8,16},{9,17... | collective-permute-start | bytes 1179656 | tf_op jit(solution)/shard_map/ppermute | solution.py:38
  18.1 1.0 collective-permute-start.3
  19.2 1.3 %collective-permute-done.4.refs_2_ = f32[4,2,8,1536]{3,2,1,0:T(8,128)S(1)} collective-permute-done((f32[4,2,8,1536]{3,2,1,0:T(8,128)S(1)}, f32[4,2,8,1536]{3,2,1,0:T(8,128)S(1)}, u32[]{:S(2)}, u32[]{:S(2)}) %collective-permute-start.4) | collective-permute-done | bytes 393248 | tf_op jit(solution)/shard_map/ppermute | solution.py:38
  20.5 0.0 collective-permute-done.5.refs_3_
  20.5 0.1 shard_map.68
  20.7 3.1 %collective-permute-start.10 = (f32[8,2,8,1536]{3,2,1,0:T(8,128)S(1)}, f32[8,2,8,1536]{3,2,1,0:T(8,128)S(1)}, u32[]{:S(2)}, u32[]{:S(2)}) collective-permute-start(f32[8,2,8,1536]{3,2,1,0:T(8,128)S(1)} %get-tuple-element.56), channel_id=1, source_target_pairs={{0,3},{1,0},{2,1},{3,2},{4,7},{5,4},{6,5},{7,6},{8,11},{9,8},{10,9... | collective-permute-start | bytes 2359304 | tf_op jit(solution)/shard_map/ppermute | solution.py:38
  23.8 3.7 %collective-permute-done.2.refs_2_ = f32[32,3072]{1,0:T(8,128)S(1)} collective-permute-done((f32[32,3072]{1,0:T(8,128)S(1)}, f32[32,3072]{1,0:T(8,128)S(1)}, u32[]{:S(2)}, u32[]{:S(2)}) %collective-permute-start.2) | collective-permute-done | bytes 393248 | tf_op jit(solution)/shard_map/ppermute | solution.py:38
  27.5 1.3 %collective-permute-done.3.refs_3_ = f32[32,3072]{1,0:T(8,128)S(1)} collective-permute-done((f32[32,3072]{1,0:T(8,128)S(1)}, f32[32,3072]{1,0:T(8,128)S(1)}, u32[]{:S(2)}, u32[]{:S(2)}) %collective-permute-start.3) | collective-permute-done | bytes 393248 | tf_op jit(solution)/shard_map/ppermute | solution.py:38
  28.7 0.1 shard_map.69
  28.9 2.4 %collective-permute-start.6 = (f32[32,3072]{1,0:T(8,128)S(1)}, f32[32,3072]{1,0:T(8,128)S(1)}, u32[]{:S(2)}, u32[]{:S(2)}) collective-permute-start(f32[32,3072]{1,0:T(8,128)S(1)} %get-tuple-element.53.refs_2_), channel_id=1, source_target_pairs={{0,8},{1,9},{2,10},{3,11},{4,12},{5,13},{6,14},{7,15},{8,16},{9,17... | collective-permute-start | bytes 1179656 | tf_op jit(solution)/shard_map/ppermute | solution.py:38
  31.3 6.9 %collective-permute-done.6.refs_1_ = f32[32,3072]{1,0:T(8,128)S(1)} collective-permute-done((f32[32,3072]{1,0:T(8,128)S(1)}, f32[32,3072]{1,0:T(8,128)S(1)}, u32[]{:S(2)}, u32[]{:S(2)}) %collective-permute-start.6) | collective-permute-done | bytes 393248 | tf_op jit(solution)/shard_map/ppermute | solution.py:38
  38.2 2.9 %collective-permute-start.7 = (f32[32,3072]{1,0:T(8,128)S(1)}, f32[32,3072]{1,0:T(8,128)S(1)}, u32[]{:S(2)}, u32[]{:S(2)}) collective-permute-start(f32[32,3072]{1,0:T(8,128)S(1)} %shard_map.70.refs_3_), channel_id=1, source_target_pairs={{0,8},{1,9},{2,10},{3,11},{4,12},{5,13},{6,14},{7,15},{8,16},{9,17... | collective-permute-start | bytes 1179656 | tf_op jit(solution)/shard_map/ppermute | solution.py:38
  41.0 1.5 %collective-permute-done.9.refs_1_ = f32[8,2,8,1536]{3,2,1,0:T(8,128)S(1)} collective-permute-done((f32[8,2,8,1536]{3,2,1,0:T(8,128)S(1)}, f32[8,2,8,1536]{3,2,1,0:T(8,128)S(1)}, u32[]{:S(2)}, u32[]{:S(2)}) %collective-permute-start.9) | collective-permute-done | bytes 786464 | tf_op jit(solution)/shard_map/ppermute | solution.py:38
  42.5 0.1 shard_map.71
  42.6 2.2 %collective-permute-start.11 = (f32[2,8,1536]{2,1,0:T(8,128)S(1)}, f32[2,8,1536]{2,1,0:T(8,128)S(1)}, u32[]{:S(2)}, u32[]{:S(2)}) collective-permute-start(f32[2,8,1536]{2,1,0:T(8,128)S(1)} %get-tuple-element.59), channel_id=1, source_target_pairs={{0,8},{1,9},{2,10},{3,11},{4,12},{5,13},{6,14},{7,15},{8,16},{9,17... | collective-permute-start | bytes 294920 | tf_op jit(solution)/shard_map/ppermute | solution.py:38
  44.8 2.4 %collective-permute-start.12 = (f32[2,8,1536]{2,1,0:T(8,128)S(1)}, f32[2,8,1536]{2,1,0:T(8,128)S(1)}, u32[]{:S(2)}, u32[]{:S(2)}) collective-permute-start(f32[2,8,1536]{2,1,0:T(8,128)S(1)} %get-tuple-element.60), channel_id=1, source_target_pairs={{0,56},{1,57},{2,58},{3,59},{4,60},{5,61},{6,62},{7,63},{8,0},{9,1... | collective-permute-start | bytes 294920 | tf_op jit(solution)/shard_map/ppermute | solution.py:38
  47.2 2.7 %collective-permute-done.11.refs_2_ = f32[2,8,1536]{2,1,0:T(8,128)S(1)} collective-permute-done((f32[2,8,1536]{2,1,0:T(8,128)S(1)}, f32[2,8,1536]{2,1,0:T(8,128)S(1)}, u32[]{:S(2)}, u32[]{:S(2)}) %collective-permute-start.11) | collective-permute-done | bytes 98336 | tf_op jit(solution)/shard_map/ppermute | solution.py:38
  49.9 0.8 collective-permute-done.12.refs_3_
  50.7 0.1 shard_map.73
  50.8 1.6 %collective-permute-start.13 = (f32[16,3072]{1,0:T(8,128)S(1)}, f32[16,3072]{1,0:T(8,128)S(1)}, u32[]{:S(2)}, u32[]{:S(2)}) collective-permute-start(f32[16,3072]{1,0:T(8,128)S(1)} %get-tuple-element.63.refs_4_), channel_id=1, source_target_pairs={{0,4},{1,5},{2,6},{3,7},{4,0},{5,1},{6,2},{7,3},{8,12},{9,13},{10,... | collective-permute-start | bytes 589832 | tf_op jit(solution)/shard_map/ppermute | solution.py:38
  52.4 2.7 %collective-permute-start.14 = (f32[2,8,1536]{2,1,0:T(8,128)S(1)}, f32[2,8,1536]{2,1,0:T(8,128)S(1)}, u32[]{:S(2)}, u32[]{:S(2)}) collective-permute-start(f32[2,8,1536]{2,1,0:T(8,128)S(1)} %get-tuple-element.61.refs_4_), channel_id=1, source_target_pairs={{0,8},{1,9},{2,10},{3,11},{4,12},{5,13},{6,14},{7,15},{8,16},{9,17... | collective-permute-start | bytes 294920 | tf_op jit(solution)/shard_map/ppermute | solution.py:38
  55.0 2.2 %collective-permute-done.14.refs_2_ = f32[2,8,1536]{2,1,0:T(8,128)S(1)} collective-permute-done((f32[2,8,1536]{2,1,0:T(8,128)S(1)}, f32[2,8,1536]{2,1,0:T(8,128)S(1)}, u32[]{:S(2)}, u32[]{:S(2)}) %collective-permute-start.14) | collective-permute-done | bytes 98336 | tf_op jit(solution)/shard_map/ppermute | solution.py:38
  57.3 4.0 %collective-permute-done.15.refs_3_ = f32[2,8,1536]{2,1,0:T(8,128)S(1)} collective-permute-done((f32[2,8,1536]{2,1,0:T(8,128)S(1)}, f32[2,8,1536]{2,1,0:T(8,128)S(1)}, u32[]{:S(2)}, u32[]{:S(2)}) %collective-permute-start.15) | collective-permute-done | bytes 98336 | tf_op jit(solution)/shard_map/ppermute | solution.py:38
  61.4 0.1 collective-permute-start.16
  61.5 2.4 %collective-permute-start.17 = (f32[2,8,1536]{2,1,0:T(8,128)S(1)}, f32[2,8,1536]{2,1,0:T(8,128)S(1)}, u32[]{:S(2)}, u32[]{:S(2)}) collective-permute-start(f32[2,8,1536]{2,1,0:T(8,128)S(1)} %get-tuple-element.67.refs_2_), channel_id=1, source_target_pairs={{0,8},{1,9},{2,10},{3,11},{4,12},{5,13},{6,14},{7,15},{8,16},{9,17... | collective-permute-start | bytes 294920 | tf_op jit(solution)/shard_map/ppermute | solution.py:38
  63.9 2.3 %collective-permute-done.17.refs_1_ = f32[2,8,1536]{2,1,0:T(8,128)S(1)} collective-permute-done((f32[2,8,1536]{2,1,0:T(8,128)S(1)}, f32[2,8,1536]{2,1,0:T(8,128)S(1)}, u32[]{:S(2)}, u32[]{:S(2)}) %collective-permute-start.17) | collective-permute-done | bytes 98336 | tf_op jit(solution)/shard_map/ppermute | solution.py:38
  66.2 2.4 %collective-permute-start.19 = (f32[2,8,1536]{2,1,0:T(8,128)S(1)}, f32[2,8,1536]{2,1,0:T(8,128)S(1)}, u32[]{:S(2)}, u32[]{:S(2)}) collective-permute-start(f32[2,8,1536]{2,1,0:T(8,128)S(1)} %shard_map.76.refs_2_), channel_id=1, source_target_pairs={{0,8},{1,9},{2,10},{3,11},{4,12},{5,13},{6,14},{7,15},{8,16},{9,17... | collective-permute-start | bytes 294920 | tf_op jit(solution)/shard_map/ppermute | solution.py:38
  68.6 0.1 collective-permute-start.18
  68.8 2.1 %collective-permute-done.19.refs_1_ = f32[2,8,1536]{2,1,0:T(8,128)S(1)} collective-permute-done((f32[2,8,1536]{2,1,0:T(8,128)S(1)}, f32[2,8,1536]{2,1,0:T(8,128)S(1)}, u32[]{:S(2)}, u32[]{:S(2)}) %collective-permute-start.19) | collective-permute-done | bytes 98336 | tf_op jit(solution)/shard_map/ppermute | solution.py:38
  70.9 0.6 collective-permute-start.21
  71.5 4.1 %collective-permute-done.21.moved_ref = f32[2,8,1536]{2,1,0:T(8,128)S(1)} collective-permute-done((f32[2,8,1536]{2,1,0:T(8,128)S(1)}, f32[2,8,1536]{2,1,0:T(8,128)S(1)}, u32[]{:S(2)}, u32[]{:S(2)}) %collective-permute-start.21) | collective-permute-done | bytes 98336 | tf_op jit(solution)/shard_map/ppermute | solution.py:38
  75.6 0.6 shard_map.79
  76.2 2.7 %collective-permute-start.22 = (f32[32,128]{1,0:T(8,128)S(1)}, f32[32,128]{1,0:T(8,128)S(1)}, u32[]{:S(2)}, u32[]{:S(2)}) collective-permute-start(f32[32,128]{1,0:T(8,128)S(1)} %shard_map.79), channel_id=1, source_target_pairs={{0,8},{1,9},{2,10},{3,11},{4,12},{5,13},{6,14},{7,15},{8,0},{9,1},... | collective-permute-start | bytes 49160 | tf_op jit(solution)/shard_map/ppermute | solution.py:38
  78.9 1.7 %collective-permute-done.22 = f32[32,128]{1,0:T(8,128)S(1)} collective-permute-done((f32[32,128]{1,0:T(8,128)S(1)}, f32[32,128]{1,0:T(8,128)S(1)}, u32[]{:S(2)}, u32[]{:S(2)}) %collective-permute-start.22) | collective-permute-done | bytes 16416 | tf_op jit(solution)/shard_map/ppermute | solution.py:38
  80.6 2.1 %collective-permute-start.23 = (f32[32,128]{1,0:T(8,128)S(1)}, f32[32,128]{1,0:T(8,128)S(1)}, u32[]{:S(2)}, u32[]{:S(2)}) collective-permute-start(f32[32,128]{1,0:T(8,128)S(1)} %add.36), channel_id=1, source_target_pairs={{0,16},{1,17},{2,18},{3,19},{4,20},{5,21},{6,22},{7,23},{8,24},{9,... | collective-permute-start | bytes 49160 | tf_op jit(solution)/shard_map/ppermute | solution.py:38
  82.7 2.5 %collective-permute-done.23 = f32[32,128]{1,0:T(8,128)S(1)} collective-permute-done((f32[32,128]{1,0:T(8,128)S(1)}, f32[32,128]{1,0:T(8,128)S(1)}, u32[]{:S(2)}, u32[]{:S(2)}) %collective-permute-start.23) | collective-permute-done | bytes 16416 | tf_op jit(solution)/shard_map/ppermute | solution.py:38
  85.3 2.8 %collective-permute-start.24 = (f32[32,128]{1,0:T(8,128)S(1)}, f32[32,128]{1,0:T(8,128)S(1)}, u32[]{:S(2)}, u32[]{:S(2)}) collective-permute-start(f32[32,128]{1,0:T(8,128)S(1)} %add.37), channel_id=1, source_target_pairs={{0,56},{1,57},{2,58},{3,59},{4,60},{5,61},{6,62},{7,63},{8,48},{9,... | collective-permute-start | bytes 49160 | tf_op jit(solution)/shard_map/ppermute | solution.py:38
  88.1 3.9 %collective-permute-done.24 = f32[32,128]{1,0:T(8,128)S(1)} collective-permute-done((f32[32,128]{1,0:T(8,128)S(1)}, f32[32,128]{1,0:T(8,128)S(1)}, u32[]{:S(2)}, u32[]{:S(2)}) %collective-permute-start.24) | collective-permute-done | bytes 16416 | tf_op jit(solution)/shard_map/ppermute | solution.py:38
  92.0 0.1 multiply_bitcast_fusion
  92.1 0.0 collective-permute-start.25
  92.1 1.2 %collective-permute-done.25 = f32[1,32,128]{2,1,0:T(8,128)S(1)} collective-permute-done((f32[1,32,128]{2,1,0:T(8,128)S(1)}, f32[1,32,128]{2,1,0:T(8,128)S(1)}, u32[]{:S(2)}, u32[]{:S(2)}) %collective-permute-start.25) | collective-permute-done | bytes 16416 | tf_op jit(solution)/shard_map/ppermute | solution.py:248
  93.3 2.8 %collective-permute-start.26 = (f32[2,32,128]{2,1,0:T(8,128)S(1)}, f32[2,32,128]{2,1,0:T(8,128)S(1)}, u32[]{:S(2)}, u32[]{:S(2)}) collective-permute-start(f32[2,32,128]{2,1,0:T(8,128)S(1)} %pad_maximum_fusion.1), channel_id=1, source_target_pairs={{0,128},{64,192},{128,0},{192,64},{1,129},{65,193},{129,1},{193,65... | collective-permute-start | bytes 98312 | tf_op jit(solution)/shard_map/ppermute | solution.py:248
  96.1 2.7 %collective-permute-done.26 = f32[2,32,128]{2,1,0:T(8,128)S(1)} collective-permute-done((f32[2,32,128]{2,1,0:T(8,128)S(1)}, f32[2,32,128]{2,1,0:T(8,128)S(1)}, u32[]{:S(2)}, u32[]{:S(2)}) %collective-permute-start.26) | collective-permute-done | bytes 32800 | tf_op jit(solution)/shard_map/ppermute | solution.py:248
  98.8 0.2 fusion
  99.1 1.7 %collective-permute-start.27 = (f32[32,128]{1,0:T(8,128)S(1)}, f32[32,128]{1,0:T(8,128)S(1)}, u32[]{:S(2)}, u32[]{:S(2)}) collective-permute-start(f32[32,128]{1,0:T(8,128)S(1)} %fusion), channel_id=1, source_target_pairs={{0,1},{1,0},{2,3},{3,2},{4,5},{5,4},{6,7},{7,6},{8,9},{9,8},{10,11... | collective-permute-start | bytes 49160 | tf_op jit(solution)/shard_map/ppermute | solution.py:38
  100.8 0.9 collective-permute-start.28
  101.7 2.2 %collective-permute-start.29 = (f32[32,128]{1,0:T(8,128)S(1)}, f32[32,128]{1,0:T(8,128)S(1)}, u32[]{:S(2)}, u32[]{:S(2)}) collective-permute-start(f32[32,128]{1,0:T(8,128)S(1)} %fusion), channel_id=1, source_target_pairs={{0,3},{1,2},{2,1},{3,0},{4,7},{5,6},{6,5},{7,4},{8,11},{9,10},{10,... | collective-permute-start | bytes 49160 | tf_op jit(solution)/shard_map/ppermute | solution.py:38
  103.9 2.2 %collective-permute-done.28 = f32[32,128]{1,0:T(8,128)S(1)} collective-permute-done((f32[32,128]{1,0:T(8,128)S(1)}, f32[32,128]{1,0:T(8,128)S(1)}, u32[]{:S(2)}, u32[]{:S(2)}) %collective-permute-start.28) | collective-permute-done | bytes 16416 | tf_op jit(solution)/shard_map/ppermute | solution.py:38
  106.0 0.6 collective-permute-done.29
  106.7 0.6 collective-permute-start.30
  107.3 3.2 %collective-permute-done.30 = f32[32,128]{1,0:T(8,128)S(1)} collective-permute-done((f32[32,128]{1,0:T(8,128)S(1)}, f32[32,128]{1,0:T(8,128)S(1)}, u32[]{:S(2)}, u32[]{:S(2)}) %collective-permute-start.30) | collective-permute-done | bytes 16416 | tf_op jit(solution)/shard_map/ppermute | solution.py:38
  110.5 0.6 add.42
  (31 shorter events, 0.3 us)
Async XLA Ops:
  0.0 71.5 %copy-start = (s32[1,24576]{1,0:T(1,128)S(1)}, s32[1,24576]{1,0:T(1,128)}, u32[]{:S(2)}) copy-start(s32[1,24576]{1,0:T(1,128)} %param.8) | copy-start | bytes 294916
  2.0 12.7 %collective-permute-start = (f32[32,3072]{1,0:T(8,128)S(1)}, f32[32,3072]{1,0:T(8,128)S(1)}, u32[]{:S(2)}, u32[]{:S(2)}) collective-permute-start(f32[32,3072]{1,0:T(8,128)S(1)} %get-tuple-element.38.refs_3_), channel_id=1, source_target_pairs={{0,8},{1,9},{2,10},{3,11},{4,12},{5,13},{6,14},{7,15},{8,16},{9,17... | collective-permute-start | bytes 1179656 | tf_op jit(solution)/shard_map/ppermute | solution.py:38
  4.0 10.8 %collective-permute-start.1 = (f32[32,3072]{1,0:T(8,128)S(1)}, f32[32,3072]{1,0:T(8,128)S(1)}, u32[]{:S(2)}, u32[]{:S(2)}) collective-permute-start(f32[32,3072]{1,0:T(8,128)S(1)} %get-tuple-element.46), channel_id=1, source_target_pairs={{0,56},{1,57},{2,58},{3,59},{4,60},{5,61},{6,62},{7,63},{8,0},{9,1... | collective-permute-start | bytes 1179656 | tf_op jit(solution)/shard_map/ppermute | solution.py:38
  8.7 11.8 %collective-permute-start.4 = (f32[4,2,8,1536]{3,2,1,0:T(8,128)S(1)}, f32[4,2,8,1536]{3,2,1,0:T(8,128)S(1)}, u32[]{:S(2)}, u32[]{:S(2)}) collective-permute-start(f32[4,2,8,1536]{3,2,1,0:T(8,128)S(1)} %get-tuple-element.39.refs_3_), channel_id=1, source_target_pairs={{0,1},{1,2},{2,3},{3,0},{4,5},{5,6},{6,7},{7,4},{8,9},{9,10},{10,1... | collective-permute-start | bytes 1179656 | tf_op jit(solution)/shard_map/ppermute | solution.py:38
  10.3 10.2 %collective-permute-start.5 = (f32[4,2,8,1536]{3,2,1,0:T(8,128)S(1)}, f32[4,2,8,1536]{3,2,1,0:T(8,128)S(1)}, u32[]{:S(2)}, u32[]{:S(2)}) collective-permute-start(f32[4,2,8,1536]{3,2,1,0:T(8,128)S(1)} %get-tuple-element.51), channel_id=1, source_target_pairs={{0,3},{1,0},{2,1},{3,2},{4,7},{5,4},{6,5},{7,6},{8,11},{9,8},{10,9... | collective-permute-start | bytes 1179656 | tf_op jit(solution)/shard_map/ppermute | solution.py:38
  14.8 73.3 %copy-start.1 = (s32[32]{0:T(128)S(1)}, s32[32]{0:T(128)}, u32[]{:S(2)}) copy-start(s32[32]{0:T(128)} %param.9) | copy-start | bytes 388
  15.0 12.5 %collective-permute-start.2 = (f32[32,3072]{1,0:T(8,128)S(1)}, f32[32,3072]{1,0:T(8,128)S(1)}, u32[]{:S(2)}, u32[]{:S(2)}) collective-permute-start(f32[32,3072]{1,0:T(8,128)S(1)} %get-tuple-element.47.refs_4_), channel_id=1, source_target_pairs={{0,8},{1,9},{2,10},{3,11},{4,12},{5,13},{6,14},{7,15},{8,16},{9,17... | collective-permute-start | bytes 1179656 | tf_op jit(solution)/shard_map/ppermute | solution.py:38
  18.1 10.6 %collective-permute-start.3 = (f32[32,3072]{1,0:T(8,128)S(1)}, f32[32,3072]{1,0:T(8,128)S(1)}, u32[]{:S(2)}, u32[]{:S(2)}) collective-permute-start(f32[32,3072]{1,0:T(8,128)S(1)} %get-tuple-element.48), channel_id=1, source_target_pairs={{0,56},{1,57},{2,58},{3,59},{4,60},{5,61},{6,62},{7,63},{8,0},{9,1... | collective-permute-start | bytes 1179656 | tf_op jit(solution)/shard_map/ppermute | solution.py:38
  20.7 20.4 %collective-permute-start.10 = (f32[8,2,8,1536]{3,2,1,0:T(8,128)S(1)}, f32[8,2,8,1536]{3,2,1,0:T(8,128)S(1)}, u32[]{:S(2)}, u32[]{:S(2)}) collective-permute-start(f32[8,2,8,1536]{3,2,1,0:T(8,128)S(1)} %get-tuple-element.56), channel_id=1, source_target_pairs={{0,3},{1,0},{2,1},{3,2},{4,7},{5,4},{6,5},{7,6},{8,11},{9,8},{10,9... | collective-permute-start | bytes 2359304 | tf_op jit(solution)/shard_map/ppermute | solution.py:38
  23.8 18.8 %collective-permute-start.9 = (f32[8,2,8,1536]{3,2,1,0:T(8,128)S(1)}, f32[8,2,8,1536]{3,2,1,0:T(8,128)S(1)}, u32[]{:S(2)}, u32[]{:S(2)}) collective-permute-start(f32[8,2,8,1536]{3,2,1,0:T(8,128)S(1)} %get-tuple-element.52.refs_4_), channel_id=1, source_target_pairs={{0,1},{1,2},{2,3},{3,0},{4,5},{5,6},{6,7},{7,4},{8,9},{9,10},{10,1... | collective-permute-start | bytes 2359304 | tf_op jit(solution)/shard_map/ppermute | solution.py:38
  28.9 9.3 %collective-permute-start.6 = (f32[32,3072]{1,0:T(8,128)S(1)}, f32[32,3072]{1,0:T(8,128)S(1)}, u32[]{:S(2)}, u32[]{:S(2)}) collective-permute-start(f32[32,3072]{1,0:T(8,128)S(1)} %get-tuple-element.53.refs_2_), channel_id=1, source_target_pairs={{0,8},{1,9},{2,10},{3,11},{4,12},{5,13},{6,14},{7,15},{8,16},{9,17... | collective-permute-start | bytes 1179656 | tf_op jit(solution)/shard_map/ppermute | solution.py:38
  31.3 19.4 %collective-permute-start.8 = (f32[32,3072]{1,0:T(8,128)S(1)}, f32[32,3072]{1,0:T(8,128)S(1)}, u32[]{:S(2)}, u32[]{:S(2)}) collective-permute-start(f32[32,3072]{1,0:T(8,128)S(1)} %get-tuple-element.54), channel_id=1, source_target_pairs={{0,56},{1,57},{2,58},{3,59},{4,60},{5,61},{6,62},{7,63},{8,0},{9,1... | collective-permute-start | bytes 1179656 | tf_op jit(solution)/shard_map/ppermute | solution.py:38
  38.2 12.5 %collective-permute-start.7 = (f32[32,3072]{1,0:T(8,128)S(1)}, f32[32,3072]{1,0:T(8,128)S(1)}, u32[]{:S(2)}, u32[]{:S(2)}) collective-permute-start(f32[32,3072]{1,0:T(8,128)S(1)} %shard_map.70.refs_3_), channel_id=1, source_target_pairs={{0,8},{1,9},{2,10},{3,11},{4,12},{5,13},{6,14},{7,15},{8,16},{9,17... | collective-permute-start | bytes 1179656 | tf_op jit(solution)/shard_map/ppermute | solution.py:38
  42.6 7.2 %collective-permute-start.11 = (f32[2,8,1536]{2,1,0:T(8,128)S(1)}, f32[2,8,1536]{2,1,0:T(8,128)S(1)}, u32[]{:S(2)}, u32[]{:S(2)}) collective-permute-start(f32[2,8,1536]{2,1,0:T(8,128)S(1)} %get-tuple-element.59), channel_id=1, source_target_pairs={{0,8},{1,9},{2,10},{3,11},{4,12},{5,13},{6,14},{7,15},{8,16},{9,17... | collective-permute-start | bytes 294920 | tf_op jit(solution)/shard_map/ppermute | solution.py:38
  44.8 5.8 %collective-permute-start.12 = (f32[2,8,1536]{2,1,0:T(8,128)S(1)}, f32[2,8,1536]{2,1,0:T(8,128)S(1)}, u32[]{:S(2)}, u32[]{:S(2)}) collective-permute-start(f32[2,8,1536]{2,1,0:T(8,128)S(1)} %get-tuple-element.60), channel_id=1, source_target_pairs={{0,56},{1,57},{2,58},{3,59},{4,60},{5,61},{6,62},{7,63},{8,0},{9,1... | collective-permute-start | bytes 294920 | tf_op jit(solution)/shard_map/ppermute | solution.py:38
  50.8 10.6 %collective-permute-start.13 = (f32[16,3072]{1,0:T(8,128)S(1)}, f32[16,3072]{1,0:T(8,128)S(1)}, u32[]{:S(2)}, u32[]{:S(2)}) collective-permute-start(f32[16,3072]{1,0:T(8,128)S(1)} %get-tuple-element.63.refs_4_), channel_id=1, source_target_pairs={{0,4},{1,5},{2,6},{3,7},{4,0},{5,1},{6,2},{7,3},{8,12},{9,13},{10,... | collective-permute-start | bytes 589832 | tf_op jit(solution)/shard_map/ppermute | solution.py:38
  52.4 4.9 %collective-permute-start.14 = (f32[2,8,1536]{2,1,0:T(8,128)S(1)}, f32[2,8,1536]{2,1,0:T(8,128)S(1)}, u32[]{:S(2)}, u32[]{:S(2)}) collective-permute-start(f32[2,8,1536]{2,1,0:T(8,128)S(1)} %get-tuple-element.61.refs_4_), channel_id=1, source_target_pairs={{0,8},{1,9},{2,10},{3,11},{4,12},{5,13},{6,14},{7,15},{8,16},{9,17... | collective-permute-start | bytes 294920 | tf_op jit(solution)/shard_map/ppermute | solution.py:38
  55.0 6.3 %collective-permute-start.15 = (f32[2,8,1536]{2,1,0:T(8,128)S(1)}, f32[2,8,1536]{2,1,0:T(8,128)S(1)}, u32[]{:S(2)}, u32[]{:S(2)}) collective-permute-start(f32[2,8,1536]{2,1,0:T(8,128)S(1)} %get-tuple-element.66), channel_id=1, source_target_pairs={{0,56},{1,57},{2,58},{3,59},{4,60},{5,61},{6,62},{7,63},{8,0},{9,1... | collective-permute-start | bytes 294920 | tf_op jit(solution)/shard_map/ppermute | solution.py:38
  61.4 7.2 %collective-permute-start.16 = (f32[16,3072]{1,0:T(8,128)S(1)}, f32[16,3072]{1,0:T(8,128)S(1)}, u32[]{:S(2)}, u32[]{:S(2)}) collective-permute-start(f32[16,3072]{1,0:T(8,128)S(1)} %shard_map.75.refs_2_.refs_0_), channel_id=1, source_target_pairs={{0,1},{1,0},{2,3},{3,2},{4,5},{5,4},{6,7},{7,6},{8,9},{9,8},{10,11... | collective-permute-start | bytes 589832 | tf_op jit(solution)/shard_map/ppermute | solution.py:38
  61.5 4.7 %collective-permute-start.17 = (f32[2,8,1536]{2,1,0:T(8,128)S(1)}, f32[2,8,1536]{2,1,0:T(8,128)S(1)}, u32[]{:S(2)}, u32[]{:S(2)}) collective-permute-start(f32[2,8,1536]{2,1,0:T(8,128)S(1)} %get-tuple-element.67.refs_2_), channel_id=1, source_target_pairs={{0,8},{1,9},{2,10},{3,11},{4,12},{5,13},{6,14},{7,15},{8,16},{9,17... | collective-permute-start | bytes 294920 | tf_op jit(solution)/shard_map/ppermute | solution.py:38
  63.9 4.9 %collective-permute-start.20 = (f32[2,8,1536]{2,1,0:T(8,128)S(1)}, f32[2,8,1536]{2,1,0:T(8,128)S(1)}, u32[]{:S(2)}, u32[]{:S(2)}) collective-permute-start(f32[2,8,1536]{2,1,0:T(8,128)S(1)} %get-tuple-element.70), channel_id=1, source_target_pairs={{0,56},{1,57},{2,58},{3,59},{4,60},{5,61},{6,62},{7,63},{8,0},{9,1... | collective-permute-start | bytes 294920 | tf_op jit(solution)/shard_map/ppermute | solution.py:38
  66.2 4.7 %collective-permute-start.19 = (f32[2,8,1536]{2,1,0:T(8,128)S(1)}, f32[2,8,1536]{2,1,0:T(8,128)S(1)}, u32[]{:S(2)}, u32[]{:S(2)}) collective-permute-start(f32[2,8,1536]{2,1,0:T(8,128)S(1)} %shard_map.76.refs_2_), channel_id=1, source_target_pairs={{0,8},{1,9},{2,10},{3,11},{4,12},{5,13},{6,14},{7,15},{8,16},{9,17... | collective-permute-start | bytes 294920 | tf_op jit(solution)/shard_map/ppermute | solution.py:38
  68.6 7.0 %collective-permute-start.18 = (f32[16,3072]{1,0:T(8,128)S(1)}, f32[16,3072]{1,0:T(8,128)S(1)}, u32[]{:S(2)}, u32[]{:S(2)}) collective-permute-start(f32[16,3072]{1,0:T(8,128)S(1)} %shard_map.77.refs_3_.own_ref), channel_id=1, source_target_pairs={{0,3},{1,2},{2,1},{3,0},{4,7},{5,6},{6,5},{7,4},{8,11},{9,10},{10,... | collective-permute-start | bytes 589832 | tf_op jit(solution)/shard_map/ppermute | solution.py:38
  70.9 4.7 %collective-permute-start.21 = (f32[2,8,1536]{2,1,0:T(8,128)S(1)}, f32[2,8,1536]{2,1,0:T(8,128)S(1)}, u32[]{:S(2)}, u32[]{:S(2)}) collective-permute-start(f32[2,8,1536]{2,1,0:T(8,128)S(1)} %shard_map.78.right_ref), channel_id=1, source_target_pairs={{0,4},{1,5},{2,6},{3,7},{4,0},{5,1},{6,2},{7,3},{8,12},{9,13},{10,... | collective-permute-start | bytes 294920 | tf_op jit(solution)/shard_map/ppermute | solution.py:38
  76.2 4.4 %collective-permute-start.22 = (f32[32,128]{1,0:T(8,128)S(1)}, f32[32,128]{1,0:T(8,128)S(1)}, u32[]{:S(2)}, u32[]{:S(2)}) collective-permute-start(f32[32,128]{1,0:T(8,128)S(1)} %shard_map.79), channel_id=1, source_target_pairs={{0,8},{1,9},{2,10},{3,11},{4,12},{5,13},{6,14},{7,15},{8,0},{9,1},... | collective-permute-start | bytes 49160 | tf_op jit(solution)/shard_map/ppermute | solution.py:38
  80.6 4.6 %collective-permute-start.23 = (f32[32,128]{1,0:T(8,128)S(1)}, f32[32,128]{1,0:T(8,128)S(1)}, u32[]{:S(2)}, u32[]{:S(2)}) collective-permute-start(f32[32,128]{1,0:T(8,128)S(1)} %add.36), channel_id=1, source_target_pairs={{0,16},{1,17},{2,18},{3,19},{4,20},{5,21},{6,22},{7,23},{8,24},{9,... | collective-permute-start | bytes 49160 | tf_op jit(solution)/shard_map/ppermute | solution.py:38
  85.3 6.7 %collective-permute-start.24 = (f32[32,128]{1,0:T(8,128)S(1)}, f32[32,128]{1,0:T(8,128)S(1)}, u32[]{:S(2)}, u32[]{:S(2)}) collective-permute-start(f32[32,128]{1,0:T(8,128)S(1)} %add.37), channel_id=1, source_target_pairs={{0,56},{1,57},{2,58},{3,59},{4,60},{5,61},{6,62},{7,63},{8,48},{9,... | collective-permute-start | bytes 49160 | tf_op jit(solution)/shard_map/ppermute | solution.py:38
  92.1 1.2 %collective-permute-start.25 = (f32[1,32,128]{2,1,0:T(8,128)S(1)}, f32[1,32,128]{2,1,0:T(8,128)S(1)}, u32[]{:S(2)}, u32[]{:S(2)}) collective-permute-start(f32[1,32,128]{2,1,0:T(8,128)S(1)} %multiply_bitcast_fusion), channel_id=1, source_target_pairs={{0,64},{64,0},{128,192},{192,128},{1,65},{65,1},{129,193},{193,129... | collective-permute-start | bytes 49160 | tf_op jit(solution)/shard_map/ppermute | solution.py:248
  93.3 5.5 %collective-permute-start.26 = (f32[2,32,128]{2,1,0:T(8,128)S(1)}, f32[2,32,128]{2,1,0:T(8,128)S(1)}, u32[]{:S(2)}, u32[]{:S(2)}) collective-permute-start(f32[2,32,128]{2,1,0:T(8,128)S(1)} %pad_maximum_fusion.1), channel_id=1, source_target_pairs={{0,128},{64,192},{128,0},{192,64},{1,129},{65,193},{129,1},{193,65... | collective-permute-start | bytes 98312 | tf_op jit(solution)/shard_map/ppermute | solution.py:248
  99.1 4.8 %collective-permute-start.27 = (f32[32,128]{1,0:T(8,128)S(1)}, f32[32,128]{1,0:T(8,128)S(1)}, u32[]{:S(2)}, u32[]{:S(2)}) collective-permute-start(f32[32,128]{1,0:T(8,128)S(1)} %fusion), channel_id=1, source_target_pairs={{0,1},{1,0},{2,3},{3,2},{4,5},{5,4},{6,7},{7,6},{8,9},{9,8},{10,11... | collective-permute-start | bytes 49160 | tf_op jit(solution)/shard_map/ppermute | solution.py:38
  100.8 5.2 %collective-permute-start.28 = (f32[32,128]{1,0:T(8,128)S(1)}, f32[32,128]{1,0:T(8,128)S(1)}, u32[]{:S(2)}, u32[]{:S(2)}) collective-permute-start(f32[32,128]{1,0:T(8,128)S(1)} %fusion), channel_id=1, source_target_pairs={{0,2},{1,3},{2,0},{3,1},{4,6},{5,7},{6,4},{7,5},{8,10},{9,11},{10,... | collective-permute-start | bytes 49160 | tf_op jit(solution)/shard_map/ppermute | solution.py:38
  101.7 4.9 %collective-permute-start.29 = (f32[32,128]{1,0:T(8,128)S(1)}, f32[32,128]{1,0:T(8,128)S(1)}, u32[]{:S(2)}, u32[]{:S(2)}) collective-permute-start(f32[32,128]{1,0:T(8,128)S(1)} %fusion), channel_id=1, source_target_pairs={{0,3},{1,2},{2,1},{3,0},{4,7},{5,6},{6,5},{7,4},{8,11},{9,10},{10,... | collective-permute-start | bytes 49160 | tf_op jit(solution)/shard_map/ppermute | solution.py:38
  106.7 3.8 %collective-permute-start.30 = (f32[32,128]{1,0:T(8,128)S(1)}, f32[32,128]{1,0:T(8,128)S(1)}, u32[]{:S(2)}, u32[]{:S(2)}) collective-permute-start(f32[32,128]{1,0:T(8,128)S(1)} %add_add_fusion), channel_id=1, source_target_pairs={{0,4},{1,5},{2,6},{3,7},{4,0},{5,1},{6,2},{7,3},{8,12},{9,13},{10,... | collective-permute-start | bytes 49160 | tf_op jit(solution)/shard_map/ppermute | solution.py:38
